TPU v7x, 32 devices: a whole 2x2x4 slice. The times are simulated.
32 devices in a mesh: batch: 16 (over z, x, core), crop: 2 (over y).
Axes of the slice: x: 2, y: 2, z: 4, core: 2. Of those that a mesh axis runs over, the one named last changes fastest.
Arguments:
- voxels: bfloat16 [2, 16384, 512], P('crop', 'batch'), may hold values from -6 to 6
- phrases: bfloat16 [256, 512], P('batch'), may hold values from -6 to 6
- pair_ids: int32 [256], P('batch'), may hold values from 0 to 63
- margin_index: int32 [2, 16, 512], P('crop', 'batch'), may hold values from 0 to 1023, as said below
Outputs:
- voxel_grad: float32 [2, 16384, 512], P('crop', 'batch')
- phrase_grad: float32 [256, 512], P('batch')
Inputs may be any that keep to these rules, and one draw needn't show every extreme that they name: Each list margin_index[c, b] holds 512 distinct rows of that batch index's 1024 rows; entry k of crop 0 and entry k of crop 1 at the same b show the same place.
All inputs are finite; a program needn't handle non-finite values.
Results may differ from a plain program's by a relative error of at most 0.0013.
Values may be sent and summed in bfloat16 or wider, within the bound.
No kernel may reach another device: no remote copies, remote signals or barrier semaphores. Data moves between devices by JAX's collectives and lax.ppermute only.
A program may use at most 64 MiB of HBM per device.

v0:
```python
import math

import jax
import jax.numpy as jnp
from jax import lax
from jax.sharding import PartitionSpec as P

VOX_VOL = 256


def partner_2(value, axis, distance):
    mask = 2**distance
    pairs = [(source, source ^ mask) for source in range(lax.axis_size(axis))]
    return lax.ppermute(value, axis, pairs)


def local(voxels, phrases, pair_ids, margin_index):
    own_vox = voxels[0]
    rows, width = own_vox.shape
    scale = 1.0 / math.sqrt(width)
    owner_ids = lax.all_gather(pair_ids, "batch", axis=0, tiled=True)
    position = lax.axis_index("batch")
    volume = (position * rows + jnp.arange(rows, dtype=jnp.int32)) // VOX_VOL

    def tile(block, block_ids):
        sign = jnp.where(volume[:, None] == block_ids[None, :], 1.0, -1.0).astype(jnp.float32)
        logit = jnp.dot(own_vox, block.T, preferred_element_type=jnp.float32) * scale - 1.0
        dlogit = (-sign * jax.nn.sigmoid(-sign * logit)).astype(jnp.bfloat16)
        match_part = jnp.dot(dlogit, block, preferred_element_type=jnp.float32) * scale
        phrase_part = (
            lax.dot_general(
                dlogit, own_vox, (((0,), (0,)), ((), ())), preferred_element_type=jnp.float32
            )
            * scale
        )
        return (match_part, phrase_part)

    gathered = lax.all_gather(phrases, "batch", axis=0, tiled=True)
    total = gathered.shape[0]
    block_rows = math.gcd(total, 1024)
    num_blocks = total // block_rows
    blocks = gathered.reshape(num_blocks, block_rows, width)
    id_blocks = owner_ids.reshape(num_blocks, block_rows)

    def one_block(match_total, pieces):
        match_part, phrase_part = tile(pieces[0], pieces[1])
        return (match_total + match_part, phrase_part)

    match_grad, phrase_terms = lax.scan(
        one_block, jnp.zeros((rows, width), jnp.float32), (blocks, id_blocks)
    )
    own_partial = lax.psum_scatter(
        phrase_terms.reshape(total, width), "batch", scatter_dimension=0, tiled=True
    )
    phrase_grad = lax.psum(own_partial, "crop")
    picked = margin_index[0, 0]
    chosen = own_vox[picked]
    partner = partner_2(chosen, "crop", 0)
    voxel_grad = match_grad.at[picked].add(chosen.astype(jnp.float32) - partner.astype(jnp.float32))
    return (voxel_grad[None], phrase_grad)


def solution(mesh):
    placed = (P("crop", "batch", None), P("batch", None), P("batch"), P("crop", "batch", None))
    return jax.shard_map(
        local,
        mesh=mesh,
        in_specs=placed,
        out_specs=(P("crop", "batch", None), P("batch", None)),
        check_vma=False,
    )
```

profile of v0, /device:TPU:0, one launch (start us, length us, event | category | flops | bytes accessed | tf_op | source)
XLA Modules:
  0.0 115.8 jit_solution(11725222575452946895)
XLA Ops:
  7.2 0.0 copy-start
  7.2 0.0 reduce-scatter.2.cloned.1.call-start
  7.2 1.3 %dynamic-slice.2 = u32[1]{0:T(128)} dynamic-slice(u32[32]{0:T(128)} %constant.56, u32[]{:T(128)S(6)} %add.45), dynamic_slice_sizes={1} | dynamic-slice | bytes 12
  9.2 0.9 dynamic-update-slice
  10.1 13.7 %all-reduce = s32[256]{0:T(256)S(1)} all-reduce(s32[256]{0:T(256)S(1)} %dynamic-update-slice), channel_id=1, replica_groups=mesh['batch'=16,'crop'=2] {'batch'}, use_global_device_ids=true, to_apply=%add | all-reduce | flops 256 | bytes 2048
  23.8 18.9 %all_gather.7 = bf16[256,512]{1,0:T(8,128)(2,1)S(1)} all-gather(bf16[16,512]{1,0:T(8,128)(2,1)} %param.5), channel_id=1, replica_groups=mesh['batch'=16,'crop'=2] {'batch'}, dimensions={0}, use_global_device_ids=true | all-gather | bytes 278528 | tf_op jit(solution)/shard_map/all_gather | solution.py:38
  42.7 0.0 copy-done
  42.7 0.7 fusion.7
  43.3 0.0 copy-start.2
  43.4 0.8 copy-done.2
  44.1 0.0 copy-start.3
  44.1 1.2 %convolution_multiply_fusion.2 = f32[256,512]{1,0:T(8,128)} fusion(bf16[1024,256]{1,0:T(8,128)(2,1)S(1)} %fusion.7, bf16[1,1024,512]{2,1,0:T(8,128)(2,1)S(1)} %copy-done), kind=kOutput, calls=%fused_computation.12 | convolution fusion | flops 268566528 | bytes 2097152 | tf_op jit(solution)/shard_map/while/body/eval_jaxpr/dot_general | solution.py:31
  45.4 0.0 reduce-scatter.2.cloned.1.call-update
  45.4 0.0 copy-done.3
  45.5 2.6 %gather_fusion = bf16[512,512]{1,0:T(8,128)(2,1)} fusion(bf16[1024,512]{1,0:T(8,128)(2,1)S(1)} %bitcast.14, s32[1024]{0:T(1024)S(1)} %pad_clamp_fusion), kind=kCustom, calls=%fused_computation | custom fusion | bytes 1050624 | tf_op jit(solution)/shard_map/gather | solution.py:57
  48.1 1.5 %collective-permute-start = (bf16[512,512]{1,0:T(8,128)(2,1)}, bf16[512,512]{1,0:T(8,128)(2,1)}, u32[]{:S(2)}, u32[]{:S(2)}) collective-permute-start(bf16[512,512]{1,0:T(8,128)(2,1)} %gather_fusion), channel_id=1, source_target_pairs={{0,1},{1,0},{2,3},{3,2},{4,5},{5,4},{6,7},{7,6},{8,9},{9,8},{10,11... | collective-permute-start | bytes 1572872 | tf_op jit(solution)/shard_map/ppermute | solution.py:14
  49.6 1.5 %convolution_multiply_fusion = f32[1024,512]{1,0:T(8,128)S(1)} fusion(bf16[1024,256]{1,0:T(8,128)(2,1)} %copy-done.2, bf16[256,512]{1,0:T(8,128)(2,1)S(1)} %all_gather.7), kind=kOutput, calls=%fused_computation.2 | convolution fusion | flops 268959744 | bytes 2883584 | tf_op jit(solution)/shard_map/while/body/eval_jaxpr/dot_general | solution.py:29
  51.1 11.5 %collective-permute-done = bf16[512,512]{1,0:T(8,128)(2,1)} collective-permute-done((bf16[512,512]{1,0:T(8,128)(2,1)}, bf16[512,512]{1,0:T(8,128)(2,1)}, u32[]{:S(2)}, u32[]{:S(2)}) %collective-permute-start) | collective-permute-done | bytes 524320 | tf_op jit(solution)/shard_map/ppermute | solution.py:14
  62.6 5.1 %scatter_custom_fusion = f32[1024,512]{1,0:T(8,128)S(1)} fusion(f32[1024,512]{1,0:T(8,128)S(1)} %convolution_multiply_fusion, s32[512]{0:T(512)S(1)} %bitcast.17, bf16[512,512]{1,0:T(8,128)(2,1)} %collective-permute-done, bf16[512,512]{1,0:T(8,128)(2,1)} %gather_fusion), kind=kCustom, calls=%fused_computation.13 | custom fusion | flops 1048576 | bytes 3145728 | tf_op jit(solution)/shard_map/scatter-add | solution.py:59
  67.7 0.0 copy-start.1
  67.7 31.7 %reduce-scatter.2.cloned.1.call-done = f32[16,512]{1,0:T(8,128)} async-done(((f32[256,512]{1,0:T(8,128)}), f32[16,512]{1,0:T(8,128)}) %reduce-scatter.2.cloned.1.call-update) | async-done | bytes 32784 | tf_op jit(solution)/shard_map/reduce_scatter | solution.py:52
  99.4 9.5 %psum.7 = f32[16,512]{1,0:T(8,128)} all-reduce(f32[16,512]{1,0:T(8,128)} %reduce-scatter.2.cloned.1.call-done), channel_id=1, replica_groups=mesh['batch'=16,'crop'=2] {'crop'}, use_global_device_ids=true, to_apply=%region_2.3 | all-reduce | flops 8192 | bytes 65536 | tf_op jit(solution)/shard_map/psum | solution.py:55
  108.9 0.0 copy-done.1
  (4 shorter events, 0.0 us)
Async XLA Ops:
  7.2 35.5 %copy-start = (bf16[1,1024,512]{2,1,0:T(8,128)(2,1)S(1)}, bf16[1,1024,512]{2,1,0:T(8,128)(2,1)}, u32[]{:S(2)}) copy-start(bf16[1,1024,512]{2,1,0:T(8,128)(2,1)} %param.4) | copy-start | bytes 3145732
  7.2 92.2 %reduce-scatter.2.cloned.1.call-start = ((), (), s32[]{:S(2)}) async-start(), calls=%async_computation.1 | async-start | bytes 557056 | tf_op jit(solution)/shard_map/reduce_scatter | solution.py:52
  43.3 0.8 copy-start.2
  44.1 1.3 %copy-start.3 = (s32[1,1,512]{2,1,0:T(1,128)S(1)}, s32[1,1,512]{2,1,0:T(1,128)}, u32[]{:S(2)}) copy-start(s32[1,1,512]{2,1,0:T(1,128)} %param.7) | copy-start | bytes 6148
  48.1 14.5 %collective-permute-start = (bf16[512,512]{1,0:T(8,128)(2,1)}, bf16[512,512]{1,0:T(8,128)(2,1)}, u32[]{:S(2)}, u32[]{:S(2)}) collective-permute-start(bf16[512,512]{1,0:T(8,128)(2,1)} %gather_fusion), channel_id=1, source_target_pairs={{0,1},{1,0},{2,3},{3,2},{4,5},{5,4},{6,7},{7,6},{8,9},{9,8},{10,11... | collective-permute-start | bytes 1572872 | tf_op jit(solution)/shard_map/ppermute | solution.py:14
  67.7 41.2 %copy-start.1 = (f32[1024,512]{1,0:T(8,128)}, f32[1024,512]{1,0:T(8,128)S(1)}, u32[]{:S(2)}) copy-start(f32[1024,512]{1,0:T(8,128)S(1)} %scatter_custom_fusion) | copy-start | bytes 6291460
Sparse Core Ops, SparseCore 0:
  45.5 53.7 reduce-scatter.1
where the time goes:
time: 116 us
  waiting for transfers between devices  43.2 us (37%)
  blocking collectives  42.2 us (36%)
  between operations  14.8 us (13%)
  local copies, waits for them, and re-layouts  5.62 us (5%)
  other arithmetic  5.12 us (4%)
  matrix products  3.37 us (3%)
  starting transfers between devices  1.56 us (1%)
    reduce_scatter x1, waiting for transfers between devices, local(): lax.psum_scatter(phrase_terms.reshape(total, width), 'batch', scatter_dim...  31.7 us
    all_gather x1, blocking collectives, local(): gathered = lax.all_gather(phrases, 'batch', axis=0, tiled=True)  18.9 us
    unnamed x1, blocking collectives  13.7 us
    ppermute x1, waiting for transfers between devices, partner_2(): return lax.ppermute(value, axis, pairs)  11.5 us
    psum x1, blocking collectives, local(): phrase_grad = lax.psum(own_partial, 'crop')  9.55 us
    scatter-add x1, other arithmetic, local(): match_grad.at[picked]  5.1 us
    unnamed x11, local copies, waits for them, and re-layouts  2.99 us
    gather x1, local copies, waits for them, and re-layouts, local(): chosen = own_vox[picked]  2.64 us
  transfers between devices with their start and end apart: 2, of which 2 were waited for; matrix products, arithmetic and copies ran while one was open for 8% of the time, Pallas kernels for 0%

commit v1 on v0

v1 whole, which is shorter than its diff:
```python
import functools
import math

import jax
import jax.numpy as jnp
from jax import lax
from jax.experimental import pallas as pl
from jax.experimental.pallas import tpu as pltpu
from jax.sharding import PartitionSpec as P

VOX_VOL = 256
VOL_SHIFT = VOX_VOL.bit_length() - 1
LANES = 128
VMEM_LIMIT = 24 * 1024 * 1024

F32 = jnp.float32
BF16 = jnp.bfloat16


def vmem_spec():
    return pl.BlockSpec(memory_space=pltpu.VMEM)


def pack_kernel(copies, ids_ref, phrases_ref, out_ref):
    rows, width = phrases_ref.shape
    row = lax.broadcasted_iota(jnp.int32, (rows, LANES), 0)
    lane = lax.broadcasted_iota(jnp.int32, (rows, LANES), 1)
    ids = jnp.zeros((rows, LANES), jnp.int32)
    for i in range(rows):
        ids = jnp.where(row == i, ids_ref[i], ids)
    parts = jnp.where(lane == 0, ids >> 8, jnp.where(lane == 1, ids & 255, 0))
    parts = parts.astype(F32).astype(BF16)
    phrases = phrases_ref[...]

    def put(i):
        out_ref[pl.ds(pl.multiple_of(i * rows, rows), rows), :width] = phrases
        out_ref[pl.ds(pl.multiple_of(i * rows, rows), rows), width:] = parts

    if copies <= 16:
        for i in range(copies):
            put(i)
    else:
        pl.loop(0, copies)(put)


def main_kernel(scale, base_ref, vox_ref, near_ref, far_ref, idx_ref, dl_ref, near_out, far_out, chosen_ref):
    rows, width = vox_ref.shape
    half = near_ref.shape[0]
    block = min(half, 128)
    volume = (base_ref[0] + lax.broadcasted_iota(jnp.int32, (1, rows), 1)) >> VOL_SHIFT
    volume = volume.astype(F32)

    def terms(src_ref, out_ref, offset, start):
        at = pl.ds(pl.multiple_of(start, block), block)
        phrases = src_ref[at, :width]
        parts = src_ref[at, width:].astype(F32)
        ids = parts[:, 0:1] * 256.0 + parts[:, 1:2]
        logit = lax.dot_general(
            phrases, vox_ref[...], (((1,), (1,)), ((), ())), preferred_element_type=F32
        )
        sign = jnp.where(ids == volume, 1.0, -1.0).astype(F32)
        dlogit = (-sign / (1.0 + jnp.exp(sign * (logit * scale - 1.0)))).astype(BF16)
        dl_ref[pl.ds(pl.multiple_of(offset + start, block), block), :] = dlogit
        out_ref[at, :] = jnp.dot(dlogit, vox_ref[...], preferred_element_type=F32) * scale

    for src_ref, out_ref, offset in ((far_ref, far_out, half), (near_ref, near_out, 0)):
        if half == block:
            terms(src_ref, out_ref, offset, 0)
        else:
            pl.loop(0, half // block)(
                lambda j, s=src_ref, o=out_ref, f=offset: terms(s, o, f, j * block)
            )

    picks = idx_ref.shape[1]
    column = jnp.broadcast_to(idx_ref[...], (8, picks)).T[:, 0:1]
    onehot = (column == lax.broadcasted_iota(jnp.int32, (picks, rows), 1)).astype(F32).astype(BF16)
    chosen_ref[...] = jnp.dot(onehot, vox_ref[...], preferred_element_type=F32).astype(BF16)


def grad_kernel(scale, idx_ref, vox_ref, partner_ref, dl_ref, near_ref, far_ref, out_ref):
    rows, width = vox_ref.shape
    half = near_ref.shape[0]
    picks = idx_ref.shape[1]
    at = pl.program_id(0) * rows + lax.broadcasted_iota(jnp.int32, (rows, picks), 0)
    spread = (at == idx_ref[...]).astype(F32)
    taken = jnp.sum(spread, axis=1, keepdims=True)
    tn = (((0,), (0,)), ((), ()))
    match = lax.dot_general(dl_ref[:half, :], near_ref[:, :width], tn, preferred_element_type=F32)
    match += lax.dot_general(dl_ref[half:, :], far_ref[:, :width], tn, preferred_element_type=F32)
    other = jnp.dot(spread.astype(BF16), partner_ref[...], preferred_element_type=F32)
    out_ref[...] = match * scale + taken * vox_ref[...].astype(F32) - other


def local(voxels, phrases, pair_ids, margin_index):
    own_vox = voxels[0]
    rows, width = own_vox.shape
    owned = phrases.shape[0]
    picks = margin_index.shape[-1]
    scale = 1.0 / math.sqrt(width)
    devices = lax.axis_size("batch")
    crops = lax.axis_size("crop")
    members = devices // 2
    half = members * owned
    total = 2 * half
    same_core = [[2 * i + core for i in range(members)] for core in range(2)]
    cores = [(i, i ^ 1) for i in range(devices)]
    swap = [(i, i ^ 1) for i in range(crops)]
    params = pltpu.CompilerParams(vmem_limit_bytes=VMEM_LIMIT)

    packed = pl.pallas_call(
        functools.partial(pack_kernel, members),
        out_shape=jax.ShapeDtypeStruct((half, width + LANES), BF16),
        in_specs=[pl.BlockSpec(memory_space=pltpu.SMEM), vmem_spec()],
        out_specs=vmem_spec(),
        compiler_params=params,
        name="pack",
    )(pair_ids, phrases)
    near = lax.all_to_all(packed, "batch", 0, 0, tiled=True, axis_index_groups=same_core)
    far = lax.ppermute(near, "batch", cores)

    picked = margin_index[0]
    base = (lax.axis_index("batch") * rows).astype(jnp.int32).reshape(1)
    dlogit, near_terms, far_terms, chosen = pl.pallas_call(
        functools.partial(main_kernel, scale),
        out_shape=[
            jax.ShapeDtypeStruct((total, rows), BF16),
            jax.ShapeDtypeStruct((half, width), F32),
            jax.ShapeDtypeStruct((half, width), F32),
            jax.ShapeDtypeStruct((picks, width), BF16),
        ],
        in_specs=[pl.BlockSpec(memory_space=pltpu.SMEM)] + [vmem_spec()] * 4,
        out_specs=[vmem_spec()] * 4,
        compiler_params=params,
        cost_estimate=pl.CostEstimate(
            flops=4 * total * rows * width + 2 * picks * rows * width,
            bytes_accessed=4 * rows * width,
            transcendentals=total * rows,
        ),
        name="terms",
    )(base, own_vox, near, far, picked)

    from_core = lax.ppermute(far_terms, "batch", cores)
    partner = lax.ppermute(chosen, "crop", swap)
    pieces = lax.all_to_all(
        near_terms + from_core, "batch", 0, 0, tiled=True, axis_index_groups=same_core
    )
    own = jnp.sum(pieces.reshape(members, owned, width), axis=0)
    own, partner = lax.optimization_barrier((own, partner))
    phrase_grad = own + lax.ppermute(own, "crop", swap)

    block = math.gcd(rows, 256)
    voxel_grad = pl.pallas_call(
        functools.partial(grad_kernel, scale),
        out_shape=jax.ShapeDtypeStruct((rows, width), F32),
        grid=(rows // block,),
        in_specs=[
            pl.BlockSpec((1, picks), lambda i: (0, 0)),
            pl.BlockSpec((block, width), lambda i: (i, 0)),
            pl.BlockSpec((picks, width), lambda i: (0, 0)),
            pl.BlockSpec((total, block), lambda i: (0, i)),
            pl.BlockSpec((half, width + LANES), lambda i: (0, 0)),
            pl.BlockSpec((half, width + LANES), lambda i: (0, 0)),
        ],
        out_specs=pl.BlockSpec((block, width), lambda i: (i, 0)),
        compiler_params=params,
        cost_estimate=pl.CostEstimate(
            flops=2 * total * rows * width + 2 * picks * rows * width,
            bytes_accessed=8 * rows * width,
            transcendentals=0,
        ),
        name="voxel_grad",
    )(picked, own_vox, partner, dlogit, near, far)
    return (voxel_grad[None], phrase_grad)


def solution(mesh):
    placed = (P("crop", "batch", None), P("batch", None), P("batch"), P("crop", "batch", None))
    return jax.shard_map(
        local,
        mesh=mesh,
        in_specs=placed,
        out_specs=(P("crop", "batch", None), P("batch", None)),
        check_vma=False,
    )
```

time: 116 us -> 42.4 us (0.37)
  waiting for transfers between devices: 43.2 us -> 2.13 us
  blocking collectives: 42.2 us -> 26.5 us
  between operations: 14.8 us -> 0.67 us
  Pallas kernels: 0 us -> 5.57 us
  other arithmetic: 5.12 us -> 0.68 us
  matrix products: 3.37 us -> 0 us
  local copies, waits for them, and re-layouts: 5.62 us -> 3.28 us
  starting transfers between devices: 1.56 us -> 3.27 us
    reduce_scatter x1 -> x0, waiting for transfers between devices: 31.7 us -> none  [local(): lax.psum_scatter(phrase_terms.reshape(total, width), 'batch', scatter_dim...]
    all_to_all x0 -> x2, blocking collectives: none -> 26.5 us  [the longest x1 14.6 us: local(): lax.all_to_all(packed, 'batch', 0, 0, tiled=True, axis_index_groups=same_...]
    all_gather x1 -> x0, blocking collectives: 18.9 us -> none  [local(): gathered = lax.all_gather(phrases, 'batch', axis=0, tiled=True)]
    unnamed x1 -> x0, blocking collectives: 13.7 us -> none
    psum x1 -> x0, blocking collectives: 9.55 us -> none  [local(): phrase_grad = lax.psum(own_partial, 'crop')]
    ppermute x1 -> x4, waiting for transfers between devices: 11.5 us -> 2.13 us  [the longest x1 1.39 us: local(): far = lax.ppermute(near, 'batch', cores)]
    pallas_call x0 -> x3, Pallas kernels: none -> 5.57 us  [the longest x1 3.11 us: local(): pl.pallas_call(functools.partial(grad_kernel, scale), out_shape=jax.Shape...]
    scatter-add x1 -> x0, other arithmetic: 5.1 us -> none  [local(): match_grad.at[picked]]
  transfers between devices with their start and end apart: 2 -> 4, of which waited for: 2 -> 2; matrix products, arithmetic and copies ran while one was open for 8% -> 0% of each run, Pallas kernels for 0% -> 7%
where the time goes in v1:
time: 42.4 us; the launch traced here: 42.1 us
  blocking collectives  26.5 us (62%)
  Pallas kernels  5.57 us (13%)
  local copies, waits for them, and re-layouts  3.28 us (8%)
  starting transfers between devices  3.27 us (8%)
  waiting for transfers between devices  2.13 us (5%)
  other arithmetic  0.68 us (2%)
  between operations  0.67 us (2%)
    all_to_all x1, blocking collectives, local(): lax.all_to_all(packed, 'batch', 0, 0, tiled=True, axis_index_groups=same_...  14.6 us
    all_to_all x1, blocking collectives, local(): lax.all_to_all(near_terms + from_core, 'batch', 0, 0, tiled=True, axis_in...  11.9 us
    unnamed x12, local copies, waits for them, and re-layouts  3.28 us
    pallas_call x1, Pallas kernels, local(): pl.pallas_call(functools.partial(grad_kernel, scale), out_shape=jax.Shape...  3.11 us
    pallas_call x1, Pallas kernels, local(): pl.pallas_call(functools.partial(main_kernel, scale), out_shape=[jax.Shap...  1.9 us
    ppermute x1, starting transfers between devices, local(): partner = lax.ppermute(chosen, 'crop', swap)  1.53 us
    ppermute x1, starting transfers between devices, local(): phrase_grad = own + lax.ppermute(own, 'crop', swap)  1.53 us
    ppermute x1, waiting for transfers between devices, local(): far = lax.ppermute(near, 'batch', cores)  1.39 us
  transfers between devices with their start and end apart: 4, of which 2 were waited for; matrix products, arithmetic and copies ran while one was open for 0% of the time, Pallas kernels for 7%

profile of v1, /device:TPU:0, one launch (start us, length us, event | category | flops | bytes accessed | tf_op | source)
XLA Modules:
  0.0 42.1 jit_solution(12098200668551527949)
XLA Ops:
  0.6 0.0 copy-start.2
  0.6 0.7 %copy-done.2 = bf16[16,512]{1,0:T(8,128)(2,1)S(1)} copy-done((bf16[16,512]{1,0:T(8,128)(2,1)S(1)}, bf16[16,512]{1,0:T(8,128)(2,1)}, u32[]{:S(2)}) %copy-start.2) | copy-done | bytes 16408
  1.3 0.0 copy-start.5
  1.4 0.7 %copy-done.5 = s32[16]{0:T(128)S(1)} copy-done((s32[16]{0:T(128)S(1)}, s32[16]{0:T(128)}, u32[]{:S(2)}) %copy-start.5) | copy-done | bytes 88
  2.0 0.6 %pack.1 = bf16[128,640]{1,0:T(8,128)(2,1)S(1)} custom-call(s32[16]{0:T(128)S(1)} %copy-done.5, bf16[16,512]{1,0:T(8,128)(2,1)S(1)} %copy-done.2), custom_call_target="tpu_custom_call" | custom-call | tf_op jit(solution)/shard_map/pack/pallas_call | solution.py:110
  2.6 14.6 %all_to_all.20 = bf16[8,16,640]{2,1,0:T(8,128)(2,1)S(1)} all-to-all(bf16[8,16,640]{2,1,0:T(8,128)(2,1)S(1)} %bitcast.12), channel_id=1, replica_groups={{0,4,8,12,16,20,24,28},{2,6,10,14,18,22,26,30},{1,5,9,13,17,21,25,29},{..., dimensions={0} | all-to-all | bytes 327680 | tf_op jit(solution)/shard_map/all_to_all | solution.py:118
  17.2 0.0 collective-permute-start
  17.2 1.4 %collective-permute-done.far_ref = bf16[128,640]{1,0:T(8,128)(2,1)S(1)} collective-permute-done((bf16[128,640]{1,0:T(8,128)(2,1)S(1)}, bf16[128,640]{1,0:T(8,128)(2,1)S(1)}, u32[]{:S(2)}, u32[]{:S(2)}) %collective-permute-start) | collective-permute-done | bytes 163872 | tf_op jit(solution)/shard_map/ppermute | solution.py:119
  18.6 0.0 copy-start
  18.6 1.2 %copy-done = bf16[1,1024,512]{2,1,0:T(8,128)(2,1)S(1)} copy-done((bf16[1,1024,512]{2,1,0:T(8,128)(2,1)S(1)}, bf16[1,1024,512]{2,1,0:T(8,128)(2,1)}, u32[]{:S(2)}) %copy-start) | copy-done | bytes 1048600
  19.8 0.0 copy-start.3
  19.8 0.7 %copy-done.3 = s32[1,1,512]{2,1,0:T(1,128)S(1)} copy-done((s32[1,1,512]{2,1,0:T(1,128)S(1)}, s32[1,1,512]{2,1,0:T(1,128)}, u32[]{:S(2)}) %copy-start.3) | copy-done | bytes 2072
  20.5 0.0 copy-start.1
  20.5 0.0 copy-start.4
  20.5 1.9 %terms.1 = (bf16[256,1024]{1,0:T(8,128)(2,1)S(1)}, f32[128,512]{1,0:T(8,128)S(1)}, f32[128,512]{1,0:T(8,128)S(1)}, bf16[512,512]{1,0:T(8,128)(2,1)S(1)}) custom-call(s32[1]{0:T(128)} %bitcast.2.base_ref, bf16[1024,512]{1,0:T(8,128)(2,1)S(1)} %bitcast.7, bf16[128,640]{1,0:T(8,128)(2,1)S(1)} %bitcast.10, bf16[128,640]{1,0:T(8,128)(2,1)S(1)} %collective-permute-done.far_ref, ...), custom_call_target="tpu_custom_call" | custom-call | flops 1073741824 | bytes 2097152 | tf_op jit(solution)/shard_map/terms/pallas_call | solution.py:123
  22.4 0.2 collective-permute-start.1
  22.6 1.5 %collective-permute-start.2 = (bf16[512,512]{1,0:T(8,128)(2,1)S(1)}, bf16[512,512]{1,0:T(8,128)(2,1)S(1)}, u32[]{:S(2)}, u32[]{:S(2)}) collective-permute-start(bf16[512,512]{1,0:T(8,128)(2,1)S(1)} %get-tuple-element.10), channel_id=1, source_target_pairs={{0,1},{1,0},{2,3},{3,2},{4,5},{5,4},{6,7},{7,6},{8,9},{9,8},{10,11... | collective-permute-start | bytes 1572872 | tf_op jit(solution)/shard_map/ppermute | solution.py:143
  24.1 0.0 collective-permute-done.1
  24.2 11.9 %all_to_all.21 = f32[8,16,512]{2,1,0:T(8,128)S(1)} all-to-all(f32[8,16,512]{2,1,0:T(8,128)S(1)} %bitcast.16), channel_id=1, replica_groups={{0,4,8,12,16,20,24,28},{2,6,10,14,18,22,26,30},{1,5,9,13,17,21,25,29},{..., dimensions={0} | all-to-all | bytes 524288 | tf_op jit(solution)/shard_map/all_to_all | solution.py:144
  36.1 0.7 %collective-permute-done.2.partner_ref = bf16[512,512]{1,0:T(8,128)(2,1)S(1)} collective-permute-done((bf16[512,512]{1,0:T(8,128)(2,1)S(1)}, bf16[512,512]{1,0:T(8,128)(2,1)S(1)}, u32[]{:S(2)}, u32[]{:S(2)}) %collective-permute-start.2) | collective-permute-done | bytes 524320 | tf_op jit(solution)/shard_map/ppermute | solution.py:143
  36.8 1.5 %collective-permute-start.3 = (f32[16,512]{1,0:T(8,128)S(1)}, f32[16,512]{1,0:T(8,128)S(1)}, u32[]{:S(2)}, u32[]{:S(2)}) collective-permute-start(f32[16,512]{1,0:T(8,128)S(1)} %reduce_sum.9), channel_id=1, source_target_pairs={{0,1},{1,0},{2,3},{3,2},{4,5},{5,4},{6,7},{7,6},{8,9},{9,8},{10,11... | collective-permute-start | bytes 98312 | tf_op jit(solution)/shard_map/ppermute | solution.py:149
  38.3 0.0 copy-done.1
  38.3 0.0 copy-done.4
  38.3 3.1 %voxel_grad.1 = f32[1024,512]{1,0:T(8,128)} custom-call(s32[1,512]{1,0:T(1,128)S(1)} %bitcast.14, bf16[1024,512]{1,0:T(8,128)(2,1)S(1)} %bitcast.8, bf16[512,512]{1,0:T(8,128)(2,1)S(1)} %collective-permute-done.2.partner_ref, bf16[256,1024]{1,0:T(8,128)(2,1)S(1)} %get-tuple-element.12.dl_ref, bf16[128,640]{1,0:T(8,128)(2,1)S(1)} %bitcast.11, ...), custom_call_target="tpu_custom_call" | custom-call | flops 805306368 | bytes 4194304 | tf_op jit(solution)/shard_map/voxel_grad/pallas_call | solution.py:152
  41.4 0.0 collective-permute-done.3
  41.4 0.6 %add.7 = f32[16,512]{1,0:T(8,128)} add(f32[16,512]{1,0:T(8,128)S(1)} %reduce_sum.9, f32[16,512]{1,0:T(8,128)S(1)} %collective-permute-done.3) | non-fusion elementwise | flops 8192 | bytes 98304 | tf_op jit(solution)/shard_map/add | solution.py:149
  (2 shorter events, 0.1 us)
Async XLA Ops:
  0.6 0.7 %copy-start.2 = (bf16[16,512]{1,0:T(8,128)(2,1)S(1)}, bf16[16,512]{1,0:T(8,128)(2,1)}, u32[]{:S(2)}) copy-start(bf16[16,512]{1,0:T(8,128)(2,1)} %phrases_ref.1) | copy-start | bytes 49156
  1.3 0.7 %copy-start.5 = (s32[16]{0:T(128)S(1)}, s32[16]{0:T(128)}, u32[]{:S(2)}) copy-start(s32[16]{0:T(128)} %ids_ref.1) | copy-start | bytes 196
  17.2 1.4 %collective-permute-start = (bf16[128,640]{1,0:T(8,128)(2,1)S(1)}, bf16[128,640]{1,0:T(8,128)(2,1)S(1)}, u32[]{:S(2)}, u32[]{:S(2)}) collective-permute-start(bf16[128,640]{1,0:T(8,128)(2,1)S(1)} %bitcast.9), channel_id=1, source_target_pairs={{0,2},{2,0},{4,6},{6,4},{8,10},{10,8},{12,14},{14,12},{16,18},{18,... | collective-permute-start | bytes 491528 | tf_op jit(solution)/shard_map/ppermute | solution.py:119
  18.6 1.2 %copy-start = (bf16[1,1024,512]{2,1,0:T(8,128)(2,1)S(1)}, bf16[1,1024,512]{2,1,0:T(8,128)(2,1)}, u32[]{:S(2)}) copy-start(bf16[1,1024,512]{2,1,0:T(8,128)(2,1)} %param.4) | copy-start | bytes 3145732
  19.8 0.7 %copy-start.3 = (s32[1,1,512]{2,1,0:T(1,128)S(1)}, s32[1,1,512]{2,1,0:T(1,128)}, u32[]{:S(2)}) copy-start(s32[1,1,512]{2,1,0:T(1,128)} %param.7) | copy-start | bytes 6148
  20.5 17.8 %copy-start.1 = (bf16[1,1024,512]{2,1,0:T(8,128)(2,1)S(1)}, bf16[1,1024,512]{2,1,0:T(8,128)(2,1)}, u32[]{:S(2)}) copy-start(bf16[1,1024,512]{2,1,0:T(8,128)(2,1)} %param.4) | copy-start | bytes 3145732
  20.5 17.8 %copy-start.4 = (s32[1,1,512]{2,1,0:T(1,128)S(1)}, s32[1,1,512]{2,1,0:T(1,128)}, u32[]{:S(2)}) copy-start(s32[1,1,512]{2,1,0:T(1,128)} %param.7) | copy-start | bytes 6148
  22.4 1.7 %collective-permute-start.1 = (f32[128,512]{1,0:T(8,128)S(1)}, f32[128,512]{1,0:T(8,128)S(1)}, u32[]{:S(2)}, u32[]{:S(2)}) collective-permute-start(f32[128,512]{1,0:T(8,128)S(1)} %get-tuple-element.9), channel_id=1, source_target_pairs={{0,2},{2,0},{4,6},{6,4},{8,10},{10,8},{12,14},{14,12},{16,18},{18,... | collective-permute-start | bytes 786440 | tf_op jit(solution)/shard_map/ppermute | solution.py:142
  22.6 14.2 %collective-permute-start.2 = (bf16[512,512]{1,0:T(8,128)(2,1)S(1)}, bf16[512,512]{1,0:T(8,128)(2,1)S(1)}, u32[]{:S(2)}, u32[]{:S(2)}) collective-permute-start(bf16[512,512]{1,0:T(8,128)(2,1)S(1)} %get-tuple-element.10), channel_id=1, source_target_pairs={{0,1},{1,0},{2,3},{3,2},{4,5},{5,4},{6,7},{7,6},{8,9},{9,8},{10,11... | collective-permute-start | bytes 1572872 | tf_op jit(solution)/shard_map/ppermute | solution.py:143
  36.8 4.6 %collective-permute-start.3 = (f32[16,512]{1,0:T(8,128)S(1)}, f32[16,512]{1,0:T(8,128)S(1)}, u32[]{:S(2)}, u32[]{:S(2)}) collective-permute-start(f32[16,512]{1,0:T(8,128)S(1)} %reduce_sum.9), channel_id=1, source_target_pairs={{0,1},{1,0},{2,3},{3,2},{4,5},{5,4},{6,7},{7,6},{8,9},{9,8},{10,11... | collective-permute-start | bytes 98312 | tf_op jit(solution)/shard_map/ppermute | solution.py:149

commit v2 on v1

v2 whole, which is shorter than its diff:
```python
import functools
import math

import jax
import jax.numpy as jnp
from jax import lax
from jax.experimental import pallas as pl
from jax.experimental.pallas import tpu as pltpu
from jax.sharding import PartitionSpec as P

VOX_VOL = 256
VOL_SHIFT = VOX_VOL.bit_length() - 1
LANES = 128
VMEM_LIMIT = 24 * 1024 * 1024

F32 = jnp.float32
BF16 = jnp.bfloat16


def vmem_spec():
    return pl.BlockSpec(memory_space=pltpu.VMEM)


def pack_kernel(copies, ids_hbm, phrases_hbm, out_ref, ids_ref, phrases_ref, sems):
    rows, width = phrases_ref.shape
    get_ids = pltpu.make_async_copy(ids_hbm, ids_ref, sems.at[0])
    get_phrases = pltpu.make_async_copy(phrases_hbm, phrases_ref, sems.at[1])
    get_ids.start()
    get_phrases.start()
    row = lax.broadcasted_iota(jnp.int32, (rows, LANES), 0)
    lane = lax.broadcasted_iota(jnp.int32, (rows, LANES), 1)
    get_ids.wait()
    ids = jnp.zeros((rows, LANES), jnp.int32)
    for i in range(rows):
        ids = jnp.where(row == i, ids_ref[i], ids)
    parts = jnp.where(lane == 0, ids >> 8, jnp.where(lane == 1, ids & 255, 0))
    parts = parts.astype(F32).astype(BF16)
    get_phrases.wait()
    phrases = phrases_ref[...]

    def put(i):
        out_ref[pl.ds(pl.multiple_of(i * rows, rows), rows), :width] = phrases
        out_ref[pl.ds(pl.multiple_of(i * rows, rows), rows), width:] = parts

    if copies <= 16:
        for i in range(copies):
            put(i)
    else:
        pl.loop(0, copies)(put)


def margin_kernel(vox_ref, idx_ref, chosen_ref):
    rows = vox_ref.shape[0]
    picks = idx_ref.shape[1]
    column = jnp.broadcast_to(idx_ref[...], (8, picks)).T[:, 0:1]
    onehot = (column == lax.broadcasted_iota(jnp.int32, (picks, rows), 1)).astype(F32).astype(BF16)
    chosen_ref[...] = jnp.dot(onehot, vox_ref[...], preferred_element_type=F32).astype(BF16)


def terms_kernel(scale, base_ref, vox_ref, packed_ref, dl_ref, out_ref):
    rows, width = vox_ref.shape
    half = packed_ref.shape[0]
    block = min(half, 128)
    volume = (base_ref[0] + lax.broadcasted_iota(jnp.int32, (1, rows), 1)) >> VOL_SHIFT
    volume = volume.astype(F32)

    def terms(start):
        at = pl.ds(pl.multiple_of(start, block), block)
        phrases = packed_ref[at, :width]
        parts = packed_ref[at, width:].astype(F32)
        ids = parts[:, 0:1] * 256.0 + parts[:, 1:2]
        logit = lax.dot_general(
            phrases, vox_ref[...], (((1,), (1,)), ((), ())), preferred_element_type=F32
        )
        sign = jnp.where(ids == volume, 1.0, -1.0).astype(F32)
        dlogit = (-sign / (1.0 + jnp.exp(sign * (logit * scale - 1.0)))).astype(BF16)
        dl_ref[at, :] = dlogit
        out_ref[at, :] = jnp.dot(dlogit, vox_ref[...], preferred_element_type=F32) * scale

    if half == block:
        terms(0)
    else:
        pl.loop(0, half // block)(lambda j: terms(j * block))


def grad_kernel(
    scale, block, idx_ref, vox_ref, partner_ref, dl_near, dl_far, near_ref, far_ref, out_hbm, out_ref, sems
):
    rows, width = vox_ref.shape
    picks = idx_ref.shape[1]
    tn = (((0,), (0,)), ((), ()))
    copies = []
    for i in range(rows // block):
        at = pl.ds(i * block, block)
        row = i * block + lax.broadcasted_iota(jnp.int32, (block, picks), 0)
        spread = (row == idx_ref[...]).astype(F32)
        taken = jnp.sum(spread, axis=1, keepdims=True)
        match = lax.dot_general(
            dl_near[:, at], near_ref[:, :width], tn, preferred_element_type=F32
        ) + lax.dot_general(dl_far[:, at], far_ref[:, :width], tn, preferred_element_type=F32)
        other = jnp.dot(spread.astype(BF16), partner_ref[...], preferred_element_type=F32)
        out_ref[at, :] = match * scale + taken * vox_ref[at, :].astype(F32) - other
        copies.append(pltpu.make_async_copy(out_ref.at[at, :], out_hbm.at[at, :], sems.at[i]))
        copies[-1].start()
    for copy in copies:
        copy.wait()


def local(voxels, phrases, pair_ids, margin_index):
    own_vox = voxels[0]
    rows, width = own_vox.shape
    owned = phrases.shape[0]
    picks = margin_index.shape[-1]
    scale = 1.0 / math.sqrt(width)
    devices = lax.axis_size("batch")
    crops = lax.axis_size("crop")
    members = devices // 2
    half = members * owned
    same_core = [[2 * i + core for i in range(members)] for core in range(2)]
    cores = [(i, i ^ 1) for i in range(devices)]
    swap = [(i, i ^ 1) for i in range(crops)]
    params = pltpu.CompilerParams(vmem_limit_bytes=VMEM_LIMIT)
    smem = pl.BlockSpec(memory_space=pltpu.SMEM)
    hbm = pl.BlockSpec(memory_space=pltpu.HBM)

    lane = lax.broadcasted_iota(jnp.int32, (owned, LANES), 1)
    id_parts = jnp.where(lane == 0, pair_ids[:, None] >> 8, pair_ids[:, None] & 255)
    id_parts = id_parts.astype(BF16)
    own_block = jnp.concatenate([phrases, id_parts], axis=1)
    packed = jnp.broadcast_to(own_block[None], (members, owned, width + LANES)).reshape(half, width + LANES)
    near = lax.all_to_all(packed, "batch", 0, 0, tiled=True, axis_index_groups=same_core)
    far = lax.ppermute(near, "batch", cores)

    picked = margin_index[0]
    chosen = pl.pallas_call(
        margin_kernel,
        out_shape=jax.ShapeDtypeStruct((picks, width), BF16),
        in_specs=[vmem_spec()] * 2,
        out_specs=vmem_spec(),
        compiler_params=params,
        cost_estimate=pl.CostEstimate(
            flops=2 * picks * rows * width, bytes_accessed=2 * rows * width, transcendentals=0
        ),
        name="margin_rows",
    )(own_vox, picked)

    base = (lax.axis_index("batch") * rows).astype(jnp.int32).reshape(1)
    terms = pl.pallas_call(
        functools.partial(terms_kernel, scale),
        out_shape=[
            jax.ShapeDtypeStruct((half, rows), BF16),
            jax.ShapeDtypeStruct((half, width), F32),
        ],
        in_specs=[smem] + [vmem_spec()] * 2,
        out_specs=[vmem_spec()] * 2,
        compiler_params=params,
        cost_estimate=pl.CostEstimate(
            flops=4 * half * rows * width,
            bytes_accessed=2 * rows * width,
            transcendentals=half * rows,
        ),
        name="terms",
    )
    far, chosen = lax.optimization_barrier((far, chosen))
    partner = lax.ppermute(chosen, "crop", swap)
    dl_far, far_terms = terms(base, own_vox, far)
    from_core = lax.ppermute(far_terms, "batch", cores)
    dl_near, near_terms = terms(base, own_vox, near)

    pieces = lax.all_to_all(
        near_terms + from_core, "batch", 0, 0, tiled=True, axis_index_groups=same_core
    )
    own = jnp.sum(pieces.reshape(members, owned, width), axis=0)
    own, partner = lax.optimization_barrier((own, partner))
    phrase_grad = own + lax.ppermute(own, "crop", swap)

    block = math.gcd(rows, 256)
    voxel_grad = pl.pallas_call(
        functools.partial(grad_kernel, scale, block),
        out_shape=jax.ShapeDtypeStruct((rows, width), F32),
        in_specs=[vmem_spec()] * 7,
        out_specs=hbm,
        scratch_shapes=[pltpu.VMEM((rows, width), F32), pltpu.SemaphoreType.DMA((rows // block,))],
        compiler_params=params,
        cost_estimate=pl.CostEstimate(
            flops=4 * half * rows * width + 2 * picks * rows * width,
            bytes_accessed=8 * rows * width,
            transcendentals=0,
        ),
        name="voxel_grad",
    )(picked, own_vox, partner, dl_near, dl_far, near, far)
    return (voxel_grad[None], phrase_grad)


def solution(mesh):
    placed = (P("crop", "batch", None), P("batch", None), P("batch"), P("crop", "batch", None))
    return jax.shard_map(
        local,
        mesh=mesh,
        in_specs=placed,
        out_specs=(P("crop", "batch", None), P("batch", None)),
        check_vma=False,
    )
```

time: 42.4 us -> 39.8 us (0.939)
  waiting for transfers between devices: 2.13 us -> 0.17 us
  other arithmetic: 0.68 us -> 2.14 us
  local copies, waits for them, and re-layouts: 3.28 us -> 1.94 us
  Pallas kernels: 5.57 us -> 4.76 us
    ppermute x1, waiting for transfers between devices: 1.39 us -> 0.01 us  [local(): far = lax.ppermute(near, 'batch', cores)]
    unnamed x12 -> x8, local copies, waits for them, and re-layouts: 3.28 us -> 1.92 us
    pallas_call x3 -> x4, Pallas kernels: 5.57 us -> 4.76 us  [the longest x1 2.29 us: local(): pl.pallas_call(functools.partial(grad_kernel, scale, block), out_shape=ja...]
    ppermute x1, waiting for transfers between devices: 0.74 us -> 0.01 us  [local(): partner = lax.ppermute(chosen, 'crop', swap)]
    concatenate x0 -> x1, other arithmetic: none -> 0.72 us  [local(): own_block = jnp.concatenate([phrases, id_parts], axis=1)]
    shift_right_arithmetic x0 -> x1, other arithmetic: none -> 0.66 us  [local(): pair_ids[:, None] >> 8]
  transfers between devices with their start and end apart: 4 -> 4, of which waited for: 2 -> 1; matrix products, arithmetic and copies ran while one was open for 0% -> 0% of each run, Pallas kernels for 7% -> 10%
where the time goes in v2:
time: 39.8 us; the launch traced here: 39.5 us
  blocking collectives  26.2 us (66%)
  Pallas kernels  4.76 us (12%)
  starting transfers between devices  3.6 us (9%)
  other arithmetic  2.14 us (5%)
  local copies, waits for them, and re-layouts  1.94 us (5%)
  between operations  0.72 us (2%)
    all_to_all x1, blocking collectives, local(): lax.all_to_all(packed, 'batch', 0, 0, tiled=True, axis_index_groups=same_...  14.6 us
    all_to_all x1, blocking collectives, local(): lax.all_to_all(near_terms + from_core, 'batch', 0, 0, tiled=True, axis_in...  11.6 us
    pallas_call x1, Pallas kernels, local(): pl.pallas_call(functools.partial(grad_kernel, scale, block), out_shape=ja...  2.29 us
    unnamed x8, local copies, waits for them, and re-layouts  1.92 us
    ppermute x1, starting transfers between devices, local(): partner = lax.ppermute(chosen, 'crop', swap)  1.52 us
    ppermute x1, starting transfers between devices, local(): phrase_grad = own + lax.ppermute(own, 'crop', swap)  1.51 us
    pallas_call x1, Pallas kernels, local(): pl.pallas_call(margin_kernel, out_shape=jax.ShapeDtypeStruct((picks, widt...  1.01 us
  transfers between devices with their start and end apart: 4, of which 1 were waited for; matrix products, arithmetic and copies ran while one was open for 0% of the time, Pallas kernels for 10%

profile of v2, /device:TPU:0, one launch (start us, length us, event | category | flops | bytes accessed | tf_op | source)
XLA Modules:
  0.0 39.5 jit_solution(7581780377809105955)
XLA Ops:
  0.6 0.7 %broadcast_shift-right-arithmetic_fusion = (s32[16]{0:T(128)S(1)}, s32[16]{0:T(128)S(1)}) fusion(s32[16]{0:T(128)} %param.6), kind=kLoop, calls=%fused_computation.4 | loop fusion | flops 32 | bytes 192 | tf_op jit(solution)/shard_map/shift_right_arithmetic | solution.py:127
  1.3 0.1 select_convert_fusion
  1.4 0.7 %pad_maximum_fusion = bf16[16,640]{1,0:T(8,128)(2,1)S(1)} fusion(bf16[16,128]{1,0:T(8,128)(2,1)S(1)} %select_convert_fusion, bf16[16,512]{1,0:T(8,128)(2,1)} %param.5), kind=kLoop, calls=%fused_computation | loop fusion | flops 40960 | bytes 40960 | tf_op jit(solution)/shard_map/concatenate | solution.py:129
  2.1 14.6 %all_to_all.17 = bf16[8,16,640]{2,1,0:T(8,128)(2,1)S(1)} all-to-all(bf16[8,16,640]{2,1,0:T(8,128)(2,1)S(1)} %broadcast_in_dim.29), channel_id=1, replica_groups={{0,4,8,12,16,20,24,28},{2,6,10,14,18,22,26,30},{1,5,9,13,17,21,25,29},{..., dimensions={0} | all-to-all | bytes 327680 | tf_op jit(solution)/shard_map/all_to_all | solution.py:131
  16.7 0.0 collective-permute-start
  16.7 0.0 copy-start
  16.7 1.2 %copy-done = bf16[1,1024,512]{2,1,0:T(8,128)(2,1)S(1)} copy-done((bf16[1,1024,512]{2,1,0:T(8,128)(2,1)S(1)}, bf16[1,1024,512]{2,1,0:T(8,128)(2,1)}, u32[]{:S(2)}) %copy-start) | copy-done | bytes 1048600
  18.0 0.0 copy-start.2
  18.0 0.7 %copy-done.2 = s32[1,1,512]{2,1,0:T(1,128)S(1)} copy-done((s32[1,1,512]{2,1,0:T(1,128)S(1)}, s32[1,1,512]{2,1,0:T(1,128)}, u32[]{:S(2)}) %copy-start.2) | copy-done | bytes 2072
  18.6 1.0 %margin_rows.1 = bf16[512,512]{1,0:T(8,128)(2,1)S(1)} custom-call(bf16[1024,512]{1,0:T(8,128)(2,1)S(1)} %bitcast.6, s32[1,512]{1,0:T(1,128)S(1)} %bitcast.13), custom_call_target="tpu_custom_call" | custom-call | flops 536870912 | bytes 1048576 | tf_op jit(solution)/shard_map/margin_rows/pallas_call | solution.py:135
  19.7 0.0 copy-start.1
  19.7 0.0 copy-start.3
  19.7 0.0 collective-permute-done.packed_ref.far_ref
  19.7 0.7 %terms.3 = (bf16[128,1024]{1,0:T(8,128)(2,1)S(1)}, f32[128,512]{1,0:T(8,128)S(1)}) custom-call(s32[1]{0:T(128)} %bitcast.2.base_ref, bf16[1024,512]{1,0:T(8,128)(2,1)S(1)} %bitcast.7, bf16[128,640]{1,0:T(8,128)(2,1)S(1)} %collective-permute-done.packed_ref.far_ref), custom_call_target="tpu_custom_call" | custom-call | flops 268435456 | bytes 1048576 | tf_op jit(solution)/shard_map/terms/pallas_call | solution.py:166
  20.4 0.6 %collective-permute-start.1 = (f32[128,512]{1,0:T(8,128)S(1)}, f32[128,512]{1,0:T(8,128)S(1)}, u32[]{:S(2)}, u32[]{:S(2)}) collective-permute-start(f32[128,512]{1,0:T(8,128)S(1)} %get-tuple-element.12), channel_id=1, source_target_pairs={{0,2},{2,0},{4,6},{6,4},{8,10},{10,8},{12,14},{14,12},{16,18},{18,... | collective-permute-start | bytes 786440 | tf_op jit(solution)/shard_map/ppermute | solution.py:167
  21.0 1.5 %collective-permute-start.2 = (bf16[512,512]{1,0:T(8,128)(2,1)S(1)}, bf16[512,512]{1,0:T(8,128)(2,1)S(1)}, u32[]{:S(2)}, u32[]{:S(2)}) collective-permute-start(bf16[512,512]{1,0:T(8,128)(2,1)S(1)} %margin_rows.1), channel_id=1, source_target_pairs={{0,1},{1,0},{2,3},{3,2},{4,5},{5,4},{6,7},{7,6},{8,9},{9,8},{10,11... | collective-permute-start | bytes 1572872 | tf_op jit(solution)/shard_map/ppermute | solution.py:165
  22.5 0.7 %terms.2 = (bf16[128,1024]{1,0:T(8,128)(2,1)S(1)}, f32[128,512]{1,0:T(8,128)S(1)}) custom-call(s32[1]{0:T(128)} %bitcast.2.base_ref, bf16[1024,512]{1,0:T(8,128)(2,1)S(1)} %bitcast.8, bf16[128,640]{1,0:T(8,128)(2,1)S(1)} %bitcast.11), custom_call_target="tpu_custom_call" | custom-call | flops 268435456 | bytes 1048576 | tf_op jit(solution)/shard_map/terms/pallas_call | solution.py:168
  23.3 0.0 collective-permute-done.1
  23.3 11.6 %all_to_all.18 = f32[8,16,512]{2,1,0:T(8,128)S(1)} all-to-all(f32[8,16,512]{2,1,0:T(8,128)S(1)} %bitcast.16), channel_id=1, replica_groups={{0,4,8,12,16,20,24,28},{2,6,10,14,18,22,26,30},{1,5,9,13,17,21,25,29},{..., dimensions={0} | all-to-all | bytes 524288 | tf_op jit(solution)/shard_map/all_to_all | solution.py:170
  34.9 0.0 collective-permute-done.2.partner_ref
  34.9 1.5 %collective-permute-start.3 = (f32[16,512]{1,0:T(8,128)S(1)}, f32[16,512]{1,0:T(8,128)S(1)}, u32[]{:S(2)}, u32[]{:S(2)}) collective-permute-start(f32[16,512]{1,0:T(8,128)S(1)} %reduce_sum.9), channel_id=1, source_target_pairs={{0,1},{1,0},{2,3},{3,2},{4,5},{5,4},{6,7},{7,6},{8,9},{9,8},{10,11... | collective-permute-start | bytes 98312 | tf_op jit(solution)/shard_map/ppermute | solution.py:175
  36.4 0.0 copy-done.1
  36.4 0.0 copy-done.3
  36.4 2.3 %voxel_grad.1 = f32[1024,512]{1,0:T(8,128)} custom-call(s32[1,512]{1,0:T(1,128)S(1)} %bitcast.14, bf16[1024,512]{1,0:T(8,128)(2,1)S(1)} %bitcast.9, bf16[512,512]{1,0:T(8,128)(2,1)S(1)} %collective-permute-done.2.partner_ref, bf16[128,1024]{1,0:T(8,128)(2,1)S(1)} %get-tuple-element.15.dl_near, bf16[128,1024]{1,0:T(8,128)(2,1)S(1)} %get-tuple-element.16.dl_far, ...), custom_call_target="tpu_custom_call" | custom-call | flops 805306368 | bytes 4194304 | tf_op jit(solution)/shard_map/voxel_grad/pallas_call | solution.py:178
  38.7 0.2 collective-permute-done.3
  38.9 0.6 %add.7 = f32[16,512]{1,0:T(8,128)} add(f32[16,512]{1,0:T(8,128)S(1)} %reduce_sum.9, f32[16,512]{1,0:T(8,128)S(1)} %collective-permute-done.3) | non-fusion elementwise | flops 8192 | bytes 98304 | tf_op jit(solution)/shard_map/add | solution.py:175
  (4 shorter events, 0.1 us)
Async XLA Ops:
  16.7 3.0 %collective-permute-start = (bf16[128,640]{1,0:T(8,128)(2,1)S(1)}, bf16[128,640]{1,0:T(8,128)(2,1)S(1)}, u32[]{:S(2)}, u32[]{:S(2)}) collective-permute-start(bf16[128,640]{1,0:T(8,128)(2,1)S(1)} %bitcast.10), channel_id=1, source_target_pairs={{0,2},{2,0},{4,6},{6,4},{8,10},{10,8},{12,14},{14,12},{16,18},{18,... | collective-permute-start | bytes 491528 | tf_op jit(solution)/shard_map/ppermute | solution.py:132
  16.7 1.2 %copy-start = (bf16[1,1024,512]{2,1,0:T(8,128)(2,1)S(1)}, bf16[1,1024,512]{2,1,0:T(8,128)(2,1)}, u32[]{:S(2)}) copy-start(bf16[1,1024,512]{2,1,0:T(8,128)(2,1)} %param.4) | copy-start | bytes 3145732
  18.0 0.7 %copy-start.2 = (s32[1,1,512]{2,1,0:T(1,128)S(1)}, s32[1,1,512]{2,1,0:T(1,128)}, u32[]{:S(2)}) copy-start(s32[1,1,512]{2,1,0:T(1,128)} %param.7) | copy-start | bytes 6148
  19.7 16.8 %copy-start.1 = (bf16[1,1024,512]{2,1,0:T(8,128)(2,1)S(1)}, bf16[1,1024,512]{2,1,0:T(8,128)(2,1)}, u32[]{:S(2)}) copy-start(bf16[1,1024,512]{2,1,0:T(8,128)(2,1)} %param.4) | copy-start | bytes 3145732
  19.7 16.8 %copy-start.3 = (s32[1,1,512]{2,1,0:T(1,128)S(1)}, s32[1,1,512]{2,1,0:T(1,128)}, u32[]{:S(2)}) copy-start(s32[1,1,512]{2,1,0:T(1,128)} %param.7) | copy-start | bytes 6148
  20.4 2.8 %collective-permute-start.1 = (f32[128,512]{1,0:T(8,128)S(1)}, f32[128,512]{1,0:T(8,128)S(1)}, u32[]{:S(2)}, u32[]{:S(2)}) collective-permute-start(f32[128,512]{1,0:T(8,128)S(1)} %get-tuple-element.12), channel_id=1, source_target_pairs={{0,2},{2,0},{4,6},{6,4},{8,10},{10,8},{12,14},{14,12},{16,18},{18,... | collective-permute-start | bytes 786440 | tf_op jit(solution)/shard_map/ppermute | solution.py:167
  21.0 13.9 %collective-permute-start.2 = (bf16[512,512]{1,0:T(8,128)(2,1)S(1)}, bf16[512,512]{1,0:T(8,128)(2,1)S(1)}, u32[]{:S(2)}, u32[]{:S(2)}) collective-permute-start(bf16[512,512]{1,0:T(8,128)(2,1)S(1)} %margin_rows.1), channel_id=1, source_target_pairs={{0,1},{1,0},{2,3},{3,2},{4,5},{5,4},{6,7},{7,6},{8,9},{9,8},{10,11... | collective-permute-start | bytes 1572872 | tf_op jit(solution)/shard_map/ppermute | solution.py:165
  34.9 4.0 %collective-permute-start.3 = (f32[16,512]{1,0:T(8,128)S(1)}, f32[16,512]{1,0:T(8,128)S(1)}, u32[]{:S(2)}, u32[]{:S(2)}) collective-permute-start(f32[16,512]{1,0:T(8,128)S(1)} %reduce_sum.9), channel_id=1, source_target_pairs={{0,1},{1,0},{2,3},{3,2},{4,5},{5,4},{6,7},{7,6},{8,9},{9,8},{10,11... | collective-permute-start | bytes 98312 | tf_op jit(solution)/shard_map/ppermute | solution.py:175

commit v3 on v2

--- a/solution.py
+++ b/solution.py
@@ -21,26 +21,22 @@
     return pl.BlockSpec(memory_space=pltpu.VMEM)
 
 
-def pack_kernel(copies, ids_hbm, phrases_hbm, out_ref, ids_ref, phrases_ref, sems):
+def cells_kernel(owned, ids_ref, out_ref):
+    row = lax.broadcasted_iota(jnp.int32, out_ref.shape, 0)
+    lane = lax.broadcasted_iota(jnp.int32, out_ref.shape, 1)
+    ids = ids_ref[...]
+    cells = jnp.where(lane == row, ids >> 8, jnp.where(lane == row + owned, ids & 255, 0))
+    out_ref[...] = cells.astype(F32).astype(BF16)
+
+
+def repeat_kernel(copies, phrases_ref, cells_ref, out_ref):
     rows, width = phrases_ref.shape
-    get_ids = pltpu.make_async_copy(ids_hbm, ids_ref, sems.at[0])
-    get_phrases = pltpu.make_async_copy(phrases_hbm, phrases_ref, sems.at[1])
-    get_ids.start()
-    get_phrases.start()
-    row = lax.broadcasted_iota(jnp.int32, (rows, LANES), 0)
-    lane = lax.broadcasted_iota(jnp.int32, (rows, LANES), 1)
-    get_ids.wait()
-    ids = jnp.zeros((rows, LANES), jnp.int32)
-    for i in range(rows):
-        ids = jnp.where(row == i, ids_ref[i], ids)
-    parts = jnp.where(lane == 0, ids >> 8, jnp.where(lane == 1, ids & 255, 0))
-    parts = parts.astype(F32).astype(BF16)
-    get_phrases.wait()
-    phrases = phrases_ref[...]
+    phrases, cells = phrases_ref[...], cells_ref[...]
 
     def put(i):
-        out_ref[pl.ds(pl.multiple_of(i * rows, rows), rows), :width] = phrases
-        out_ref[pl.ds(pl.multiple_of(i * rows, rows), rows), width:] = parts
+        at = pl.ds(pl.multiple_of(i * rows, rows), rows)
+        out_ref[at, :width] = phrases
+        out_ref[at, width:] = cells
 
     if copies <= 16:
         for i in range(copies):
@@ -57,7 +53,7 @@
     chosen_ref[...] = jnp.dot(onehot, vox_ref[...], preferred_element_type=F32).astype(BF16)
 
 
-def terms_kernel(scale, base_ref, vox_ref, packed_ref, dl_ref, out_ref):
+def terms_kernel(scale, owned, base_ref, vox_ref, packed_ref, dl_ref, out_ref):
     rows, width = vox_ref.shape
     half = packed_ref.shape[0]
     block = min(half, 128)
@@ -67,8 +63,9 @@
     def terms(start):
         at = pl.ds(pl.multiple_of(start, block), block)
         phrases = packed_ref[at, :width]
-        parts = packed_ref[at, width:].astype(F32)
-        ids = parts[:, 0:1] * 256.0 + parts[:, 1:2]
+        cells = packed_ref[at, width:].astype(F32)
+        lane = lax.broadcasted_iota(jnp.int32, cells.shape, 1)
+        ids = jnp.sum(jnp.where(lane < owned, cells * 256.0, cells), axis=1, keepdims=True)
         logit = lax.dot_general(
             phrases, vox_ref[...], (((1,), (1,)), ((), ())), preferred_element_type=F32
         )
@@ -123,11 +120,24 @@
     smem = pl.BlockSpec(memory_space=pltpu.SMEM)
     hbm = pl.BlockSpec(memory_space=pltpu.HBM)
 
-    lane = lax.broadcasted_iota(jnp.int32, (owned, LANES), 1)
-    id_parts = jnp.where(lane == 0, pair_ids[:, None] >> 8, pair_ids[:, None] & 255)
-    id_parts = id_parts.astype(BF16)
-    own_block = jnp.concatenate([phrases, id_parts], axis=1)
-    packed = jnp.broadcast_to(own_block[None], (members, owned, width + LANES)).reshape(half, width + LANES)
+    cells = pl.pallas_call(
+        functools.partial(cells_kernel, owned),
+        out_shape=jax.ShapeDtypeStruct((owned, LANES), BF16),
+        in_specs=[vmem_spec()],
+        out_specs=vmem_spec(),
+        compiler_params=params,
+        cost_estimate=pl.CostEstimate(flops=10**9, bytes_accessed=1024, transcendentals=0),
+        name="id_cells",
+    )(jnp.pad(jnp.concatenate([pair_ids, pair_ids]), (0, LANES - 2 * owned))[None, :])
+    packed = pl.pallas_call(
+        functools.partial(repeat_kernel, members),
+        out_shape=jax.ShapeDtypeStruct((half, width + LANES), BF16),
+        in_specs=[vmem_spec()] * 2,
+        out_specs=vmem_spec(),
+        compiler_params=params,
+        cost_estimate=pl.CostEstimate(flops=10**9, bytes_accessed=1024, transcendentals=0),
+        name="repeat",
+    )(phrases, cells)
     near = lax.all_to_all(packed, "batch", 0, 0, tiled=True, axis_index_groups=same_core)
     far = lax.ppermute(near, "batch", cores)
 
@@ -146,7 +156,7 @@
 
     base = (lax.axis_index("batch") * rows).astype(jnp.int32).reshape(1)
     terms = pl.pallas_call(
-        functools.partial(terms_kernel, scale),
+        functools.partial(terms_kernel, scale, owned),
         out_shape=[
             jax.ShapeDtypeStruct((half, rows), BF16),
             jax.ShapeDtypeStruct((half, width), F32),

time: 39.8 us -> 37.6 us (0.945)
  local copies, waits for them, and re-layouts: 1.94 us -> 0.02 us
  other arithmetic: 2.14 us -> 1.48 us
  blocking collectives: 26.2 us -> 26.6 us
    unnamed x8 -> x6, local copies, waits for them, and re-layouts: 1.92 us -> 0.02 us
    shift_right_arithmetic x1 -> x0, other arithmetic: 0.66 us -> none  [local(): pair_ids[:, None] >> 8]
  transfers between devices with their start and end apart: 4 -> 4, of which waited for: 1 -> 2; matrix products, arithmetic and copies ran while one was open for 0% -> 0% of each run, Pallas kernels for 10% -> 11%
where the time goes in v3:
time: 37.6 us; the launch traced here: 37.4 us
  blocking collectives  26.6 us (71%)
  Pallas kernels  4.77 us (13%)
  starting transfers between devices  3.27 us (9%)
  other arithmetic  1.48 us (4%)
  between operations  0.73 us (2%)
  waiting for transfers between devices  0.54 us (1%)
    all_to_all x1, blocking collectives, local(): lax.all_to_all(packed, 'batch', 0, 0, tiled=True, axis_index_groups=same_...  14.7 us
    all_to_all x1, blocking collectives, local(): lax.all_to_all(near_terms + from_core, 'batch', 0, 0, tiled=True, axis_in...  11.8 us
    pallas_call x1, Pallas kernels, local(): pl.pallas_call(functools.partial(grad_kernel, scale, block), out_shape=ja...  2.29 us
    ppermute x1, starting transfers between devices, local(): partner = lax.ppermute(chosen, 'crop', swap)  1.54 us
    ppermute x1, starting transfers between devices, local(): phrase_grad = own + lax.ppermute(own, 'crop', swap)  1.52 us
    pallas_call x1, Pallas kernels, local(): pl.pallas_call(margin_kernel, out_shape=jax.ShapeDtypeStruct((picks, widt...  1.01 us
    concatenate x1, other arithmetic, local(): jnp.concatenate([pair_ids, pair_ids])  0.81 us
  transfers between devices with their start and end apart: 4, of which 2 were waited for; matrix products, arithmetic and copies ran while one was open for 0% of the time, Pallas kernels for 11%

profile of v3, /device:TPU:0, one launch (start us, length us, event | category | flops | bytes accessed | tf_op | source)
XLA Modules:
  0.0 37.4 jit_solution(15253033057719493822)
XLA Ops:
  0.6 0.0 copy-start.2
  0.6 0.8 %pad_add_fusion = s32[32]{0:T(128)S(1)} fusion(s32[16]{0:T(128)} %param.6), kind=kLoop, calls=%fused_computation | loop fusion | flops 32 | bytes 192 | tf_op jit(solution)/shard_map/concatenate | solution.py:131
  1.5 0.0 copy-done.2
  1.5 0.0 copy-start
  1.5 0.0 copy-start.1
  1.5 14.7 %all_to_all.20 = bf16[8,16,640]{2,1,0:T(8,128)(2,1)S(1)} all-to-all(bf16[8,16,640]{2,1,0:T(8,128)(2,1)S(1)} %bitcast.16), channel_id=1, replica_groups={{0,4,8,12,16,20,24,28},{2,6,10,14,18,22,26,30},{1,5,9,13,17,21,25,29},{..., dimensions={0} | all-to-all | bytes 327680 | tf_op jit(solution)/shard_map/all_to_all | solution.py:141
  16.3 0.0 collective-permute-start
  16.3 0.0 copy-done
  16.3 0.0 copy-done.1
  16.3 1.0 %margin_rows.1 = bf16[512,512]{1,0:T(8,128)(2,1)S(1)} custom-call(bf16[1024,512]{1,0:T(8,128)(2,1)S(1)} %bitcast.9, s32[1,512]{1,0:T(1,128)S(1)} %bitcast.17), custom_call_target="tpu_custom_call" | custom-call | flops 536870912 | bytes 1048576 | tf_op jit(solution)/shard_map/margin_rows/pallas_call | solution.py:145
  17.3 0.4 collective-permute-done.packed_ref.far_ref
  17.7 0.7 %terms.3 = (bf16[128,1024]{1,0:T(8,128)(2,1)S(1)}, f32[128,512]{1,0:T(8,128)S(1)}) custom-call(s32[1]{0:T(128)} %bitcast.2.base_ref, bf16[1024,512]{1,0:T(8,128)(2,1)S(1)} %bitcast.10, bf16[128,640]{1,0:T(8,128)(2,1)S(1)} %collective-permute-done.packed_ref.far_ref), custom_call_target="tpu_custom_call" | custom-call | flops 268435456 | bytes 1048576 | tf_op jit(solution)/shard_map/terms/pallas_call | solution.py:176
  18.4 0.2 collective-permute-start.1
  18.6 1.5 %collective-permute-start.2 = (bf16[512,512]{1,0:T(8,128)(2,1)S(1)}, bf16[512,512]{1,0:T(8,128)(2,1)S(1)}, u32[]{:S(2)}, u32[]{:S(2)}) collective-permute-start(bf16[512,512]{1,0:T(8,128)(2,1)S(1)} %margin_rows.1), channel_id=1, source_target_pairs={{0,1},{1,0},{2,3},{3,2},{4,5},{5,4},{6,7},{7,6},{8,9},{9,8},{10,11... | collective-permute-start | bytes 1572872 | tf_op jit(solution)/shard_map/ppermute | solution.py:175
  20.1 0.7 %terms.2 = (bf16[128,1024]{1,0:T(8,128)(2,1)S(1)}, f32[128,512]{1,0:T(8,128)S(1)}) custom-call(s32[1]{0:T(128)} %bitcast.2.base_ref, bf16[1024,512]{1,0:T(8,128)(2,1)S(1)} %bitcast.11, bf16[128,640]{1,0:T(8,128)(2,1)S(1)} %bitcast.14), custom_call_target="tpu_custom_call" | custom-call | flops 268435456 | bytes 1048576 | tf_op jit(solution)/shard_map/terms/pallas_call | solution.py:178
  20.9 0.0 collective-permute-done.1
  20.9 11.8 %all_to_all.21 = f32[8,16,512]{2,1,0:T(8,128)S(1)} all-to-all(f32[8,16,512]{2,1,0:T(8,128)S(1)} %bitcast.20), channel_id=1, replica_groups={{0,4,8,12,16,20,24,28},{2,6,10,14,18,22,26,30},{1,5,9,13,17,21,25,29},{..., dimensions={0} | all-to-all | bytes 524288 | tf_op jit(solution)/shard_map/all_to_all | solution.py:180
  32.8 0.0 collective-permute-done.2.partner_ref
  32.8 1.5 %collective-permute-start.3 = (f32[16,512]{1,0:T(8,128)S(1)}, f32[16,512]{1,0:T(8,128)S(1)}, u32[]{:S(2)}, u32[]{:S(2)}) collective-permute-start(f32[16,512]{1,0:T(8,128)S(1)} %reduce_sum.9), channel_id=1, source_target_pairs={{0,1},{1,0},{2,3},{3,2},{4,5},{5,4},{6,7},{7,6},{8,9},{9,8},{10,11... | collective-permute-start | bytes 98312 | tf_op jit(solution)/shard_map/ppermute | solution.py:185
  34.3 2.3 %voxel_grad.1 = f32[1024,512]{1,0:T(8,128)} custom-call(s32[1,512]{1,0:T(1,128)S(1)} %bitcast.18, bf16[1024,512]{1,0:T(8,128)(2,1)S(1)} %bitcast.12, bf16[512,512]{1,0:T(8,128)(2,1)S(1)} %collective-permute-done.2.partner_ref, bf16[128,1024]{1,0:T(8,128)(2,1)S(1)} %get-tuple-element.15.dl_near, bf16[128,1024]{1,0:T(8,128)(2,1)S(1)} %get-tuple-element.16.dl_far, ...), custom_call_target="tpu_custom_call" | custom-call | flops 805306368 | bytes 4194304 | tf_op jit(solution)/shard_map/voxel_grad/pallas_call | solution.py:188
  36.6 0.2 collective-permute-done.3
  36.8 0.6 %add.9 = f32[16,512]{1,0:T(8,128)} add(f32[16,512]{1,0:T(8,128)S(1)} %reduce_sum.9, f32[16,512]{1,0:T(8,128)S(1)} %collective-permute-done.3) | non-fusion elementwise | flops 8192 | bytes 98304 | tf_op jit(solution)/shard_map/add | solution.py:185
  (5 shorter events, 0.1 us)
Async XLA Ops:
  0.6 0.8 %copy-start.2 = (bf16[16,512]{1,0:T(8,128)(2,1)S(1)}, bf16[16,512]{1,0:T(8,128)(2,1)}, u32[]{:S(2)}) copy-start(bf16[16,512]{1,0:T(8,128)(2,1)} %phrases_ref.1) | copy-start | bytes 49156
  1.5 14.8 %copy-start = (bf16[1,1024,512]{2,1,0:T(8,128)(2,1)S(1)}, bf16[1,1024,512]{2,1,0:T(8,128)(2,1)}, u32[]{:S(2)}) copy-start(bf16[1,1024,512]{2,1,0:T(8,128)(2,1)} %param.4) | copy-start | bytes 3145732
  1.5 14.8 %copy-start.1 = (s32[1,1,512]{2,1,0:T(1,128)S(1)}, s32[1,1,512]{2,1,0:T(1,128)}, u32[]{:S(2)}) copy-start(s32[1,1,512]{2,1,0:T(1,128)} %param.7) | copy-start | bytes 6148
  16.3 1.4 %collective-permute-start = (bf16[128,640]{1,0:T(8,128)(2,1)S(1)}, bf16[128,640]{1,0:T(8,128)(2,1)S(1)}, u32[]{:S(2)}, u32[]{:S(2)}) collective-permute-start(bf16[128,640]{1,0:T(8,128)(2,1)S(1)} %bitcast.13), channel_id=1, source_target_pairs={{0,2},{2,0},{4,6},{6,4},{8,10},{10,8},{12,14},{14,12},{16,18},{18,... | collective-permute-start | bytes 491528 | tf_op jit(solution)/shard_map/ppermute | solution.py:142
  18.4 2.5 %collective-permute-start.1 = (f32[128,512]{1,0:T(8,128)S(1)}, f32[128,512]{1,0:T(8,128)S(1)}, u32[]{:S(2)}, u32[]{:S(2)}) collective-permute-start(f32[128,512]{1,0:T(8,128)S(1)} %get-tuple-element.12), channel_id=1, source_target_pairs={{0,2},{2,0},{4,6},{6,4},{8,10},{10,8},{12,14},{14,12},{16,18},{18,... | collective-permute-start | bytes 786440 | tf_op jit(solution)/shard_map/ppermute | solution.py:177
  18.6 14.2 %collective-permute-start.2 = (bf16[512,512]{1,0:T(8,128)(2,1)S(1)}, bf16[512,512]{1,0:T(8,128)(2,1)S(1)}, u32[]{:S(2)}, u32[]{:S(2)}) collective-permute-start(bf16[512,512]{1,0:T(8,128)(2,1)S(1)} %margin_rows.1), channel_id=1, source_target_pairs={{0,1},{1,0},{2,3},{3,2},{4,5},{5,4},{6,7},{7,6},{8,9},{9,8},{10,11... | collective-permute-start | bytes 1572872 | tf_op jit(solution)/shard_map/ppermute | solution.py:175
  32.8 4.0 %collective-permute-start.3 = (f32[16,512]{1,0:T(8,128)S(1)}, f32[16,512]{1,0:T(8,128)S(1)}, u32[]{:S(2)}, u32[]{:S(2)}) collective-permute-start(f32[16,512]{1,0:T(8,128)S(1)} %reduce_sum.9), channel_id=1, source_target_pairs={{0,1},{1,0},{2,3},{3,2},{4,5},{5,4},{6,7},{7,6},{8,9},{9,8},{10,11... | collective-permute-start | bytes 98312 | tf_op jit(solution)/shard_map/ppermute | solution.py:185

commit v4 on v3

--- a/solution.py
+++ b/solution.py
@@ -29,28 +29,28 @@
     out_ref[...] = cells.astype(F32).astype(BF16)
 
 
-def repeat_kernel(copies, phrases_ref, cells_ref, out_ref):
-    rows, width = phrases_ref.shape
-    phrases, cells = phrases_ref[...], cells_ref[...]
-
-    def put(i):
-        at = pl.ds(pl.multiple_of(i * rows, rows), rows)
-        out_ref[at, :width] = phrases
-        out_ref[at, width:] = cells
-
-    if copies <= 16:
-        for i in range(copies):
-            put(i)
-    else:
-        pl.loop(0, copies)(put)
+def stack_kernel(*refs):
+    out_ref = refs[-1]
+    start = 0
+    for ref in refs[:-1]:
+        rows = ref.shape[0]
+        out_ref[start : start + rows, :] = ref[...]
+        start += rows
+
+
+def beside_kernel(phrases_ref, cells_ref, out_ref):
+    width = phrases_ref.shape[1]
+    out_ref[:, :width] = phrases_ref[...]
+    out_ref[:, width:] = cells_ref[...]
 
 
 def margin_kernel(vox_ref, idx_ref, chosen_ref):
     rows = vox_ref.shape[0]
     picks = idx_ref.shape[1]
-    column = jnp.broadcast_to(idx_ref[...], (8, picks)).T[:, 0:1]
-    onehot = (column == lax.broadcasted_iota(jnp.int32, (picks, rows), 1)).astype(F32).astype(BF16)
-    chosen_ref[...] = jnp.dot(onehot, vox_ref[...], preferred_element_type=F32).astype(BF16)
+    onehot = (idx_ref[...] == lax.broadcasted_iota(jnp.int32, (rows, picks), 0)).astype(F32).astype(BF16)
+    chosen_ref[...] = lax.dot_general(
+        onehot, vox_ref[...], (((0,), (0,)), ((), ())), preferred_element_type=F32
+    ).astype(BF16)
 
 
 def terms_kernel(scale, owned, base_ref, vox_ref, packed_ref, dl_ref, out_ref):
@@ -80,23 +80,31 @@
         pl.loop(0, half // block)(lambda j: terms(j * block))
 
 
-def grad_kernel(
-    scale, block, idx_ref, vox_ref, partner_ref, dl_near, dl_far, near_ref, far_ref, out_hbm, out_ref, sems
-):
+def match_kernel(scale, idx_ref, vox_ref, dl_near, dl_far, near_ref, far_ref, out_ref):
     rows, width = vox_ref.shape
     picks = idx_ref.shape[1]
+    block = math.gcd(rows, 256)
     tn = (((0,), (0,)), ((), ()))
+    for i in range(rows // block):
+        at = pl.ds(i * block, block)
+        row = i * block + lax.broadcasted_iota(jnp.int32, (block, picks), 0)
+        taken = jnp.sum((row == idx_ref[...]).astype(F32), axis=1, keepdims=True)
+        match = lax.dot_general(
+            dl_near[:, at], near_ref[:, :width], tn, preferred_element_type=F32
+        ) + lax.dot_general(dl_far[:, at], far_ref[:, :width], tn, preferred_element_type=F32)
+        out_ref[at, :] = match * scale + taken * vox_ref[at, :].astype(F32)
+
+
+def grad_kernel(block, idx_ref, part_ref, partner_ref, out_hbm, out_ref, sems):
+    rows, width = part_ref.shape
+    picks = idx_ref.shape[1]
     copies = []
     for i in range(rows // block):
         at = pl.ds(i * block, block)
         row = i * block + lax.broadcasted_iota(jnp.int32, (block, picks), 0)
-        spread = (row == idx_ref[...]).astype(F32)
-        taken = jnp.sum(spread, axis=1, keepdims=True)
-        match = lax.dot_general(
-            dl_near[:, at], near_ref[:, :width], tn, preferred_element_type=F32
-        ) + lax.dot_general(dl_far[:, at], far_ref[:, :width], tn, preferred_element_type=F32)
-        other = jnp.dot(spread.astype(BF16), partner_ref[...], preferred_element_type=F32)
-        out_ref[at, :] = match * scale + taken * vox_ref[at, :].astype(F32) - other
+        spread = (row == idx_ref[...]).astype(F32).astype(BF16)
+        other = jnp.dot(spread, partner_ref[...], preferred_element_type=F32)
+        out_ref[at, :] = part_ref[at, :] - other
         copies.append(pltpu.make_async_copy(out_ref.at[at, :], out_hbm.at[at, :], sems.at[i]))
         copies[-1].start()
     for copy in copies:
@@ -113,8 +121,6 @@
     crops = lax.axis_size("crop")
     members = devices // 2
     half = members * owned
-    same_core = [[2 * i + core for i in range(members)] for core in range(2)]
-    cores = [(i, i ^ 1) for i in range(devices)]
     swap = [(i, i ^ 1) for i in range(crops)]
     params = pltpu.CompilerParams(vmem_limit_bytes=VMEM_LIMIT)
     smem = pl.BlockSpec(memory_space=pltpu.SMEM)
@@ -129,17 +135,37 @@
         cost_estimate=pl.CostEstimate(flops=10**9, bytes_accessed=1024, transcendentals=0),
         name="id_cells",
     )(jnp.pad(jnp.concatenate([pair_ids, pair_ids]), (0, LANES - 2 * owned))[None, :])
-    packed = pl.pallas_call(
-        functools.partial(repeat_kernel, members),
-        out_shape=jax.ShapeDtypeStruct((half, width + LANES), BF16),
+    def stack(*blocks):
+        rows_out = sum(block.shape[0] for block in blocks)
+        return pl.pallas_call(
+            stack_kernel,
+            out_shape=jax.ShapeDtypeStruct((rows_out, blocks[0].shape[1]), blocks[0].dtype),
+            in_specs=[vmem_spec()] * len(blocks),
+            out_specs=vmem_spec(),
+            compiler_params=params,
+            name="stack",
+        )(*blocks)
+
+    def over(value, mask):
+        return lax.ppermute(value, "batch", [(i, i ^ mask) for i in range(devices)])
+
+    own_block = pl.pallas_call(
+        beside_kernel,
+        out_shape=jax.ShapeDtypeStruct((owned, width + LANES), BF16),
         in_specs=[vmem_spec()] * 2,
         out_specs=vmem_spec(),
         compiler_params=params,
         cost_estimate=pl.CostEstimate(flops=10**9, bytes_accessed=1024, transcendentals=0),
-        name="repeat",
+        name="own_block",
     )(phrases, cells)
-    near = lax.all_to_all(packed, "batch", 0, 0, tiled=True, axis_index_groups=same_core)
-    far = lax.ppermute(near, "batch", cores)
+
+    bits = devices.bit_length() - 1
+    top, next_top = 1 << (bits - 1), 1 << (bits - 2)
+    masks = [0, next_top | 1, top | 1, top | next_top]
+    part = stack(own_block, *[over(own_block, mask) for mask in masks[1:]])
+    for bit in reversed(range(2, bits - 2)):
+        part = stack(part, over(part, 1 << bit | 1))
+        masks = masks + [mask ^ (1 << bit | 1) for mask in masks]
 
     picked = margin_index[0]
     chosen = pl.pallas_call(
@@ -153,6 +179,11 @@
         ),
         name="margin_rows",
     )(own_vox, picked)
+
+    part, chosen = lax.optimization_barrier((part, chosen))
+    partner = lax.ppermute(chosen, "crop", swap)
+    near = stack(part, over(part, 3))
+    far = over(near, 1)
 
     base = (lax.axis_index("batch") * rows).astype(jnp.int32).reshape(1)
     terms = pl.pallas_call(
@@ -171,34 +202,46 @@
         ),
         name="terms",
     )
-    far, chosen = lax.optimization_barrier((far, chosen))
-    partner = lax.ppermute(chosen, "crop", swap)
+    dl_near, near_terms = terms(base, own_vox, near)
+    far, near_terms = lax.optimization_barrier((far, near_terms))
     dl_far, far_terms = terms(base, own_vox, far)
-    from_core = lax.ppermute(far_terms, "batch", cores)
-    dl_near, near_terms = terms(base, own_vox, near)
-
-    pieces = lax.all_to_all(
-        near_terms + from_core, "batch", 0, 0, tiled=True, axis_index_groups=same_core
-    )
-    own = jnp.sum(pieces.reshape(members, owned, width), axis=0)
-    own, partner = lax.optimization_barrier((own, partner))
+    matched = pl.pallas_call(
+        functools.partial(match_kernel, scale),
+        out_shape=jax.ShapeDtypeStruct((rows, width), F32),
+        in_specs=[vmem_spec()] * 6,
+        out_specs=vmem_spec(),
+        compiler_params=params,
+        cost_estimate=pl.CostEstimate(
+            flops=40 * half * rows * width, bytes_accessed=2 * rows * width, transcendentals=0
+        ),
+        name="match_grad",
+    )(picked, own_vox, dl_near, dl_far, near, far)
+
+    sums = near_terms + over(far_terms, 1)
+    for bit in range(1, bits - 2):
+        count = sums.shape[0] // 2
+        back = over(sums[count:], 1 << bit | 1)
+        if bit == 1:
+            back, matched = lax.optimization_barrier((back, matched))
+        sums = sums[:count] + back
+    own = sums[:owned]
+    for i in (3, 2, 1):
+        own = own + over(sums[i * owned : (i + 1) * owned], masks[i])
     phrase_grad = own + lax.ppermute(own, "crop", swap)
-
+    partner, _ = lax.optimization_barrier((partner, own))
     block = math.gcd(rows, 256)
     voxel_grad = pl.pallas_call(
-        functools.partial(grad_kernel, scale, block),
+        functools.partial(grad_kernel, block),
         out_shape=jax.ShapeDtypeStruct((rows, width), F32),
-        in_specs=[vmem_spec()] * 7,
+        in_specs=[vmem_spec()] * 3,
         out_specs=hbm,
         scratch_shapes=[pltpu.VMEM((rows, width), F32), pltpu.SemaphoreType.DMA((rows // block,))],
         compiler_params=params,
         cost_estimate=pl.CostEstimate(
-            flops=4 * half * rows * width + 2 * picks * rows * width,
-            bytes_accessed=8 * rows * width,
-            transcendentals=0,
+            flops=2 * picks * rows * width, bytes_accessed=8 * rows * width, transcendentals=0
         ),
         name="voxel_grad",
-    )(picked, own_vox, partner, dl_near, dl_far, near, far)
+    )(picked, matched, partner)
     return (voxel_grad[None], phrase_grad)
 
 

time: 37.6 us -> 36.6 us (0.973)
  blocking collectives: 26.6 us -> 0 us
  waiting for transfers between devices: 0.54 us -> 15 us
  starting transfers between devices: 3.27 us -> 14.4 us
    all_to_all x2 -> x0, blocking collectives: 26.6 us -> none  [the longest x1 14.7 us: local(): lax.all_to_all(packed, 'batch', 0, 0, tiled=True, axis_index_groups=same_...]
    ppermute x2 -> x10, waiting for transfers between devices: 0.37 us -> 13.8 us  [over(): return lax.ppermute(value, 'batch', [(i, i ^ mask) for i in range(devices)])]
    ppermute x2 -> x10, starting transfers between devices: 0.21 us -> 11.8 us  [over(): return lax.ppermute(value, 'batch', [(i, i ^ mask) for i in range(devices)])]
    ppermute x1, waiting for transfers between devices: 0.16 us -> 1.22 us  [local(): phrase_grad = own + lax.ppermute(own, 'crop', swap)]
    ppermute x1, starting transfers between devices: 1.52 us -> 1.1 us  [local(): phrase_grad = own + lax.ppermute(own, 'crop', swap)]
    pallas_call x2 -> x5, Pallas kernels: 2.31 us -> 2.49 us  [the longest x1 1.65 us: local(): pl.pallas_call(functools.partial(grad_kernel, block), out_shape=jax.Shape...]
  transfers between devices with their start and end apart: 4 -> 12, of which waited for: 2 -> 8; matrix products, arithmetic and copies ran while one was open for 0% -> 0% of each run, Pallas kernels for 11% -> 11%
where the time goes in v4:
time: 36.6 us; the launch traced here: 36.4 us
  waiting for transfers between devices  15 us (41%)
  starting transfers between devices  14.4 us (39%)
  Pallas kernels  4.68 us (13%)
  other arithmetic  1.49 us (4%)
  between operations  0.75 us (2%)
    ppermute x10, waiting for transfers between devices, over(): return lax.ppermute(value, 'batch', [(i, i ^ mask) for i in range(devices)])  13.8 us
    ppermute x10, starting transfers between devices, over(): return lax.ppermute(value, 'batch', [(i, i ^ mask) for i in range(devices)])  11.8 us
    pallas_call x1, Pallas kernels, local(): pl.pallas_call(functools.partial(grad_kernel, block), out_shape=jax.Shape...  1.65 us
    ppermute x1, starting transfers between devices, local(): partner = lax.ppermute(chosen, 'crop', swap)  1.53 us
    ppermute x1, waiting for transfers between devices, local(): phrase_grad = own + lax.ppermute(own, 'crop', swap)  1.22 us
    ppermute x1, starting transfers between devices, local(): phrase_grad = own + lax.ppermute(own, 'crop', swap)  1.1 us
    pallas_call x1, Pallas kernels, local(): pl.pallas_call(functools.partial(match_kernel, scale), out_shape=jax.Shap...  0.81 us
    concatenate x1, other arithmetic, local(): jnp.concatenate([pair_ids, pair_ids])  0.81 us
  transfers between devices with their start and end apart: 12, of which 8 were waited for; matrix products, arithmetic and copies ran while one was open for 0% of the time, Pallas kernels for 11%

profile of v4, /device:TPU:0, one launch (start us, length us, event | category | flops | bytes accessed | tf_op | source)
XLA Modules:
  0.0 36.4 jit_solution(6078593753858493405)
XLA Ops:
  0.6 0.8 %pad_add_fusion = s32[32]{0:T(128)S(1)} fusion(s32[16]{0:T(128)} %param.6), kind=kLoop, calls=%fused_computation.4 | loop fusion | flops 32 | bytes 192 | tf_op jit(solution)/shard_map/concatenate | solution.py:137
  1.5 0.0 copy-start
  1.5 0.0 copy-start.1
  1.5 5.1 %collective-permute-start.2 = (bf16[16,640]{1,0:T(8,128)(2,1)S(1)}, bf16[16,640]{1,0:T(8,128)(2,1)S(1)}, u32[]{:S(2)}, u32[]{:S(2)}) collective-permute-start(bf16[16,640]{1,0:T(8,128)(2,1)S(1)} %own_block.1.refs_0_), channel_id=1, source_target_pairs={{0,24},{2,26},{4,28},{6,30},{8,16},{10,18},{12,20},{14,22},{16,8},... | collective-permute-start | bytes 61448 | tf_op jit(solution)/shard_map/ppermute | solution.py:150
  6.6 0.0 collective-permute-start.1
  6.6 0.4 collective-permute-start
  7.0 0.7 %margin_rows.1 = bf16[512,512]{1,0:T(8,128)(2,1)S(1)} custom-call(bf16[1024,512]{1,0:T(8,128)(2,1)S(1)} %bitcast.6, s32[1,512]{1,0:T(1,128)S(1)} %bitcast.10), custom_call_target="tpu_custom_call" | custom-call | flops 536870912 | bytes 1048576 | tf_op jit(solution)/shard_map/margin_rows/pallas_call | solution.py:171
  7.7 0.6 %collective-permute-done.2.refs_3_ = bf16[16,640]{1,0:T(8,128)(2,1)S(1)} collective-permute-done((bf16[16,640]{1,0:T(8,128)(2,1)S(1)}, bf16[16,640]{1,0:T(8,128)(2,1)S(1)}, u32[]{:S(2)}, u32[]{:S(2)}) %collective-permute-start.2) | collective-permute-done | bytes 20512 | tf_op jit(solution)/shard_map/ppermute | solution.py:150
  8.4 2.3 %collective-permute-done.1.refs_2_ = bf16[16,640]{1,0:T(8,128)(2,1)S(1)} collective-permute-done((bf16[16,640]{1,0:T(8,128)(2,1)S(1)}, bf16[16,640]{1,0:T(8,128)(2,1)S(1)}, u32[]{:S(2)}, u32[]{:S(2)}) %collective-permute-start.1) | collective-permute-done | bytes 20512 | tf_op jit(solution)/shard_map/ppermute | solution.py:150
  10.7 0.7 %collective-permute-start.3 = (bf16[64,640]{1,0:T(8,128)(2,1)S(1)}, bf16[64,640]{1,0:T(8,128)(2,1)S(1)}, u32[]{:S(2)}, u32[]{:S(2)}) collective-permute-start(bf16[64,640]{1,0:T(8,128)(2,1)S(1)} %stack.2.refs_0_), channel_id=1, source_target_pairs={{0,6},{2,4},{4,2},{6,0},{8,14},{10,12},{12,10},{14,8},{16,22},{18,... | collective-permute-start | bytes 245768 | tf_op jit(solution)/shard_map/ppermute | solution.py:150
  11.5 4.0 %collective-permute-done.3.refs_1_ = bf16[64,640]{1,0:T(8,128)(2,1)S(1)} collective-permute-done((bf16[64,640]{1,0:T(8,128)(2,1)S(1)}, bf16[64,640]{1,0:T(8,128)(2,1)S(1)}, u32[]{:S(2)}, u32[]{:S(2)}) %collective-permute-start.3) | collective-permute-done | bytes 81952 | tf_op jit(solution)/shard_map/ppermute | solution.py:150
  15.5 0.2 collective-permute-start.4
  15.7 0.7 %terms.2 = (bf16[128,1024]{1,0:T(8,128)(2,1)S(1)}, f32[128,512]{1,0:T(8,128)S(1)}) custom-call(s32[1]{0:T(128)} %bitcast.3.base_ref, bf16[1024,512]{1,0:T(8,128)(2,1)S(1)} %bitcast.7, bf16[128,640]{1,0:T(8,128)(2,1)S(1)} %stack.3.packed_ref.near_ref), custom_call_target="tpu_custom_call" | custom-call | flops 268435456 | bytes 1048576 | tf_op jit(solution)/shard_map/terms/pallas_call | solution.py:205
  16.4 0.6 %collective-permute-done.4.packed_ref.far_ref = bf16[128,640]{1,0:T(8,128)(2,1)S(1)} collective-permute-done((bf16[128,640]{1,0:T(8,128)(2,1)S(1)}, bf16[128,640]{1,0:T(8,128)(2,1)S(1)}, u32[]{:S(2)}, u32[]{:S(2)}) %collective-permute-start.4) | collective-permute-done | bytes 163872 | tf_op jit(solution)/shard_map/ppermute | solution.py:150
  17.0 0.7 %terms.3 = (bf16[128,1024]{1,0:T(8,128)(2,1)S(1)}, f32[128,512]{1,0:T(8,128)S(1)}) custom-call(s32[1]{0:T(128)} %bitcast.3.base_ref, bf16[1024,512]{1,0:T(8,128)(2,1)S(1)} %bitcast.8, bf16[128,640]{1,0:T(8,128)(2,1)S(1)} %collective-permute-done.4.packed_ref.far_ref), custom_call_target="tpu_custom_call" | custom-call | flops 268435456 | bytes 1048576 | tf_op jit(solution)/shard_map/terms/pallas_call | solution.py:207
  17.7 0.2 collective-permute-start.5
  17.9 1.5 %collective-permute-start.7 = (bf16[512,512]{1,0:T(8,128)(2,1)S(1)}, bf16[512,512]{1,0:T(8,128)(2,1)S(1)}, u32[]{:S(2)}, u32[]{:S(2)}) collective-permute-start(bf16[512,512]{1,0:T(8,128)(2,1)S(1)} %margin_rows.1), channel_id=1, source_target_pairs={{0,1},{1,0},{2,3},{3,2},{4,5},{5,4},{6,7},{7,6},{8,9},{9,8},{10,11... | collective-permute-start | bytes 1572872 | tf_op jit(solution)/shard_map/ppermute | solution.py:184
  19.5 0.0 collective-permute-done.5
  19.5 1.0 %collective-permute-start.6 = (f32[64,512]{1,0:T(8,128)S(1)}, f32[64,512]{1,0:T(8,128)S(1)}, u32[]{:S(2)}, u32[]{:S(2)}) collective-permute-start(f32[64,512]{1,0:T(8,128)S(1)} %slice.24), channel_id=1, source_target_pairs={{0,6},{2,4},{4,2},{6,0},{8,14},{10,12},{12,10},{14,8},{16,22},{18,... | collective-permute-start | bytes 393224 | tf_op jit(solution)/shard_map/ppermute | solution.py:150
  20.5 0.8 %match_grad.1.part_ref = f32[1024,512]{1,0:T(8,128)S(1)} custom-call(s32[1,512]{1,0:T(1,128)S(1)} %bitcast.11, bf16[1024,512]{1,0:T(8,128)(2,1)S(1)} %bitcast.9, bf16[128,1024]{1,0:T(8,128)(2,1)S(1)} %get-tuple-element.18.dl_near, bf16[128,1024]{1,0:T(8,128)(2,1)S(1)} %get-tuple-element.19.dl_far, bf16[128,640]{1,0:T(8,128)(2,1)S(1)} %stack.3.packed_ref.near_ref, ...), custom_call_target="tpu_custom_call" | custom-call | flops 2684354560 | bytes 1048576 | tf_op jit(solution)/shard_map/match_grad/pallas_call | solution.py:208
  21.4 3.8 %collective-permute-done.6 = f32[64,512]{1,0:T(8,128)S(1)} collective-permute-done((f32[64,512]{1,0:T(8,128)S(1)}, f32[64,512]{1,0:T(8,128)S(1)}, u32[]{:S(2)}, u32[]{:S(2)}) %collective-permute-start.6) | collective-permute-done | bytes 131104 | tf_op jit(solution)/shard_map/ppermute | solution.py:150
  25.2 1.7 %collective-permute-start.8 = (f32[16,512]{1,0:T(8,128)S(1)}, f32[16,512]{1,0:T(8,128)S(1)}, u32[]{:S(2)}, u32[]{:S(2)}) collective-permute-start(f32[16,512]{1,0:T(8,128)S(1)} %get-tuple-element.24), channel_id=1, source_target_pairs={{0,24},{2,26},{4,28},{6,30},{8,16},{10,18},{12,20},{14,22},{16,8},... | collective-permute-start | bytes 98312 | tf_op jit(solution)/shard_map/ppermute | solution.py:150
  26.9 0.0 collective-permute-start.10
  26.9 2.5 %collective-permute-start.9 = (f32[16,512]{1,0:T(8,128)S(1)}, f32[16,512]{1,0:T(8,128)S(1)}, u32[]{:S(2)}, u32[]{:S(2)}) collective-permute-start(f32[16,512]{1,0:T(8,128)S(1)} %get-tuple-element.26), channel_id=1, source_target_pairs={{0,18},{2,16},{4,22},{6,20},{8,26},{10,24},{12,30},{14,28},{16,2},... | collective-permute-start | bytes 98312 | tf_op jit(solution)/shard_map/ppermute | solution.py:150
  29.4 1.8 %collective-permute-done.8 = f32[16,512]{1,0:T(8,128)S(1)} collective-permute-done((f32[16,512]{1,0:T(8,128)S(1)}, f32[16,512]{1,0:T(8,128)S(1)}, u32[]{:S(2)}, u32[]{:S(2)}) %collective-permute-start.8) | collective-permute-done | bytes 32800 | tf_op jit(solution)/shard_map/ppermute | solution.py:150
  31.2 0.6 %collective-permute-done.10 = f32[16,512]{1,0:T(8,128)S(1)} collective-permute-done((f32[16,512]{1,0:T(8,128)S(1)}, f32[16,512]{1,0:T(8,128)S(1)}, u32[]{:S(2)}, u32[]{:S(2)}) %collective-permute-start.10) | collective-permute-done | bytes 32800 | tf_op jit(solution)/shard_map/ppermute | solution.py:150
  31.8 0.0 collective-permute-done.9
  31.8 1.1 %collective-permute-start.11 = (f32[16,512]{1,0:T(8,128)S(1)}, f32[16,512]{1,0:T(8,128)S(1)}, u32[]{:S(2)}, u32[]{:S(2)}) collective-permute-start(f32[16,512]{1,0:T(8,128)S(1)} %fusion.1), channel_id=1, source_target_pairs={{0,1},{1,0},{2,3},{3,2},{4,5},{5,4},{6,7},{7,6},{8,9},{9,8},{10,11... | collective-permute-start | bytes 98312 | tf_op jit(solution)/shard_map/ppermute | solution.py:230
  32.9 0.0 collective-permute-done.7.partner_ref
  32.9 1.6 %voxel_grad.1 = f32[1024,512]{1,0:T(8,128)} custom-call(s32[1,512]{1,0:T(1,128)S(1)} %bitcast.12, f32[1024,512]{1,0:T(8,128)S(1)} %match_grad.1.part_ref, bf16[512,512]{1,0:T(8,128)(2,1)S(1)} %collective-permute-done.7.partner_ref), custom_call_target="tpu_custom_call" | custom-call | flops 536870912 | bytes 4194304 | tf_op jit(solution)/shard_map/voxel_grad/pallas_call | solution.py:233
  34.6 1.2 %collective-permute-done.11 = f32[16,512]{1,0:T(8,128)S(1)} collective-permute-done((f32[16,512]{1,0:T(8,128)S(1)}, f32[16,512]{1,0:T(8,128)S(1)}, u32[]{:S(2)}, u32[]{:S(2)}) %collective-permute-start.11) | collective-permute-done | bytes 32800 | tf_op jit(solution)/shard_map/ppermute | solution.py:230
  35.8 0.6 %add.25 = f32[16,512]{1,0:T(8,128)} add(f32[16,512]{1,0:T(8,128)S(1)} %fusion.1, f32[16,512]{1,0:T(8,128)S(1)} %collective-permute-done.11) | non-fusion elementwise | flops 8192 | bytes 98304 | tf_op jit(solution)/shard_map/add | solution.py:230
  (15 shorter events, 0.1 us)
Async XLA Ops:
  0.6 0.8 %copy-start.2 = (bf16[16,512]{1,0:T(8,128)(2,1)S(1)}, bf16[16,512]{1,0:T(8,128)(2,1)}, u32[]{:S(2)}) copy-start(bf16[16,512]{1,0:T(8,128)(2,1)} %phrases_ref.1) | copy-start | bytes 49156
  1.5 5.5 %copy-start = (bf16[1,1024,512]{2,1,0:T(8,128)(2,1)S(1)}, bf16[1,1024,512]{2,1,0:T(8,128)(2,1)}, u32[]{:S(2)}) copy-start(bf16[1,1024,512]{2,1,0:T(8,128)(2,1)} %param.4) | copy-start | bytes 3145732
  1.5 5.5 %copy-start.1 = (s32[1,1,512]{2,1,0:T(1,128)S(1)}, s32[1,1,512]{2,1,0:T(1,128)}, u32[]{:S(2)}) copy-start(s32[1,1,512]{2,1,0:T(1,128)} %param.7) | copy-start | bytes 6148
  1.5 6.9 %collective-permute-start.2 = (bf16[16,640]{1,0:T(8,128)(2,1)S(1)}, bf16[16,640]{1,0:T(8,128)(2,1)S(1)}, u32[]{:S(2)}, u32[]{:S(2)}) collective-permute-start(bf16[16,640]{1,0:T(8,128)(2,1)S(1)} %own_block.1.refs_0_), channel_id=1, source_target_pairs={{0,24},{2,26},{4,28},{6,30},{8,16},{10,18},{12,20},{14,22},{16,8},... | collective-permute-start | bytes 61448 | tf_op jit(solution)/shard_map/ppermute | solution.py:150
  6.6 4.1 %collective-permute-start.1 = (bf16[16,640]{1,0:T(8,128)(2,1)S(1)}, bf16[16,640]{1,0:T(8,128)(2,1)S(1)}, u32[]{:S(2)}, u32[]{:S(2)}) collective-permute-start(bf16[16,640]{1,0:T(8,128)(2,1)S(1)} %own_block.1.refs_0_), channel_id=1, source_target_pairs={{0,18},{2,16},{4,22},{6,20},{8,26},{10,24},{12,30},{14,28},{16,2},... | collective-permute-start | bytes 61448 | tf_op jit(solution)/shard_map/ppermute | solution.py:150
  6.6 4.1 %collective-permute-start = (bf16[16,640]{1,0:T(8,128)(2,1)S(1)}, bf16[16,640]{1,0:T(8,128)(2,1)S(1)}, u32[]{:S(2)}, u32[]{:S(2)}) collective-permute-start(bf16[16,640]{1,0:T(8,128)(2,1)S(1)} %own_block.1.refs_0_), channel_id=1, source_target_pairs={{0,10},{2,8},{4,14},{6,12},{8,2},{10,0},{12,6},{14,4},{16,26},{18,... | collective-permute-start | bytes 61448 | tf_op jit(solution)/shard_map/ppermute | solution.py:150
  10.7 4.8 %collective-permute-start.3 = (bf16[64,640]{1,0:T(8,128)(2,1)S(1)}, bf16[64,640]{1,0:T(8,128)(2,1)S(1)}, u32[]{:S(2)}, u32[]{:S(2)}) collective-permute-start(bf16[64,640]{1,0:T(8,128)(2,1)S(1)} %stack.2.refs_0_), channel_id=1, source_target_pairs={{0,6},{2,4},{4,2},{6,0},{8,14},{10,12},{12,10},{14,8},{16,22},{18,... | collective-permute-start | bytes 245768 | tf_op jit(solution)/shard_map/ppermute | solution.py:150
  15.5 1.5 %collective-permute-start.4 = (bf16[128,640]{1,0:T(8,128)(2,1)S(1)}, bf16[128,640]{1,0:T(8,128)(2,1)S(1)}, u32[]{:S(2)}, u32[]{:S(2)}) collective-permute-start(bf16[128,640]{1,0:T(8,128)(2,1)S(1)} %stack.3.packed_ref.near_ref), channel_id=1, source_target_pairs={{0,2},{2,0},{4,6},{6,4},{8,10},{10,8},{12,14},{14,12},{16,18},{18,... | collective-permute-start | bytes 491528 | tf_op jit(solution)/shard_map/ppermute | solution.py:150
  17.7 1.7 %collective-permute-start.5 = (f32[128,512]{1,0:T(8,128)S(1)}, f32[128,512]{1,0:T(8,128)S(1)}, u32[]{:S(2)}, u32[]{:S(2)}) collective-permute-start(f32[128,512]{1,0:T(8,128)S(1)} %get-tuple-element.17), channel_id=1, source_target_pairs={{0,2},{2,0},{4,6},{6,4},{8,10},{10,8},{12,14},{14,12},{16,18},{18,... | collective-permute-start | bytes 786440 | tf_op jit(solution)/shard_map/ppermute | solution.py:150
  17.9 15.0 %collective-permute-start.7 = (bf16[512,512]{1,0:T(8,128)(2,1)S(1)}, bf16[512,512]{1,0:T(8,128)(2,1)S(1)}, u32[]{:S(2)}, u32[]{:S(2)}) collective-permute-start(bf16[512,512]{1,0:T(8,128)(2,1)S(1)} %margin_rows.1), channel_id=1, source_target_pairs={{0,1},{1,0},{2,3},{3,2},{4,5},{5,4},{6,7},{7,6},{8,9},{9,8},{10,11... | collective-permute-start | bytes 1572872 | tf_op jit(solution)/shard_map/ppermute | solution.py:184
  19.5 5.6 %collective-permute-start.6 = (f32[64,512]{1,0:T(8,128)S(1)}, f32[64,512]{1,0:T(8,128)S(1)}, u32[]{:S(2)}, u32[]{:S(2)}) collective-permute-start(f32[64,512]{1,0:T(8,128)S(1)} %slice.24), channel_id=1, source_target_pairs={{0,6},{2,4},{4,2},{6,0},{8,14},{10,12},{12,10},{14,8},{16,22},{18,... | collective-permute-start | bytes 393224 | tf_op jit(solution)/shard_map/ppermute | solution.py:150
  25.2 6.0 %collective-permute-start.8 = (f32[16,512]{1,0:T(8,128)S(1)}, f32[16,512]{1,0:T(8,128)S(1)}, u32[]{:S(2)}, u32[]{:S(2)}) collective-permute-start(f32[16,512]{1,0:T(8,128)S(1)} %get-tuple-element.24), channel_id=1, source_target_pairs={{0,24},{2,26},{4,28},{6,30},{8,16},{10,18},{12,20},{14,22},{16,8},... | collective-permute-start | bytes 98312 | tf_op jit(solution)/shard_map/ppermute | solution.py:150
  26.9 4.9 %collective-permute-start.10 = (f32[16,512]{1,0:T(8,128)S(1)}, f32[16,512]{1,0:T(8,128)S(1)}, u32[]{:S(2)}, u32[]{:S(2)}) collective-permute-start(f32[16,512]{1,0:T(8,128)S(1)} %get-tuple-element.25), channel_id=1, source_target_pairs={{0,10},{2,8},{4,14},{6,12},{8,2},{10,0},{12,6},{14,4},{16,26},{18,... | collective-permute-start | bytes 98312 | tf_op jit(solution)/shard_map/ppermute | solution.py:150
  26.9 4.9 %collective-permute-start.9 = (f32[16,512]{1,0:T(8,128)S(1)}, f32[16,512]{1,0:T(8,128)S(1)}, u32[]{:S(2)}, u32[]{:S(2)}) collective-permute-start(f32[16,512]{1,0:T(8,128)S(1)} %get-tuple-element.26), channel_id=1, source_target_pairs={{0,18},{2,16},{4,22},{6,20},{8,26},{10,24},{12,30},{14,28},{16,2},... | collective-permute-start | bytes 98312 | tf_op jit(solution)/shard_map/ppermute | solution.py:150
  31.8 4.0 %collective-permute-start.11 = (f32[16,512]{1,0:T(8,128)S(1)}, f32[16,512]{1,0:T(8,128)S(1)}, u32[]{:S(2)}, u32[]{:S(2)}) collective-permute-start(f32[16,512]{1,0:T(8,128)S(1)} %fusion.1), channel_id=1, source_target_pairs={{0,1},{1,0},{2,3},{3,2},{4,5},{5,4},{6,7},{7,6},{8,9},{9,8},{10,11... | collective-permute-start | bytes 98312 | tf_op jit(solution)/shard_map/ppermute | solution.py:230

commit v5 on v4

--- a/solution.py
+++ b/solution.py
@@ -9,6 +9,7 @@
 from jax.sharding import PartitionSpec as P
 
 VOX_VOL = 256
+VOX_MAX = 6.0
 VOL_SHIFT = VOX_VOL.bit_length() - 1
 LANES = 128
 VMEM_LIMIT = 24 * 1024 * 1024
@@ -27,6 +28,18 @@
     ids = ids_ref[...]
     cells = jnp.where(lane == row, ids >> 8, jnp.where(lane == row + owned, ids & 255, 0))
     out_ref[...] = cells.astype(F32).astype(BF16)
+
+
+def to_half(value, bound):
+    gain = 2.0 ** math.floor(math.log2(65504.0**2 / bound))
+    root = jnp.sqrt(jnp.abs(value) * gain)
+    return jnp.where(value < 0, -root, root).astype(jnp.float16)
+
+
+def from_half(code, bound):
+    gain = 2.0 ** math.floor(math.log2(65504.0**2 / bound))
+    root = code.astype(F32)
+    return root * jnp.abs(root) * (1.0 / gain)
 
 
 def stack_kernel(*refs):
@@ -217,16 +230,20 @@
         name="match_grad",
     )(picked, own_vox, dl_near, dl_far, near, far)
 
+    bound = VOX_MAX * rows * scale
     sums = near_terms + over(far_terms, 1)
+    bound = 2 * bound
     for bit in range(1, bits - 2):
         count = sums.shape[0] // 2
-        back = over(sums[count:], 1 << bit | 1)
+        back = over(to_half(sums[count:], bound), 1 << bit | 1)
         if bit == 1:
             back, matched = lax.optimization_barrier((back, matched))
-        sums = sums[:count] + back
+        sums = sums[:count] + from_half(back, bound)
+        bound = 2 * bound
     own = sums[:owned]
     for i in (3, 2, 1):
-        own = own + over(sums[i * owned : (i + 1) * owned], masks[i])
+        block = to_half(sums[i * owned : (i + 1) * owned], bound)
+        own = own + from_half(over(block, masks[i]), bound)
     phrase_grad = own + lax.ppermute(own, "crop", swap)
     partner, _ = lax.optimization_barrier((partner, own))
     block = math.gcd(rows, 256)

time: 36.6 us -> 34.6 us (0.945)
  waiting for transfers between devices: 15 us -> 12.7 us
    ppermute x10, waiting for transfers between devices: 13.8 us -> 11.6 us  [over(): return lax.ppermute(value, 'batch', [(i, i ^ mask) for i in range(devices)])]
    ppermute x1, waiting for transfers between devices: 1.22 us -> 0.01 us  [local(): phrase_grad = own + lax.ppermute(own, 'crop', swap)]
    ppermute x1, waiting for transfers between devices: 0.01 us -> 1.08 us  [local(): partner = lax.ppermute(chosen, 'crop', swap)]
  transfers between devices with their start and end apart: 12 -> 12, of which waited for: 8 -> 8; matrix products, arithmetic and copies ran while one was open for 0% -> 1% of each run, Pallas kernels for 11% -> 11%
where the time goes in v5:
time: 34.6 us; the launch traced here: 34.4 us
  starting transfers between devices  14.7 us (42%)
  waiting for transfers between devices  12.7 us (37%)
  Pallas kernels  4.67 us (13%)
  other arithmetic  1.62 us (5%)
  between operations  0.76 us (2%)
    ppermute x10, starting transfers between devices, over(): return lax.ppermute(value, 'batch', [(i, i ^ mask) for i in range(devices)])  11.8 us
    ppermute x10, waiting for transfers between devices, over(): return lax.ppermute(value, 'batch', [(i, i ^ mask) for i in range(devices)])  11.6 us
    pallas_call x1, Pallas kernels, local(): pl.pallas_call(functools.partial(grad_kernel, block), out_shape=jax.Shape...  1.65 us
    ppermute x1, starting transfers between devices, local(): partner = lax.ppermute(chosen, 'crop', swap)  1.53 us
    ppermute x1, starting transfers between devices, local(): phrase_grad = own + lax.ppermute(own, 'crop', swap)  1.34 us
    ppermute x1, waiting for transfers between devices, local(): partner = lax.ppermute(chosen, 'crop', swap)  1.08 us
    concatenate x1, other arithmetic, local(): jnp.concatenate([pair_ids, pair_ids])  0.81 us
    pallas_call x1, Pallas kernels, local(): pl.pallas_call(functools.partial(match_kernel, scale), out_shape=jax.Shap...  0.8 us
  transfers between devices with their start and end apart: 12, of which 8 were waited for; matrix products, arithmetic and copies ran while one was open for 1% of the time, Pallas kernels for 11%

profile of v5, /device:TPU:0, one launch (start us, length us, event | category | flops | bytes accessed | tf_op | source)
XLA Modules:
  0.0 34.4 jit_solution(6075111225137178510)
XLA Ops:
  0.6 0.8 %pad_add_fusion = s32[32]{0:T(128)S(1)} fusion(s32[16]{0:T(128)} %param.6), kind=kLoop, calls=%fused_computation.20 | loop fusion | flops 32 | bytes 192 | tf_op jit(solution)/shard_map/concatenate | solution.py:150
  1.5 0.0 copy-start
  1.5 0.0 copy-start.1
  1.5 5.1 %collective-permute-start.2 = (bf16[16,640]{1,0:T(8,128)(2,1)S(1)}, bf16[16,640]{1,0:T(8,128)(2,1)S(1)}, u32[]{:S(2)}, u32[]{:S(2)}) collective-permute-start(bf16[16,640]{1,0:T(8,128)(2,1)S(1)} %own_block.1.refs_0_), channel_id=1, source_target_pairs={{0,24},{2,26},{4,28},{6,30},{8,16},{10,18},{12,20},{14,22},{16,8},... | collective-permute-start | bytes 61448 | tf_op jit(solution)/shard_map/ppermute | solution.py:163
  6.6 0.4 %collective-permute-start = (bf16[16,640]{1,0:T(8,128)(2,1)S(1)}, bf16[16,640]{1,0:T(8,128)(2,1)S(1)}, u32[]{:S(2)}, u32[]{:S(2)}) collective-permute-start(bf16[16,640]{1,0:T(8,128)(2,1)S(1)} %own_block.1.refs_0_), channel_id=1, source_target_pairs={{0,10},{2,8},{4,14},{6,12},{8,2},{10,0},{12,6},{14,4},{16,26},{18,... | collective-permute-start | bytes 61448 | tf_op jit(solution)/shard_map/ppermute | solution.py:163
  7.0 0.7 %margin_rows.1 = bf16[512,512]{1,0:T(8,128)(2,1)S(1)} custom-call(bf16[1024,512]{1,0:T(8,128)(2,1)S(1)} %bitcast.6, s32[1,512]{1,0:T(1,128)S(1)} %bitcast.10), custom_call_target="tpu_custom_call" | custom-call | flops 536870912 | bytes 1048576 | tf_op jit(solution)/shard_map/margin_rows/pallas_call | solution.py:184
  7.7 0.6 %collective-permute-done.2.refs_3_ = bf16[16,640]{1,0:T(8,128)(2,1)S(1)} collective-permute-done((bf16[16,640]{1,0:T(8,128)(2,1)S(1)}, bf16[16,640]{1,0:T(8,128)(2,1)S(1)}, u32[]{:S(2)}, u32[]{:S(2)}) %collective-permute-start.2) | collective-permute-done | bytes 20512 | tf_op jit(solution)/shard_map/ppermute | solution.py:163
  8.4 2.3 %collective-permute-done.1.refs_2_ = bf16[16,640]{1,0:T(8,128)(2,1)S(1)} collective-permute-done((bf16[16,640]{1,0:T(8,128)(2,1)S(1)}, bf16[16,640]{1,0:T(8,128)(2,1)S(1)}, u32[]{:S(2)}, u32[]{:S(2)}) %collective-permute-start.1) | collective-permute-done | bytes 20512 | tf_op jit(solution)/shard_map/ppermute | solution.py:163
  10.7 0.0 collective-permute-done.refs_1_
  10.7 0.7 %collective-permute-start.3 = (bf16[64,640]{1,0:T(8,128)(2,1)S(1)}, bf16[64,640]{1,0:T(8,128)(2,1)S(1)}, u32[]{:S(2)}, u32[]{:S(2)}) collective-permute-start(bf16[64,640]{1,0:T(8,128)(2,1)S(1)} %stack.2.refs_0_), channel_id=1, source_target_pairs={{0,6},{2,4},{4,2},{6,0},{8,14},{10,12},{12,10},{14,8},{16,22},{18,... | collective-permute-start | bytes 245768 | tf_op jit(solution)/shard_map/ppermute | solution.py:163
  11.5 4.0 %collective-permute-done.3.refs_1_ = bf16[64,640]{1,0:T(8,128)(2,1)S(1)} collective-permute-done((bf16[64,640]{1,0:T(8,128)(2,1)S(1)}, bf16[64,640]{1,0:T(8,128)(2,1)S(1)}, u32[]{:S(2)}, u32[]{:S(2)}) %collective-permute-start.3) | collective-permute-done | bytes 81952 | tf_op jit(solution)/shard_map/ppermute | solution.py:163
  15.5 0.2 collective-permute-start.4
  15.7 0.7 %terms.2 = (bf16[128,1024]{1,0:T(8,128)(2,1)S(1)}, f32[128,512]{1,0:T(8,128)S(1)}) custom-call(s32[1]{0:T(128)} %bitcast.3.base_ref, bf16[1024,512]{1,0:T(8,128)(2,1)S(1)} %bitcast.7, bf16[128,640]{1,0:T(8,128)(2,1)S(1)} %stack.3.packed_ref.near_ref), custom_call_target="tpu_custom_call" | custom-call | flops 268435456 | bytes 1048576 | tf_op jit(solution)/shard_map/terms/pallas_call | solution.py:218
  16.4 0.6 %collective-permute-done.4.packed_ref.far_ref = bf16[128,640]{1,0:T(8,128)(2,1)S(1)} collective-permute-done((bf16[128,640]{1,0:T(8,128)(2,1)S(1)}, bf16[128,640]{1,0:T(8,128)(2,1)S(1)}, u32[]{:S(2)}, u32[]{:S(2)}) %collective-permute-start.4) | collective-permute-done | bytes 163872 | tf_op jit(solution)/shard_map/ppermute | solution.py:163
  17.0 0.7 %terms.3 = (bf16[128,1024]{1,0:T(8,128)(2,1)S(1)}, f32[128,512]{1,0:T(8,128)S(1)}) custom-call(s32[1]{0:T(128)} %bitcast.3.base_ref, bf16[1024,512]{1,0:T(8,128)(2,1)S(1)} %bitcast.8, bf16[128,640]{1,0:T(8,128)(2,1)S(1)} %collective-permute-done.4.packed_ref.far_ref), custom_call_target="tpu_custom_call" | custom-call | flops 268435456 | bytes 1048576 | tf_op jit(solution)/shard_map/terms/pallas_call | solution.py:220
  17.7 0.2 collective-permute-start.5
  17.9 1.5 %collective-permute-start.7 = (bf16[512,512]{1,0:T(8,128)(2,1)S(1)}, bf16[512,512]{1,0:T(8,128)(2,1)S(1)}, u32[]{:S(2)}, u32[]{:S(2)}) collective-permute-start(bf16[512,512]{1,0:T(8,128)(2,1)S(1)} %margin_rows.1), channel_id=1, source_target_pairs={{0,1},{1,0},{2,3},{3,2},{4,5},{5,4},{6,7},{7,6},{8,9},{9,8},{10,11... | collective-permute-start | bytes 1572872 | tf_op jit(solution)/shard_map/ppermute | solution.py:197
  19.5 0.0 collective-permute-done.5
  19.5 0.1 fusion
  19.6 1.0 %collective-permute-start.6 = (f16[64,512]{1,0:T(8,128)(2,1)S(1)}, f16[64,512]{1,0:T(8,128)(2,1)S(1)}, u32[]{:S(2)}, u32[]{:S(2)}) collective-permute-start(f16[64,512]{1,0:T(8,128)(2,1)S(1)} %fusion), channel_id=1, source_target_pairs={{0,6},{2,4},{4,2},{6,0},{8,14},{10,12},{12,10},{14,8},{16,22},{18,... | collective-permute-start | bytes 196616 | tf_op jit(solution)/shard_map/ppermute | solution.py:163
  20.6 0.8 %match_grad.1.part_ref = f32[1024,512]{1,0:T(8,128)S(1)} custom-call(s32[1,512]{1,0:T(1,128)S(1)} %bitcast.11, bf16[1024,512]{1,0:T(8,128)(2,1)S(1)} %bitcast.9, bf16[128,1024]{1,0:T(8,128)(2,1)S(1)} %get-tuple-element.18.dl_near, bf16[128,1024]{1,0:T(8,128)(2,1)S(1)} %get-tuple-element.19.dl_far, bf16[128,640]{1,0:T(8,128)(2,1)S(1)} %stack.3.packed_ref.near_ref, ...), custom_call_target="tpu_custom_call" | custom-call | flops 2684354560 | bytes 1048576 | tf_op jit(solution)/shard_map/match_grad/pallas_call | solution.py:221
  21.4 2.4 %collective-permute-done.6 = f16[64,512]{1,0:T(8,128)(2,1)S(1)} collective-permute-done((f16[64,512]{1,0:T(8,128)(2,1)S(1)}, f16[64,512]{1,0:T(8,128)(2,1)S(1)}, u32[]{:S(2)}, u32[]{:S(2)}) %collective-permute-start.6) | collective-permute-done | bytes 65568 | tf_op jit(solution)/shard_map/ppermute | solution.py:163
  23.8 0.1 fusion.3
  23.9 1.7 %collective-permute-start.8 = (f16[16,512]{1,0:T(8,128)(2,1)S(1)}, f16[16,512]{1,0:T(8,128)(2,1)S(1)}, u32[]{:S(2)}, u32[]{:S(2)}) collective-permute-start(f16[16,512]{1,0:T(8,128)(2,1)S(1)} %get-tuple-element.24), channel_id=1, source_target_pairs={{0,24},{2,26},{4,28},{6,30},{8,16},{10,18},{12,20},{14,22},{16,8},... | collective-permute-start | bytes 49160 | tf_op jit(solution)/shard_map/ppermute | solution.py:163
  25.6 0.0 collective-permute-start.10
  25.6 2.5 %collective-permute-start.9 = (f16[16,512]{1,0:T(8,128)(2,1)S(1)}, f16[16,512]{1,0:T(8,128)(2,1)S(1)}, u32[]{:S(2)}, u32[]{:S(2)}) collective-permute-start(f16[16,512]{1,0:T(8,128)(2,1)S(1)} %get-tuple-element.26), channel_id=1, source_target_pairs={{0,18},{2,16},{4,22},{6,20},{8,26},{10,24},{12,30},{14,28},{16,2},... | collective-permute-start | bytes 49160 | tf_op jit(solution)/shard_map/ppermute | solution.py:163
  28.1 1.4 %collective-permute-done.8 = f16[16,512]{1,0:T(8,128)(2,1)S(1)} collective-permute-done((f16[16,512]{1,0:T(8,128)(2,1)S(1)}, f16[16,512]{1,0:T(8,128)(2,1)S(1)}, u32[]{:S(2)}, u32[]{:S(2)}) %collective-permute-start.8) | collective-permute-done | bytes 16416 | tf_op jit(solution)/shard_map/ppermute | solution.py:163
  29.5 0.2 collective-permute-done.9
  29.7 1.3 %collective-permute-start.11 = (f32[16,512]{1,0:T(8,128)S(1)}, f32[16,512]{1,0:T(8,128)S(1)}, u32[]{:S(2)}, u32[]{:S(2)}) collective-permute-start(f32[16,512]{1,0:T(8,128)S(1)} %fusion.7), channel_id=1, source_target_pairs={{0,1},{1,0},{2,3},{3,2},{4,5},{5,4},{6,7},{7,6},{8,9},{9,8},{10,11... | collective-permute-start | bytes 98312 | tf_op jit(solution)/shard_map/ppermute | solution.py:247
  31.0 1.1 %collective-permute-done.7.partner_ref = bf16[512,512]{1,0:T(8,128)(2,1)S(1)} collective-permute-done((bf16[512,512]{1,0:T(8,128)(2,1)S(1)}, bf16[512,512]{1,0:T(8,128)(2,1)S(1)}, u32[]{:S(2)}, u32[]{:S(2)}) %collective-permute-start.7) | collective-permute-done | bytes 524320 | tf_op jit(solution)/shard_map/ppermute | solution.py:197
  32.1 1.6 %voxel_grad.1 = f32[1024,512]{1,0:T(8,128)} custom-call(s32[1,512]{1,0:T(1,128)S(1)} %bitcast.12, f32[1024,512]{1,0:T(8,128)S(1)} %match_grad.1.part_ref, bf16[512,512]{1,0:T(8,128)(2,1)S(1)} %collective-permute-done.7.partner_ref), custom_call_target="tpu_custom_call" | custom-call | flops 536870912 | bytes 4194304 | tf_op jit(solution)/shard_map/voxel_grad/pallas_call | solution.py:250
  33.8 0.6 %add.25 = f32[16,512]{1,0:T(8,128)} add(f32[16,512]{1,0:T(8,128)S(1)} %fusion.7, f32[16,512]{1,0:T(8,128)S(1)} %collective-permute-done.11) | non-fusion elementwise | flops 8192 | bytes 98304 | tf_op jit(solution)/shard_map/add | solution.py:247
  (15 shorter events, 0.1 us)
Async XLA Ops:
  0.6 0.8 %copy-start.2 = (bf16[16,512]{1,0:T(8,128)(2,1)S(1)}, bf16[16,512]{1,0:T(8,128)(2,1)}, u32[]{:S(2)}) copy-start(bf16[16,512]{1,0:T(8,128)(2,1)} %phrases_ref.1) | copy-start | bytes 49156
  1.5 5.5 %copy-start = (bf16[1,1024,512]{2,1,0:T(8,128)(2,1)S(1)}, bf16[1,1024,512]{2,1,0:T(8,128)(2,1)}, u32[]{:S(2)}) copy-start(bf16[1,1024,512]{2,1,0:T(8,128)(2,1)} %param.4) | copy-start | bytes 3145732
  1.5 5.5 %copy-start.1 = (s32[1,1,512]{2,1,0:T(1,128)S(1)}, s32[1,1,512]{2,1,0:T(1,128)}, u32[]{:S(2)}) copy-start(s32[1,1,512]{2,1,0:T(1,128)} %param.7) | copy-start | bytes 6148
  1.5 6.9 %collective-permute-start.2 = (bf16[16,640]{1,0:T(8,128)(2,1)S(1)}, bf16[16,640]{1,0:T(8,128)(2,1)S(1)}, u32[]{:S(2)}, u32[]{:S(2)}) collective-permute-start(bf16[16,640]{1,0:T(8,128)(2,1)S(1)} %own_block.1.refs_0_), channel_id=1, source_target_pairs={{0,24},{2,26},{4,28},{6,30},{8,16},{10,18},{12,20},{14,22},{16,8},... | collective-permute-start | bytes 61448 | tf_op jit(solution)/shard_map/ppermute | solution.py:163
  6.6 4.1 %collective-permute-start.1 = (bf16[16,640]{1,0:T(8,128)(2,1)S(1)}, bf16[16,640]{1,0:T(8,128)(2,1)S(1)}, u32[]{:S(2)}, u32[]{:S(2)}) collective-permute-start(bf16[16,640]{1,0:T(8,128)(2,1)S(1)} %own_block.1.refs_0_), channel_id=1, source_target_pairs={{0,18},{2,16},{4,22},{6,20},{8,26},{10,24},{12,30},{14,28},{16,2},... | collective-permute-start | bytes 61448 | tf_op jit(solution)/shard_map/ppermute | solution.py:163
  6.6 4.1 %collective-permute-start = (bf16[16,640]{1,0:T(8,128)(2,1)S(1)}, bf16[16,640]{1,0:T(8,128)(2,1)S(1)}, u32[]{:S(2)}, u32[]{:S(2)}) collective-permute-start(bf16[16,640]{1,0:T(8,128)(2,1)S(1)} %own_block.1.refs_0_), channel_id=1, source_target_pairs={{0,10},{2,8},{4,14},{6,12},{8,2},{10,0},{12,6},{14,4},{16,26},{18,... | collective-permute-start | bytes 61448 | tf_op jit(solution)/shard_map/ppermute | solution.py:163
  10.7 4.8 %collective-permute-start.3 = (bf16[64,640]{1,0:T(8,128)(2,1)S(1)}, bf16[64,640]{1,0:T(8,128)(2,1)S(1)}, u32[]{:S(2)}, u32[]{:S(2)}) collective-permute-start(bf16[64,640]{1,0:T(8,128)(2,1)S(1)} %stack.2.refs_0_), channel_id=1, source_target_pairs={{0,6},{2,4},{4,2},{6,0},{8,14},{10,12},{12,10},{14,8},{16,22},{18,... | collective-permute-start | bytes 245768 | tf_op jit(solution)/shard_map/ppermute | solution.py:163
  15.5 1.5 %collective-permute-start.4 = (bf16[128,640]{1,0:T(8,128)(2,1)S(1)}, bf16[128,640]{1,0:T(8,128)(2,1)S(1)}, u32[]{:S(2)}, u32[]{:S(2)}) collective-permute-start(bf16[128,640]{1,0:T(8,128)(2,1)S(1)} %stack.3.packed_ref.near_ref), channel_id=1, source_target_pairs={{0,2},{2,0},{4,6},{6,4},{8,10},{10,8},{12,14},{14,12},{16,18},{18,... | collective-permute-start | bytes 491528 | tf_op jit(solution)/shard_map/ppermute | solution.py:163
  17.7 1.7 %collective-permute-start.5 = (f32[128,512]{1,0:T(8,128)S(1)}, f32[128,512]{1,0:T(8,128)S(1)}, u32[]{:S(2)}, u32[]{:S(2)}) collective-permute-start(f32[128,512]{1,0:T(8,128)S(1)} %get-tuple-element.17), channel_id=1, source_target_pairs={{0,2},{2,0},{4,6},{6,4},{8,10},{10,8},{12,14},{14,12},{16,18},{18,... | collective-permute-start | bytes 786440 | tf_op jit(solution)/shard_map/ppermute | solution.py:163
  17.9 14.2 %collective-permute-start.7 = (bf16[512,512]{1,0:T(8,128)(2,1)S(1)}, bf16[512,512]{1,0:T(8,128)(2,1)S(1)}, u32[]{:S(2)}, u32[]{:S(2)}) collective-permute-start(bf16[512,512]{1,0:T(8,128)(2,1)S(1)} %margin_rows.1), channel_id=1, source_target_pairs={{0,1},{1,0},{2,3},{3,2},{4,5},{5,4},{6,7},{7,6},{8,9},{9,8},{10,11... | collective-permute-start | bytes 1572872 | tf_op jit(solution)/shard_map/ppermute | solution.py:197
  19.6 4.2 %collective-permute-start.6 = (f16[64,512]{1,0:T(8,128)(2,1)S(1)}, f16[64,512]{1,0:T(8,128)(2,1)S(1)}, u32[]{:S(2)}, u32[]{:S(2)}) collective-permute-start(f16[64,512]{1,0:T(8,128)(2,1)S(1)} %fusion), channel_id=1, source_target_pairs={{0,6},{2,4},{4,2},{6,0},{8,14},{10,12},{12,10},{14,8},{16,22},{18,... | collective-permute-start | bytes 196616 | tf_op jit(solution)/shard_map/ppermute | solution.py:163
  23.9 5.6 %collective-permute-start.8 = (f16[16,512]{1,0:T(8,128)(2,1)S(1)}, f16[16,512]{1,0:T(8,128)(2,1)S(1)}, u32[]{:S(2)}, u32[]{:S(2)}) collective-permute-start(f16[16,512]{1,0:T(8,128)(2,1)S(1)} %get-tuple-element.24), channel_id=1, source_target_pairs={{0,24},{2,26},{4,28},{6,30},{8,16},{10,18},{12,20},{14,22},{16,8},... | collective-permute-start | bytes 49160 | tf_op jit(solution)/shard_map/ppermute | solution.py:163
  25.6 3.9 %collective-permute-start.10 = (f16[16,512]{1,0:T(8,128)(2,1)S(1)}, f16[16,512]{1,0:T(8,128)(2,1)S(1)}, u32[]{:S(2)}, u32[]{:S(2)}) collective-permute-start(f16[16,512]{1,0:T(8,128)(2,1)S(1)} %get-tuple-element.25), channel_id=1, source_target_pairs={{0,10},{2,8},{4,14},{6,12},{8,2},{10,0},{12,6},{14,4},{16,26},{18,... | collective-permute-start | bytes 49160 | tf_op jit(solution)/shard_map/ppermute | solution.py:163
  25.6 4.1 %collective-permute-start.9 = (f16[16,512]{1,0:T(8,128)(2,1)S(1)}, f16[16,512]{1,0:T(8,128)(2,1)S(1)}, u32[]{:S(2)}, u32[]{:S(2)}) collective-permute-start(f16[16,512]{1,0:T(8,128)(2,1)S(1)} %get-tuple-element.26), channel_id=1, source_target_pairs={{0,18},{2,16},{4,22},{6,20},{8,26},{10,24},{12,30},{14,28},{16,2},... | collective-permute-start | bytes 49160 | tf_op jit(solution)/shard_map/ppermute | solution.py:163
  29.7 4.1 %collective-permute-start.11 = (f32[16,512]{1,0:T(8,128)S(1)}, f32[16,512]{1,0:T(8,128)S(1)}, u32[]{:S(2)}, u32[]{:S(2)}) collective-permute-start(f32[16,512]{1,0:T(8,128)S(1)} %fusion.7), channel_id=1, source_target_pairs={{0,1},{1,0},{2,3},{3,2},{4,5},{5,4},{6,7},{7,6},{8,9},{9,8},{10,11... | collective-permute-start | bytes 98312 | tf_op jit(solution)/shard_map/ppermute | solution.py:247

commit v6 on v5

--- a/solution.py
+++ b/solution.py
@@ -42,13 +42,10 @@
     return root * jnp.abs(root) * (1.0 / gain)
 
 
-def stack_kernel(*refs):
+def stack_kernel(starts, *refs):
     out_ref = refs[-1]
-    start = 0
-    for ref in refs[:-1]:
-        rows = ref.shape[0]
-        out_ref[start : start + rows, :] = ref[...]
-        start += rows
+    for start, ref in zip(starts, refs[:-1], strict=True):
+        out_ref[start : start + ref.shape[0], :] = ref[...]
 
 
 def beside_kernel(phrases_ref, cells_ref, out_ref):
@@ -148,16 +145,19 @@
         cost_estimate=pl.CostEstimate(flops=10**9, bytes_accessed=1024, transcendentals=0),
         name="id_cells",
     )(jnp.pad(jnp.concatenate([pair_ids, pair_ids]), (0, LANES - 2 * owned))[None, :])
-    def stack(*blocks):
-        rows_out = sum(block.shape[0] for block in blocks)
+
+    def stack(blocks, order):
+        starts = [sum(block.shape[0] for block in blocks[:i]) for i in order]
         return pl.pallas_call(
-            stack_kernel,
-            out_shape=jax.ShapeDtypeStruct((rows_out, blocks[0].shape[1]), blocks[0].dtype),
+            functools.partial(stack_kernel, starts),
+            out_shape=jax.ShapeDtypeStruct(
+                (sum(block.shape[0] for block in blocks), blocks[0].shape[1]), blocks[0].dtype
+            ),
             in_specs=[vmem_spec()] * len(blocks),
             out_specs=vmem_spec(),
             compiler_params=params,
             name="stack",
-        )(*blocks)
+        )(*[blocks[i] for i in order])
 
     def over(value, mask):
         return lax.ppermute(value, "batch", [(i, i ^ mask) for i in range(devices)])
@@ -174,10 +174,10 @@
 
     bits = devices.bit_length() - 1
     top, next_top = 1 << (bits - 1), 1 << (bits - 2)
-    masks = [0, next_top | 1, top | 1, top | next_top]
-    part = stack(own_block, *[over(own_block, mask) for mask in masks[1:]])
+    masks = [0, next_top, top | 1, top | next_top | 1]
+    part = stack([own_block] + [over(own_block, mask) for mask in masks[1:]], (0, 3, 1, 2))
     for bit in reversed(range(2, bits - 2)):
-        part = stack(part, over(part, 1 << bit | 1))
+        part = stack([part, over(part, 1 << bit | 1)], (0, 1))
         masks = masks + [mask ^ (1 << bit | 1) for mask in masks]
 
     picked = margin_index[0]
@@ -195,7 +195,7 @@
 
     part, chosen = lax.optimization_barrier((part, chosen))
     partner = lax.ppermute(chosen, "crop", swap)
-    near = stack(part, over(part, 3))
+    near = stack([part, over(part, 3)], (0, 1))
     far = over(near, 1)
 
     base = (lax.axis_index("batch") * rows).astype(jnp.int32).reshape(1)
@@ -241,10 +241,11 @@
         sums = sums[:count] + from_half(back, bound)
         bound = 2 * bound
     own = sums[:owned]
-    for i in (3, 2, 1):
+    for i in (1, 2, 3):
         block = to_half(sums[i * owned : (i + 1) * owned], bound)
         own = own + from_half(over(block, masks[i]), bound)
-    phrase_grad = own + lax.ppermute(own, "crop", swap)
+    bound = 4 * bound
+    phrase_grad = own + from_half(lax.ppermute(to_half(own, bound), "crop", swap), bound)
     partner, _ = lax.optimization_barrier((partner, own))
     block = math.gcd(rows, 256)
     voxel_grad = pl.pallas_call(

time: 34.6 us -> 34 us (0.983)
  waiting for transfers between devices: 12.7 us -> 10.8 us
  starting transfers between devices: 14.7 us -> 16 us
    ppermute x10, waiting for transfers between devices: 11.6 us -> 10.2 us  [over(): return lax.ppermute(value, 'batch', [(i, i ^ mask) for i in range(devices)])]
    ppermute x10, starting transfers between devices: 11.8 us -> 12.9 us  [over(): return lax.ppermute(value, 'batch', [(i, i ^ mask) for i in range(devices)])]
    ppermute x1, waiting for transfers between devices: 1.08 us -> 0.1 us  [local(): partner = lax.ppermute(chosen, 'crop', swap)]
    ppermute x1, waiting for transfers between devices: 0.01 us -> 0.47 us  [local(): lax.ppermute(to_half(own, bound), 'crop', swap)]
  transfers between devices with their start and end apart: 12 -> 12, of which waited for: 8 -> 11; matrix products, arithmetic and copies ran while one was open for 1% -> 1% of each run, Pallas kernels for 11% -> 12%
where the time goes in v6:
time: 34 us; the launch traced here: 33.8 us
  starting transfers between devices  16 us (47%)
  waiting for transfers between devices  10.8 us (32%)
  Pallas kernels  4.68 us (14%)
  other arithmetic  1.65 us (5%)
  between operations  0.75 us (2%)
    ppermute x10, starting transfers between devices, over(): return lax.ppermute(value, 'batch', [(i, i ^ mask) for i in range(devices)])  12.9 us
    ppermute x10, waiting for transfers between devices, over(): return lax.ppermute(value, 'batch', [(i, i ^ mask) for i in range(devices)])  10.2 us
    pallas_call x1, Pallas kernels, local(): pl.pallas_call(functools.partial(grad_kernel, block), out_shape=jax.Shape...  1.65 us
    ppermute x1, starting transfers between devices, local(): lax.ppermute(to_half(own, bound), 'crop', swap)  1.57 us
    ppermute x1, starting transfers between devices, local(): partner = lax.ppermute(chosen, 'crop', swap)  1.52 us
    pallas_call x1, Pallas kernels, local(): pl.pallas_call(functools.partial(match_kernel, scale), out_shape=jax.Shap...  0.81 us
    concatenate x1, other arithmetic, local(): jnp.concatenate([pair_ids, pair_ids])  0.81 us
    pallas_call x1, Pallas kernels, local(): pl.pallas_call(margin_kernel, out_shape=jax.ShapeDtypeStruct((picks, widt...  0.74 us
  transfers between devices with their start and end apart: 12, of which 11 were waited for; matrix products, arithmetic and copies ran while one was open for 1% of the time, Pallas kernels for 12%

profile of v6, /device:TPU:0, one launch (start us, length us, event | category | flops | bytes accessed | tf_op | source)
XLA Modules:
  0.0 33.8 jit_solution(16867974430662613813)
XLA Ops:
  0.6 0.8 %pad_add_fusion = s32[32]{0:T(128)S(1)} fusion(s32[16]{0:T(128)} %param.6), kind=kLoop, calls=%fused_computation.25 | loop fusion | flops 32 | bytes 192 | tf_op jit(solution)/shard_map/concatenate | solution.py:147
  1.5 0.0 copy-start.1
  1.5 4.6 %collective-permute-start = (bf16[16,640]{1,0:T(8,128)(2,1)S(1)}, bf16[16,640]{1,0:T(8,128)(2,1)S(1)}, u32[]{:S(2)}, u32[]{:S(2)}) collective-permute-start(bf16[16,640]{1,0:T(8,128)(2,1)S(1)} %own_block.1.refs_0_), channel_id=1, source_target_pairs={{0,26},{2,24},{4,30},{6,28},{8,18},{10,16},{12,22},{14,20},{16,10}... | collective-permute-start | bytes 61448 | tf_op jit(solution)/shard_map/ppermute | solution.py:163
  6.1 0.4 %collective-permute-start.2 = (bf16[16,640]{1,0:T(8,128)(2,1)S(1)}, bf16[16,640]{1,0:T(8,128)(2,1)S(1)}, u32[]{:S(2)}, u32[]{:S(2)}) collective-permute-start(bf16[16,640]{1,0:T(8,128)(2,1)S(1)} %own_block.1.refs_0_), channel_id=1, source_target_pairs={{0,18},{2,16},{4,22},{6,20},{8,26},{10,24},{12,30},{14,28},{16,2},... | collective-permute-start | bytes 61448 | tf_op jit(solution)/shard_map/ppermute | solution.py:163
  6.4 0.7 %margin_rows.1 = bf16[512,512]{1,0:T(8,128)(2,1)S(1)} custom-call(bf16[1024,512]{1,0:T(8,128)(2,1)S(1)} %bitcast.6, s32[1,512]{1,0:T(1,128)S(1)} %bitcast.10), custom_call_target="tpu_custom_call" | custom-call | flops 536870912 | bytes 1048576 | tf_op jit(solution)/shard_map/margin_rows/pallas_call | solution.py:184
  7.2 0.5 %collective-permute-done.refs_1_ = bf16[16,640]{1,0:T(8,128)(2,1)S(1)} collective-permute-done((bf16[16,640]{1,0:T(8,128)(2,1)S(1)}, bf16[16,640]{1,0:T(8,128)(2,1)S(1)}, u32[]{:S(2)}, u32[]{:S(2)}) %collective-permute-start) | collective-permute-done | bytes 20512 | tf_op jit(solution)/shard_map/ppermute | solution.py:163
  7.6 2.2 %collective-permute-done.1.refs_2_ = bf16[16,640]{1,0:T(8,128)(2,1)S(1)} collective-permute-done((bf16[16,640]{1,0:T(8,128)(2,1)S(1)}, bf16[16,640]{1,0:T(8,128)(2,1)S(1)}, u32[]{:S(2)}, u32[]{:S(2)}) %collective-permute-start.1) | collective-permute-done | bytes 20512 | tf_op jit(solution)/shard_map/ppermute | solution.py:163
  9.8 0.3 collective-permute-done.2.refs_3_
  10.2 1.8 %collective-permute-start.3 = (bf16[64,640]{1,0:T(8,128)(2,1)S(1)}, bf16[64,640]{1,0:T(8,128)(2,1)S(1)}, u32[]{:S(2)}, u32[]{:S(2)}) collective-permute-start(bf16[64,640]{1,0:T(8,128)(2,1)S(1)} %stack.2.refs_0_), channel_id=1, source_target_pairs={{0,6},{2,4},{4,2},{6,0},{8,14},{10,12},{12,10},{14,8},{16,22},{18,... | collective-permute-start | bytes 245768 | tf_op jit(solution)/shard_map/ppermute | solution.py:163
  12.0 2.2 %collective-permute-done.3.refs_1_ = bf16[64,640]{1,0:T(8,128)(2,1)S(1)} collective-permute-done((bf16[64,640]{1,0:T(8,128)(2,1)S(1)}, bf16[64,640]{1,0:T(8,128)(2,1)S(1)}, u32[]{:S(2)}, u32[]{:S(2)}) %collective-permute-start.3) | collective-permute-done | bytes 81952 | tf_op jit(solution)/shard_map/ppermute | solution.py:163
  14.2 0.7 %collective-permute-start.4 = (bf16[128,640]{1,0:T(8,128)(2,1)S(1)}, bf16[128,640]{1,0:T(8,128)(2,1)S(1)}, u32[]{:S(2)}, u32[]{:S(2)}) collective-permute-start(bf16[128,640]{1,0:T(8,128)(2,1)S(1)} %stack.3.packed_ref.near_ref), channel_id=1, source_target_pairs={{0,2},{2,0},{4,6},{6,4},{8,10},{10,8},{12,14},{14,12},{16,18},{18,... | collective-permute-start | bytes 491528 | tf_op jit(solution)/shard_map/ppermute | solution.py:163
  14.9 0.7 %terms.2 = (bf16[128,1024]{1,0:T(8,128)(2,1)S(1)}, f32[128,512]{1,0:T(8,128)S(1)}) custom-call(s32[1]{0:T(128)} %bitcast.3.base_ref, bf16[1024,512]{1,0:T(8,128)(2,1)S(1)} %bitcast.7, bf16[128,640]{1,0:T(8,128)(2,1)S(1)} %stack.3.packed_ref.near_ref), custom_call_target="tpu_custom_call" | custom-call | flops 268435456 | bytes 1048576 | tf_op jit(solution)/shard_map/terms/pallas_call | solution.py:218
  15.7 0.3 collective-permute-done.4.packed_ref.far_ref
  16.0 0.7 %terms.3 = (bf16[128,1024]{1,0:T(8,128)(2,1)S(1)}, f32[128,512]{1,0:T(8,128)S(1)}) custom-call(s32[1]{0:T(128)} %bitcast.3.base_ref, bf16[1024,512]{1,0:T(8,128)(2,1)S(1)} %bitcast.8, bf16[128,640]{1,0:T(8,128)(2,1)S(1)} %collective-permute-done.4.packed_ref.far_ref), custom_call_target="tpu_custom_call" | custom-call | flops 268435456 | bytes 1048576 | tf_op jit(solution)/shard_map/terms/pallas_call | solution.py:220
  16.7 0.4 %collective-permute-start.5 = (f32[128,512]{1,0:T(8,128)S(1)}, f32[128,512]{1,0:T(8,128)S(1)}, u32[]{:S(2)}, u32[]{:S(2)}) collective-permute-start(f32[128,512]{1,0:T(8,128)S(1)} %get-tuple-element.17), channel_id=1, source_target_pairs={{0,2},{2,0},{4,6},{6,4},{8,10},{10,8},{12,14},{14,12},{16,18},{18,... | collective-permute-start | bytes 786440 | tf_op jit(solution)/shard_map/ppermute | solution.py:163
  17.1 1.5 %collective-permute-start.7 = (bf16[512,512]{1,0:T(8,128)(2,1)S(1)}, bf16[512,512]{1,0:T(8,128)(2,1)S(1)}, u32[]{:S(2)}, u32[]{:S(2)}) collective-permute-start(bf16[512,512]{1,0:T(8,128)(2,1)S(1)} %margin_rows.1), channel_id=1, source_target_pairs={{0,1},{1,0},{2,3},{3,2},{4,5},{5,4},{6,7},{7,6},{8,9},{9,8},{10,11... | collective-permute-start | bytes 1572872 | tf_op jit(solution)/shard_map/ppermute | solution.py:197
  18.7 0.1 fusion
  18.8 1.1 %collective-permute-start.6 = (f16[64,512]{1,0:T(8,128)(2,1)S(1)}, f16[64,512]{1,0:T(8,128)(2,1)S(1)}, u32[]{:S(2)}, u32[]{:S(2)}) collective-permute-start(f16[64,512]{1,0:T(8,128)(2,1)S(1)} %fusion), channel_id=1, source_target_pairs={{0,6},{2,4},{4,2},{6,0},{8,14},{10,12},{12,10},{14,8},{16,22},{18,... | collective-permute-start | bytes 196616 | tf_op jit(solution)/shard_map/ppermute | solution.py:163
  19.9 0.8 %match_grad.1.part_ref = f32[1024,512]{1,0:T(8,128)S(1)} custom-call(s32[1,512]{1,0:T(1,128)S(1)} %bitcast.11, bf16[1024,512]{1,0:T(8,128)(2,1)S(1)} %bitcast.9, bf16[128,1024]{1,0:T(8,128)(2,1)S(1)} %get-tuple-element.18.dl_near, bf16[128,1024]{1,0:T(8,128)(2,1)S(1)} %get-tuple-element.19.dl_far, bf16[128,640]{1,0:T(8,128)(2,1)S(1)} %stack.3.packed_ref.near_ref, ...), custom_call_target="tpu_custom_call" | custom-call | flops 2684354560 | bytes 1048576 | tf_op jit(solution)/shard_map/match_grad/pallas_call | solution.py:221
  20.7 2.3 %collective-permute-done.6 = f16[64,512]{1,0:T(8,128)(2,1)S(1)} collective-permute-done((f16[64,512]{1,0:T(8,128)(2,1)S(1)}, f16[64,512]{1,0:T(8,128)(2,1)S(1)}, u32[]{:S(2)}, u32[]{:S(2)}) %collective-permute-start.6) | collective-permute-done | bytes 65568 | tf_op jit(solution)/shard_map/ppermute | solution.py:163
  23.0 0.1 fusion.3
  23.1 2.0 %collective-permute-start.10 = (f16[16,512]{1,0:T(8,128)(2,1)S(1)}, f16[16,512]{1,0:T(8,128)(2,1)S(1)}, u32[]{:S(2)}, u32[]{:S(2)}) collective-permute-start(f16[16,512]{1,0:T(8,128)(2,1)S(1)} %get-tuple-element.27), channel_id=1, source_target_pairs={{0,26},{2,24},{4,30},{6,28},{8,18},{10,16},{12,22},{14,20},{16,10}... | collective-permute-start | bytes 49160 | tf_op jit(solution)/shard_map/ppermute | solution.py:163
  25.1 0.2 collective-permute-start.8
  25.3 1.7 %collective-permute-start.9 = (f16[16,512]{1,0:T(8,128)(2,1)S(1)}, f16[16,512]{1,0:T(8,128)(2,1)S(1)}, u32[]{:S(2)}, u32[]{:S(2)}) collective-permute-start(f16[16,512]{1,0:T(8,128)(2,1)S(1)} %get-tuple-element.28), channel_id=1, source_target_pairs={{0,18},{2,16},{4,22},{6,20},{8,26},{10,24},{12,30},{14,28},{16,2},... | collective-permute-start | bytes 49160 | tf_op jit(solution)/shard_map/ppermute | solution.py:163
  27.0 1.2 %collective-permute-done.10 = f16[16,512]{1,0:T(8,128)(2,1)S(1)} collective-permute-done((f16[16,512]{1,0:T(8,128)(2,1)S(1)}, f16[16,512]{1,0:T(8,128)(2,1)S(1)}, u32[]{:S(2)}, u32[]{:S(2)}) %collective-permute-start.10) | collective-permute-done | bytes 16416 | tf_op jit(solution)/shard_map/ppermute | solution.py:163
  28.2 0.6 %collective-permute-done.8 = f16[16,512]{1,0:T(8,128)(2,1)S(1)} collective-permute-done((f16[16,512]{1,0:T(8,128)(2,1)S(1)}, f16[16,512]{1,0:T(8,128)(2,1)S(1)}, u32[]{:S(2)}, u32[]{:S(2)}) %collective-permute-start.8) | collective-permute-done | bytes 16416 | tf_op jit(solution)/shard_map/ppermute | solution.py:163
  28.8 0.6 %collective-permute-done.9 = f16[16,512]{1,0:T(8,128)(2,1)S(1)} collective-permute-done((f16[16,512]{1,0:T(8,128)(2,1)S(1)}, f16[16,512]{1,0:T(8,128)(2,1)S(1)}, u32[]{:S(2)}, u32[]{:S(2)}) %collective-permute-start.9) | collective-permute-done | bytes 16416 | tf_op jit(solution)/shard_map/ppermute | solution.py:163
  29.4 1.6 %collective-permute-start.11 = (f16[16,512]{1,0:T(8,128)(2,1)S(1)}, f16[16,512]{1,0:T(8,128)(2,1)S(1)}, u32[]{:S(2)}, u32[]{:S(2)}) collective-permute-start(f16[16,512]{1,0:T(8,128)(2,1)S(1)} %get-tuple-element.24), channel_id=1, source_target_pairs={{0,1},{1,0},{2,3},{3,2},{4,5},{5,4},{6,7},{7,6},{8,9},{9,8},{10,11... | collective-permute-start | bytes 49160 | tf_op jit(solution)/shard_map/ppermute | solution.py:248
  31.0 0.1 collective-permute-done.7.partner_ref
  31.1 1.6 %voxel_grad.1 = f32[1024,512]{1,0:T(8,128)} custom-call(s32[1,512]{1,0:T(1,128)S(1)} %bitcast.12, f32[1024,512]{1,0:T(8,128)S(1)} %match_grad.1.part_ref, bf16[512,512]{1,0:T(8,128)(2,1)S(1)} %collective-permute-done.7.partner_ref), custom_call_target="tpu_custom_call" | custom-call | flops 536870912 | bytes 4194304 | tf_op jit(solution)/shard_map/voxel_grad/pallas_call | solution.py:251
  32.7 0.5 %collective-permute-done.11 = f16[16,512]{1,0:T(8,128)(2,1)S(1)} collective-permute-done((f16[16,512]{1,0:T(8,128)(2,1)S(1)}, f16[16,512]{1,0:T(8,128)(2,1)S(1)}, u32[]{:S(2)}, u32[]{:S(2)}) %collective-permute-start.11) | collective-permute-done | bytes 16416 | tf_op jit(solution)/shard_map/ppermute | solution.py:248
  33.2 0.6 %fusion.14 = f32[16,512]{1,0:T(8,128)} fusion(f32[16,512]{1,0:T(8,128)S(1)} %get-tuple-element.25, f16[16,512]{1,0:T(8,128)(2,1)S(1)} %collective-permute-done.11), kind=kLoop, calls=%fused_computation.24 | loop fusion | flops 40960 | bytes 81920 | tf_op jit(solution)/shard_map/add | solution.py:248
  (15 shorter events, 0.2 us)
Async XLA Ops:
  0.6 0.8 %copy-start.2 = (bf16[16,512]{1,0:T(8,128)(2,1)S(1)}, bf16[16,512]{1,0:T(8,128)(2,1)}, u32[]{:S(2)}) copy-start(bf16[16,512]{1,0:T(8,128)(2,1)} %phrases_ref.1) | copy-start | bytes 49156
  1.5 5.0 %copy-start = (bf16[1,1024,512]{2,1,0:T(8,128)(2,1)S(1)}, bf16[1,1024,512]{2,1,0:T(8,128)(2,1)}, u32[]{:S(2)}) copy-start(bf16[1,1024,512]{2,1,0:T(8,128)(2,1)} %param.4) | copy-start | bytes 3145732
  1.5 4.9 %copy-start.1 = (s32[1,1,512]{2,1,0:T(1,128)S(1)}, s32[1,1,512]{2,1,0:T(1,128)}, u32[]{:S(2)}) copy-start(s32[1,1,512]{2,1,0:T(1,128)} %param.7) | copy-start | bytes 6148
  1.5 6.1 %collective-permute-start = (bf16[16,640]{1,0:T(8,128)(2,1)S(1)}, bf16[16,640]{1,0:T(8,128)(2,1)S(1)}, u32[]{:S(2)}, u32[]{:S(2)}) collective-permute-start(bf16[16,640]{1,0:T(8,128)(2,1)S(1)} %own_block.1.refs_0_), channel_id=1, source_target_pairs={{0,26},{2,24},{4,30},{6,28},{8,18},{10,16},{12,22},{14,20},{16,10}... | collective-permute-start | bytes 61448 | tf_op jit(solution)/shard_map/ppermute | solution.py:163
  6.1 3.8 %collective-permute-start.1 = (bf16[16,640]{1,0:T(8,128)(2,1)S(1)}, bf16[16,640]{1,0:T(8,128)(2,1)S(1)}, u32[]{:S(2)}, u32[]{:S(2)}) collective-permute-start(bf16[16,640]{1,0:T(8,128)(2,1)S(1)} %own_block.1.refs_0_), channel_id=1, source_target_pairs={{0,8},{2,10},{4,12},{6,14},{8,0},{10,2},{12,4},{14,6},{16,24},{18,... | collective-permute-start | bytes 61448 | tf_op jit(solution)/shard_map/ppermute | solution.py:163
  6.1 4.1 %collective-permute-start.2 = (bf16[16,640]{1,0:T(8,128)(2,1)S(1)}, bf16[16,640]{1,0:T(8,128)(2,1)S(1)}, u32[]{:S(2)}, u32[]{:S(2)}) collective-permute-start(bf16[16,640]{1,0:T(8,128)(2,1)S(1)} %own_block.1.refs_0_), channel_id=1, source_target_pairs={{0,18},{2,16},{4,22},{6,20},{8,26},{10,24},{12,30},{14,28},{16,2},... | collective-permute-start | bytes 61448 | tf_op jit(solution)/shard_map/ppermute | solution.py:163
  10.2 4.0 %collective-permute-start.3 = (bf16[64,640]{1,0:T(8,128)(2,1)S(1)}, bf16[64,640]{1,0:T(8,128)(2,1)S(1)}, u32[]{:S(2)}, u32[]{:S(2)}) collective-permute-start(bf16[64,640]{1,0:T(8,128)(2,1)S(1)} %stack.2.refs_0_), channel_id=1, source_target_pairs={{0,6},{2,4},{4,2},{6,0},{8,14},{10,12},{12,10},{14,8},{16,22},{18,... | collective-permute-start | bytes 245768 | tf_op jit(solution)/shard_map/ppermute | solution.py:163
  14.2 1.7 %collective-permute-start.4 = (bf16[128,640]{1,0:T(8,128)(2,1)S(1)}, bf16[128,640]{1,0:T(8,128)(2,1)S(1)}, u32[]{:S(2)}, u32[]{:S(2)}) collective-permute-start(bf16[128,640]{1,0:T(8,128)(2,1)S(1)} %stack.3.packed_ref.near_ref), channel_id=1, source_target_pairs={{0,2},{2,0},{4,6},{6,4},{8,10},{10,8},{12,14},{14,12},{16,18},{18,... | collective-permute-start | bytes 491528 | tf_op jit(solution)/shard_map/ppermute | solution.py:163
  16.7 2.0 %collective-permute-start.5 = (f32[128,512]{1,0:T(8,128)S(1)}, f32[128,512]{1,0:T(8,128)S(1)}, u32[]{:S(2)}, u32[]{:S(2)}) collective-permute-start(f32[128,512]{1,0:T(8,128)S(1)} %get-tuple-element.17), channel_id=1, source_target_pairs={{0,2},{2,0},{4,6},{6,4},{8,10},{10,8},{12,14},{14,12},{16,18},{18,... | collective-permute-start | bytes 786440 | tf_op jit(solution)/shard_map/ppermute | solution.py:163
  17.1 14.0 %collective-permute-start.7 = (bf16[512,512]{1,0:T(8,128)(2,1)S(1)}, bf16[512,512]{1,0:T(8,128)(2,1)S(1)}, u32[]{:S(2)}, u32[]{:S(2)}) collective-permute-start(bf16[512,512]{1,0:T(8,128)(2,1)S(1)} %margin_rows.1), channel_id=1, source_target_pairs={{0,1},{1,0},{2,3},{3,2},{4,5},{5,4},{6,7},{7,6},{8,9},{9,8},{10,11... | collective-permute-start | bytes 1572872 | tf_op jit(solution)/shard_map/ppermute | solution.py:197
  18.8 4.3 %collective-permute-start.6 = (f16[64,512]{1,0:T(8,128)(2,1)S(1)}, f16[64,512]{1,0:T(8,128)(2,1)S(1)}, u32[]{:S(2)}, u32[]{:S(2)}) collective-permute-start(f16[64,512]{1,0:T(8,128)(2,1)S(1)} %fusion), channel_id=1, source_target_pairs={{0,6},{2,4},{4,2},{6,0},{8,14},{10,12},{12,10},{14,8},{16,22},{18,... | collective-permute-start | bytes 196616 | tf_op jit(solution)/shard_map/ppermute | solution.py:163
  23.1 5.1 %collective-permute-start.10 = (f16[16,512]{1,0:T(8,128)(2,1)S(1)}, f16[16,512]{1,0:T(8,128)(2,1)S(1)}, u32[]{:S(2)}, u32[]{:S(2)}) collective-permute-start(f16[16,512]{1,0:T(8,128)(2,1)S(1)} %get-tuple-element.27), channel_id=1, source_target_pairs={{0,26},{2,24},{4,30},{6,28},{8,18},{10,16},{12,22},{14,20},{16,10}... | collective-permute-start | bytes 49160 | tf_op jit(solution)/shard_map/ppermute | solution.py:163
  25.1 3.7 %collective-permute-start.8 = (f16[16,512]{1,0:T(8,128)(2,1)S(1)}, f16[16,512]{1,0:T(8,128)(2,1)S(1)}, u32[]{:S(2)}, u32[]{:S(2)}) collective-permute-start(f16[16,512]{1,0:T(8,128)(2,1)S(1)} %get-tuple-element.26), channel_id=1, source_target_pairs={{0,8},{2,10},{4,12},{6,14},{8,0},{10,2},{12,4},{14,6},{16,24},{18,... | collective-permute-start | bytes 49160 | tf_op jit(solution)/shard_map/ppermute | solution.py:163
  25.3 4.1 %collective-permute-start.9 = (f16[16,512]{1,0:T(8,128)(2,1)S(1)}, f16[16,512]{1,0:T(8,128)(2,1)S(1)}, u32[]{:S(2)}, u32[]{:S(2)}) collective-permute-start(f16[16,512]{1,0:T(8,128)(2,1)S(1)} %get-tuple-element.28), channel_id=1, source_target_pairs={{0,18},{2,16},{4,22},{6,20},{8,26},{10,24},{12,30},{14,28},{16,2},... | collective-permute-start | bytes 49160 | tf_op jit(solution)/shard_map/ppermute | solution.py:163
  29.4 3.8 %collective-permute-start.11 = (f16[16,512]{1,0:T(8,128)(2,1)S(1)}, f16[16,512]{1,0:T(8,128)(2,1)S(1)}, u32[]{:S(2)}, u32[]{:S(2)}) collective-permute-start(f16[16,512]{1,0:T(8,128)(2,1)S(1)} %get-tuple-element.24), channel_id=1, source_target_pairs={{0,1},{1,0},{2,3},{3,2},{4,5},{5,4},{6,7},{7,6},{8,9},{9,8},{10,11... | collective-permute-start | bytes 49160 | tf_op jit(solution)/shard_map/ppermute | solution.py:248

commit v7 on v6

--- a/solution.py
+++ b/solution.py
@@ -175,7 +175,7 @@
     bits = devices.bit_length() - 1
     top, next_top = 1 << (bits - 1), 1 << (bits - 2)
     masks = [0, next_top, top | 1, top | next_top | 1]
-    part = stack([own_block] + [over(own_block, mask) for mask in masks[1:]], (0, 3, 1, 2))
+    part = stack([own_block] + [over(own_block, mask) for mask in masks[1:]], (0, 1, 3, 2))
     for bit in reversed(range(2, bits - 2)):
         part = stack([part, over(part, 1 << bit | 1)], (0, 1))
         masks = masks + [mask ^ (1 << bit | 1) for mask in masks]
@@ -209,7 +209,7 @@
         out_specs=[vmem_spec()] * 2,
         compiler_params=params,
         cost_estimate=pl.CostEstimate(
-            flops=4 * half * rows * width,
+            flops=40 * half * rows * width,
             bytes_accessed=2 * rows * width,
             transcendentals=half * rows,
         ),
@@ -231,21 +231,24 @@
     )(picked, own_vox, dl_near, dl_far, near, far)
 
     bound = VOX_MAX * rows * scale
-    sums = near_terms + over(far_terms, 1)
-    bound = 2 * bound
-    for bit in range(1, bits - 2):
+    count = near_terms.shape[0] // 2
+    from_core = over(far_terms[:count], 1)
+    across = over(to_half(near_terms[count:], bound), 3)
+    along = over(to_half(far_terms[count:], bound), 2)
+    along, matched = lax.optimization_barrier((along, matched))
+    sums = near_terms[:count] + from_core + from_half(across, bound) + from_half(along, bound)
+    bound = 4 * bound
+    for bit in range(2, bits - 2):
         count = sums.shape[0] // 2
         back = over(to_half(sums[count:], bound), 1 << bit | 1)
-        if bit == 1:
-            back, matched = lax.optimization_barrier((back, matched))
         sums = sums[:count] + from_half(back, bound)
         bound = 2 * bound
     own = sums[:owned]
-    for i in (1, 2, 3):
+    for i in (3, 2, 1):
         block = to_half(sums[i * owned : (i + 1) * owned], bound)
         own = own + from_half(over(block, masks[i]), bound)
     bound = 4 * bound
-    phrase_grad = own + from_half(lax.ppermute(to_half(own, bound), "crop", swap), bound)
+    other = lax.ppermute(to_half(own, bound), "crop", swap)
     partner, _ = lax.optimization_barrier((partner, own))
     block = math.gcd(rows, 256)
     voxel_grad = pl.pallas_call(
@@ -260,6 +263,8 @@
         ),
         name="voxel_grad",
     )(picked, matched, partner)
+    other, voxel_grad = lax.optimization_barrier((other, voxel_grad))
+    phrase_grad = own + from_half(other, bound)
     return (voxel_grad[None], phrase_grad)
 
 

time: 34 us -> 33.5 us (0.985)
  waiting for transfers between devices: 10.8 us -> 10.2 us
    ppermute x10 -> x11, waiting for transfers between devices: 10.2 us -> 9.63 us  [over(): return lax.ppermute(value, 'batch', [(i, i ^ mask) for i in range(devices)])]
    ppermute x10 -> x11, starting transfers between devices: 12.9 us -> 12.8 us  [over(): return lax.ppermute(value, 'batch', [(i, i ^ mask) for i in range(devices)])]
    add x3 -> x2, other arithmetic: 0.68 us -> 0.68 us  [the longest x1 0.62 us: local(): phrase_grad = own + from_half(other, bound)]
  transfers between devices with their start and end apart: 12 -> 13, of which waited for: 11 -> 8; matrix products, arithmetic and copies ran while one was open for 1% -> 1% of each run, Pallas kernels for 12% -> 14%
where the time goes in v7:
time: 33.5 us; the launch traced here: 33.3 us
  starting transfers between devices  15.8 us (47%)
  waiting for transfers between devices  10.2 us (30%)
  Pallas kernels  4.74 us (14%)
  other arithmetic  1.71 us (5%)
  between operations  0.76 us (2%)
    ppermute x11, starting transfers between devices, over(): return lax.ppermute(value, 'batch', [(i, i ^ mask) for i in range(devices)])  12.8 us
    ppermute x11, waiting for transfers between devices, over(): return lax.ppermute(value, 'batch', [(i, i ^ mask) for i in range(devices)])  9.63 us
    pallas_call x1, Pallas kernels, local(): pl.pallas_call(functools.partial(grad_kernel, block), out_shape=jax.Shape...  1.65 us
    ppermute x1, starting transfers between devices, local(): other = lax.ppermute(to_half(own, bound), 'crop', swap)  1.58 us
    ppermute x1, starting transfers between devices, local(): partner = lax.ppermute(chosen, 'crop', swap)  1.52 us
    pallas_call x1, Pallas kernels, local(): pl.pallas_call(functools.partial(match_kernel, scale), out_shape=jax.Shap...  0.82 us
    concatenate x1, other arithmetic, local(): jnp.concatenate([pair_ids, pair_ids])  0.81 us
    pallas_call x1, Pallas kernels, local(): dl_far, far_terms = terms(base, own_vox, far)  0.75 us
  transfers between devices with their start and end apart: 13, of which 8 were waited for; matrix products, arithmetic and copies ran while one was open for 1% of the time, Pallas kernels for 14%

profile of v7, /device:TPU:0, one launch (start us, length us, event | category | flops | bytes accessed | tf_op | source)
XLA Modules:
  0.0 33.3 jit_solution(13304475875633289630)
XLA Ops:
  0.6 0.8 %pad_add_fusion = s32[32]{0:T(128)S(1)} fusion(s32[16]{0:T(128)} %param.6), kind=kLoop, calls=%fused_computation.30 | loop fusion | flops 32 | bytes 192 | tf_op jit(solution)/shard_map/concatenate | solution.py:147
  1.5 0.0 copy-start
  1.5 0.0 copy-start.1
  1.5 3.5 %collective-permute-start.2 = (bf16[16,640]{1,0:T(8,128)(2,1)S(1)}, bf16[16,640]{1,0:T(8,128)(2,1)S(1)}, u32[]{:S(2)}, u32[]{:S(2)}) collective-permute-start(bf16[16,640]{1,0:T(8,128)(2,1)S(1)} %own_block.1.refs_0_), channel_id=1, source_target_pairs={{0,18},{2,16},{4,22},{6,20},{8,26},{10,24},{12,30},{14,28},{16,2},... | collective-permute-start | bytes 61448 | tf_op jit(solution)/shard_map/ppermute | solution.py:163
  5.0 1.6 %collective-permute-start.1 = (bf16[16,640]{1,0:T(8,128)(2,1)S(1)}, bf16[16,640]{1,0:T(8,128)(2,1)S(1)}, u32[]{:S(2)}, u32[]{:S(2)}) collective-permute-start(bf16[16,640]{1,0:T(8,128)(2,1)S(1)} %own_block.1.refs_0_), channel_id=1, source_target_pairs={{0,26},{2,24},{4,30},{6,28},{8,18},{10,16},{12,22},{14,20},{16,10}... | collective-permute-start | bytes 61448 | tf_op jit(solution)/shard_map/ppermute | solution.py:163
  6.7 0.7 %margin_rows.1 = bf16[512,512]{1,0:T(8,128)(2,1)S(1)} custom-call(bf16[1024,512]{1,0:T(8,128)(2,1)S(1)} %bitcast.9, s32[1,512]{1,0:T(1,128)S(1)} %bitcast.6), custom_call_target="tpu_custom_call" | custom-call | flops 536870912 | bytes 1048576 | tf_op jit(solution)/shard_map/margin_rows/pallas_call | solution.py:184
  7.4 2.6 %collective-permute-done.1.refs_2_ = bf16[16,640]{1,0:T(8,128)(2,1)S(1)} collective-permute-done((bf16[16,640]{1,0:T(8,128)(2,1)S(1)}, bf16[16,640]{1,0:T(8,128)(2,1)S(1)}, u32[]{:S(2)}, u32[]{:S(2)}) %collective-permute-start.1) | collective-permute-done | bytes 20512 | tf_op jit(solution)/shard_map/ppermute | solution.py:163
  10.1 0.4 %collective-permute-done.refs_1_ = bf16[16,640]{1,0:T(8,128)(2,1)S(1)} collective-permute-done((bf16[16,640]{1,0:T(8,128)(2,1)S(1)}, bf16[16,640]{1,0:T(8,128)(2,1)S(1)}, u32[]{:S(2)}, u32[]{:S(2)}) %collective-permute-start) | collective-permute-done | bytes 20512 | tf_op jit(solution)/shard_map/ppermute | solution.py:163
  10.5 1.4 %collective-permute-start.3 = (bf16[64,640]{1,0:T(8,128)(2,1)S(1)}, bf16[64,640]{1,0:T(8,128)(2,1)S(1)}, u32[]{:S(2)}, u32[]{:S(2)}) collective-permute-start(bf16[64,640]{1,0:T(8,128)(2,1)S(1)} %stack.2.refs_0_), channel_id=1, source_target_pairs={{0,6},{2,4},{4,2},{6,0},{8,14},{10,12},{12,10},{14,8},{16,22},{18,... | collective-permute-start | bytes 245768 | tf_op jit(solution)/shard_map/ppermute | solution.py:163
  11.9 1.5 %collective-permute-start.12 = (bf16[512,512]{1,0:T(8,128)(2,1)S(1)}, bf16[512,512]{1,0:T(8,128)(2,1)S(1)}, u32[]{:S(2)}, u32[]{:S(2)}) collective-permute-start(bf16[512,512]{1,0:T(8,128)(2,1)S(1)} %margin_rows.1), channel_id=1, source_target_pairs={{0,1},{1,0},{2,3},{3,2},{4,5},{5,4},{6,7},{7,6},{8,9},{9,8},{10,11... | collective-permute-start | bytes 1572872 | tf_op jit(solution)/shard_map/ppermute | solution.py:197
  13.4 1.5 %collective-permute-done.3.refs_1_ = bf16[64,640]{1,0:T(8,128)(2,1)S(1)} collective-permute-done((bf16[64,640]{1,0:T(8,128)(2,1)S(1)}, bf16[64,640]{1,0:T(8,128)(2,1)S(1)}, u32[]{:S(2)}, u32[]{:S(2)}) %collective-permute-start.3) | collective-permute-done | bytes 81952 | tf_op jit(solution)/shard_map/ppermute | solution.py:163
  14.9 0.3 collective-permute-start.4
  15.2 0.7 %terms.2 = (bf16[128,1024]{1,0:T(8,128)(2,1)S(1)}, f32[128,512]{1,0:T(8,128)S(1)}) custom-call(s32[1]{0:T(128)} %bitcast.3.base_ref, bf16[1024,512]{1,0:T(8,128)(2,1)S(1)} %bitcast.10, bf16[128,640]{1,0:T(8,128)(2,1)S(1)} %stack.3.packed_ref.near_ref), custom_call_target="tpu_custom_call" | custom-call | flops 2684354560 | bytes 1048576 | tf_op jit(solution)/shard_map/terms/pallas_call | solution.py:218
  15.9 0.4 %collective-permute-done.4.packed_ref.far_ref = bf16[128,640]{1,0:T(8,128)(2,1)S(1)} collective-permute-done((bf16[128,640]{1,0:T(8,128)(2,1)S(1)}, bf16[128,640]{1,0:T(8,128)(2,1)S(1)}, u32[]{:S(2)}, u32[]{:S(2)}) %collective-permute-start.4) | collective-permute-done | bytes 163872 | tf_op jit(solution)/shard_map/ppermute | solution.py:163
  16.4 0.1 fusion
  16.4 1.7 %collective-permute-start.6 = (f16[64,512]{1,0:T(8,128)(2,1)S(1)}, f16[64,512]{1,0:T(8,128)(2,1)S(1)}, u32[]{:S(2)}, u32[]{:S(2)}) collective-permute-start(f16[64,512]{1,0:T(8,128)(2,1)S(1)} %fusion), channel_id=1, source_target_pairs={{0,6},{2,4},{4,2},{6,0},{8,14},{10,12},{12,10},{14,8},{16,22},{18,... | collective-permute-start | bytes 196616 | tf_op jit(solution)/shard_map/ppermute | solution.py:163
  18.1 0.7 %terms.3 = (bf16[128,1024]{1,0:T(8,128)(2,1)S(1)}, f32[128,512]{1,0:T(8,128)S(1)}) custom-call(s32[1]{0:T(128)} %bitcast.3.base_ref, bf16[1024,512]{1,0:T(8,128)(2,1)S(1)} %bitcast.11, bf16[128,640]{1,0:T(8,128)(2,1)S(1)} %collective-permute-done.4.packed_ref.far_ref), custom_call_target="tpu_custom_call" | custom-call | flops 2684354560 | bytes 1048576 | tf_op jit(solution)/shard_map/terms/pallas_call | solution.py:220
  18.9 0.1 fusion.19
  18.9 0.3 collective-permute-start.7
  19.2 0.0 collective-permute-start.5
  19.3 0.8 %match_grad.1.part_ref = f32[1024,512]{1,0:T(8,128)S(1)} custom-call(s32[1,512]{1,0:T(1,128)S(1)} %bitcast.7, bf16[1024,512]{1,0:T(8,128)(2,1)S(1)} %bitcast.12, bf16[128,1024]{1,0:T(8,128)(2,1)S(1)} %get-tuple-element.20.dl_near, bf16[128,1024]{1,0:T(8,128)(2,1)S(1)} %get-tuple-element.21.dl_far, bf16[128,640]{1,0:T(8,128)(2,1)S(1)} %stack.3.packed_ref.near_ref, ...), custom_call_target="tpu_custom_call" | custom-call | flops 2684354560 | bytes 1048576 | tf_op jit(solution)/shard_map/match_grad/pallas_call | solution.py:221
  20.1 3.2 %collective-permute-done.7 = f16[64,512]{1,0:T(8,128)(2,1)S(1)} collective-permute-done((f16[64,512]{1,0:T(8,128)(2,1)S(1)}, f16[64,512]{1,0:T(8,128)(2,1)S(1)}, u32[]{:S(2)}, u32[]{:S(2)}) %collective-permute-start.7) | collective-permute-done | bytes 65568 | tf_op jit(solution)/shard_map/ppermute | solution.py:163
  23.3 0.1 fusion.3
  23.3 0.1 fusion.6
  23.4 1.2 %collective-permute-start.8 = (f16[16,512]{1,0:T(8,128)(2,1)S(1)}, f16[16,512]{1,0:T(8,128)(2,1)S(1)}, u32[]{:S(2)}, u32[]{:S(2)}) collective-permute-start(f16[16,512]{1,0:T(8,128)(2,1)S(1)} %get-tuple-element.32), channel_id=1, source_target_pairs={{0,26},{2,24},{4,30},{6,28},{8,18},{10,16},{12,22},{14,20},{16,10}... | collective-permute-start | bytes 49160 | tf_op jit(solution)/shard_map/ppermute | solution.py:163
  24.5 2.7 %collective-permute-start.9 = (f16[16,512]{1,0:T(8,128)(2,1)S(1)}, f16[16,512]{1,0:T(8,128)(2,1)S(1)}, u32[]{:S(2)}, u32[]{:S(2)}) collective-permute-start(f16[16,512]{1,0:T(8,128)(2,1)S(1)} %get-tuple-element.34), channel_id=1, source_target_pairs={{0,18},{2,16},{4,22},{6,20},{8,26},{10,24},{12,30},{14,28},{16,2},... | collective-permute-start | bytes 49160 | tf_op jit(solution)/shard_map/ppermute | solution.py:163
  27.3 1.2 %collective-permute-done.8 = f16[16,512]{1,0:T(8,128)(2,1)S(1)} collective-permute-done((f16[16,512]{1,0:T(8,128)(2,1)S(1)}, f16[16,512]{1,0:T(8,128)(2,1)S(1)}, u32[]{:S(2)}, u32[]{:S(2)}) %collective-permute-start.8) | collective-permute-done | bytes 16416 | tf_op jit(solution)/shard_map/ppermute | solution.py:163
  28.5 0.3 collective-permute-done.10
  28.9 1.6 %collective-permute-start.11 = (f16[16,512]{1,0:T(8,128)(2,1)S(1)}, f16[16,512]{1,0:T(8,128)(2,1)S(1)}, u32[]{:S(2)}, u32[]{:S(2)}) collective-permute-start(f16[16,512]{1,0:T(8,128)(2,1)S(1)} %get-tuple-element.28), channel_id=1, source_target_pairs={{0,1},{1,0},{2,3},{3,2},{4,5},{5,4},{6,7},{7,6},{8,9},{9,8},{10,11... | collective-permute-start | bytes 49160 | tf_op jit(solution)/shard_map/ppermute | solution.py:251
  30.4 1.6 %voxel_grad.1 = f32[1024,512]{1,0:T(8,128)} custom-call(s32[1,512]{1,0:T(1,128)S(1)} %bitcast.8, f32[1024,512]{1,0:T(8,128)S(1)} %match_grad.1.part_ref, bf16[512,512]{1,0:T(8,128)(2,1)S(1)} %collective-permute-done.12.partner_ref), custom_call_target="tpu_custom_call" | custom-call | flops 536870912 | bytes 4194304 | tf_op jit(solution)/shard_map/voxel_grad/pallas_call | solution.py:254
  32.1 0.6 %collective-permute-done.11 = f16[16,512]{1,0:T(8,128)(2,1)S(1)} collective-permute-done((f16[16,512]{1,0:T(8,128)(2,1)S(1)}, f16[16,512]{1,0:T(8,128)(2,1)S(1)}, u32[]{:S(2)}, u32[]{:S(2)}) %collective-permute-start.11) | collective-permute-done | bytes 16416 | tf_op jit(solution)/shard_map/ppermute | solution.py:251
  32.7 0.6 %fusion.17 = f32[16,512]{1,0:T(8,128)} fusion(f32[16,512]{1,0:T(8,128)S(1)} %get-tuple-element.29, f16[16,512]{1,0:T(8,128)(2,1)S(1)} %collective-permute-done.11), kind=kLoop, calls=%fused_computation.29 | loop fusion | flops 40960 | bytes 81920 | tf_op jit(solution)/shard_map/add | solution.py:267
  (17 shorter events, 0.1 us)
Async XLA Ops:
  0.6 0.8 %copy-start.2 = (bf16[16,512]{1,0:T(8,128)(2,1)S(1)}, bf16[16,512]{1,0:T(8,128)(2,1)}, u32[]{:S(2)}) copy-start(bf16[16,512]{1,0:T(8,128)(2,1)} %phrases_ref.1) | copy-start | bytes 49156
  1.5 5.2 %copy-start = (s32[1,1,512]{2,1,0:T(1,128)S(1)}, s32[1,1,512]{2,1,0:T(1,128)}, u32[]{:S(2)}) copy-start(s32[1,1,512]{2,1,0:T(1,128)} %param.7) | copy-start | bytes 6148
  1.5 5.2 %copy-start.1 = (bf16[1,1024,512]{2,1,0:T(8,128)(2,1)S(1)}, bf16[1,1024,512]{2,1,0:T(8,128)(2,1)}, u32[]{:S(2)}) copy-start(bf16[1,1024,512]{2,1,0:T(8,128)(2,1)} %param.4) | copy-start | bytes 3145732
  1.5 5.9 %collective-permute-start.2 = (bf16[16,640]{1,0:T(8,128)(2,1)S(1)}, bf16[16,640]{1,0:T(8,128)(2,1)S(1)}, u32[]{:S(2)}, u32[]{:S(2)}) collective-permute-start(bf16[16,640]{1,0:T(8,128)(2,1)S(1)} %own_block.1.refs_0_), channel_id=1, source_target_pairs={{0,18},{2,16},{4,22},{6,20},{8,26},{10,24},{12,30},{14,28},{16,2},... | collective-permute-start | bytes 61448 | tf_op jit(solution)/shard_map/ppermute | solution.py:163
  5.0 5.0 %collective-permute-start.1 = (bf16[16,640]{1,0:T(8,128)(2,1)S(1)}, bf16[16,640]{1,0:T(8,128)(2,1)S(1)}, u32[]{:S(2)}, u32[]{:S(2)}) collective-permute-start(bf16[16,640]{1,0:T(8,128)(2,1)S(1)} %own_block.1.refs_0_), channel_id=1, source_target_pairs={{0,26},{2,24},{4,30},{6,28},{8,18},{10,16},{12,22},{14,20},{16,10}... | collective-permute-start | bytes 61448 | tf_op jit(solution)/shard_map/ppermute | solution.py:163
  6.7 3.8 %collective-permute-start = (bf16[16,640]{1,0:T(8,128)(2,1)S(1)}, bf16[16,640]{1,0:T(8,128)(2,1)S(1)}, u32[]{:S(2)}, u32[]{:S(2)}) collective-permute-start(bf16[16,640]{1,0:T(8,128)(2,1)S(1)} %own_block.1.refs_0_), channel_id=1, source_target_pairs={{0,8},{2,10},{4,12},{6,14},{8,0},{10,2},{12,4},{14,6},{16,24},{18,... | collective-permute-start | bytes 61448 | tf_op jit(solution)/shard_map/ppermute | solution.py:163
  10.5 4.4 %collective-permute-start.3 = (bf16[64,640]{1,0:T(8,128)(2,1)S(1)}, bf16[64,640]{1,0:T(8,128)(2,1)S(1)}, u32[]{:S(2)}, u32[]{:S(2)}) collective-permute-start(bf16[64,640]{1,0:T(8,128)(2,1)S(1)} %stack.2.refs_0_), channel_id=1, source_target_pairs={{0,6},{2,4},{4,2},{6,0},{8,14},{10,12},{12,10},{14,8},{16,22},{18,... | collective-permute-start | bytes 245768 | tf_op jit(solution)/shard_map/ppermute | solution.py:163
  11.9 18.5 %collective-permute-start.12 = (bf16[512,512]{1,0:T(8,128)(2,1)S(1)}, bf16[512,512]{1,0:T(8,128)(2,1)S(1)}, u32[]{:S(2)}, u32[]{:S(2)}) collective-permute-start(bf16[512,512]{1,0:T(8,128)(2,1)S(1)} %margin_rows.1), channel_id=1, source_target_pairs={{0,1},{1,0},{2,3},{3,2},{4,5},{5,4},{6,7},{7,6},{8,9},{9,8},{10,11... | collective-permute-start | bytes 1572872 | tf_op jit(solution)/shard_map/ppermute | solution.py:197
  14.9 1.5 %collective-permute-start.4 = (bf16[128,640]{1,0:T(8,128)(2,1)S(1)}, bf16[128,640]{1,0:T(8,128)(2,1)S(1)}, u32[]{:S(2)}, u32[]{:S(2)}) collective-permute-start(bf16[128,640]{1,0:T(8,128)(2,1)S(1)} %stack.3.packed_ref.near_ref), channel_id=1, source_target_pairs={{0,2},{2,0},{4,6},{6,4},{8,10},{10,8},{12,14},{14,12},{16,18},{18,... | collective-permute-start | bytes 491528 | tf_op jit(solution)/shard_map/ppermute | solution.py:163
  16.4 6.8 %collective-permute-start.6 = (f16[64,512]{1,0:T(8,128)(2,1)S(1)}, f16[64,512]{1,0:T(8,128)(2,1)S(1)}, u32[]{:S(2)}, u32[]{:S(2)}) collective-permute-start(f16[64,512]{1,0:T(8,128)(2,1)S(1)} %fusion), channel_id=1, source_target_pairs={{0,6},{2,4},{4,2},{6,0},{8,14},{10,12},{12,10},{14,8},{16,22},{18,... | collective-permute-start | bytes 196616 | tf_op jit(solution)/shard_map/ppermute | solution.py:163
  18.9 4.3 %collective-permute-start.7 = (f16[64,512]{1,0:T(8,128)(2,1)S(1)}, f16[64,512]{1,0:T(8,128)(2,1)S(1)}, u32[]{:S(2)}, u32[]{:S(2)}) collective-permute-start(f16[64,512]{1,0:T(8,128)(2,1)S(1)} %get-tuple-element.31), channel_id=1, source_target_pairs={{0,4},{2,6},{4,0},{6,2},{8,12},{10,14},{12,8},{14,10},{16,20},{18,... | collective-permute-start | bytes 196616 | tf_op jit(solution)/shard_map/ppermute | solution.py:163
  19.2 4.0 %collective-permute-start.5 = (f32[64,512]{1,0:T(8,128)S(1)}, f32[64,512]{1,0:T(8,128)S(1)}, u32[]{:S(2)}, u32[]{:S(2)}) collective-permute-start(f32[64,512]{1,0:T(8,128)S(1)} %get-tuple-element.30), channel_id=1, source_target_pairs={{0,2},{2,0},{4,6},{6,4},{8,10},{10,8},{12,14},{14,12},{16,18},{18,... | collective-permute-start | bytes 393224 | tf_op jit(solution)/shard_map/ppermute | solution.py:163
  23.4 5.1 %collective-permute-start.8 = (f16[16,512]{1,0:T(8,128)(2,1)S(1)}, f16[16,512]{1,0:T(8,128)(2,1)S(1)}, u32[]{:S(2)}, u32[]{:S(2)}) collective-permute-start(f16[16,512]{1,0:T(8,128)(2,1)S(1)} %get-tuple-element.32), channel_id=1, source_target_pairs={{0,26},{2,24},{4,30},{6,28},{8,18},{10,16},{12,22},{14,20},{16,10}... | collective-permute-start | bytes 49160 | tf_op jit(solution)/shard_map/ppermute | solution.py:163
  24.5 4.3 %collective-permute-start.10 = (f16[16,512]{1,0:T(8,128)(2,1)S(1)}, f16[16,512]{1,0:T(8,128)(2,1)S(1)}, u32[]{:S(2)}, u32[]{:S(2)}) collective-permute-start(f16[16,512]{1,0:T(8,128)(2,1)S(1)} %get-tuple-element.33), channel_id=1, source_target_pairs={{0,8},{2,10},{4,12},{6,14},{8,0},{10,2},{12,4},{14,6},{16,24},{18,... | collective-permute-start | bytes 49160 | tf_op jit(solution)/shard_map/ppermute | solution.py:163
  24.5 4.3 %collective-permute-start.9 = (f16[16,512]{1,0:T(8,128)(2,1)S(1)}, f16[16,512]{1,0:T(8,128)(2,1)S(1)}, u32[]{:S(2)}, u32[]{:S(2)}) collective-permute-start(f16[16,512]{1,0:T(8,128)(2,1)S(1)} %get-tuple-element.34), channel_id=1, source_target_pairs={{0,18},{2,16},{4,22},{6,20},{8,26},{10,24},{12,30},{14,28},{16,2},... | collective-permute-start | bytes 49160 | tf_op jit(solution)/shard_map/ppermute | solution.py:163
  28.9 3.8 %collective-permute-start.11 = (f16[16,512]{1,0:T(8,128)(2,1)S(1)}, f16[16,512]{1,0:T(8,128)(2,1)S(1)}, u32[]{:S(2)}, u32[]{:S(2)}) collective-permute-start(f16[16,512]{1,0:T(8,128)(2,1)S(1)} %get-tuple-element.28), channel_id=1, source_target_pairs={{0,1},{1,0},{2,3},{3,2},{4,5},{5,4},{6,7},{7,6},{8,9},{9,8},{10,11... | collective-permute-start | bytes 49160 | tf_op jit(solution)/shard_map/ppermute | solution.py:251

commit v8 on v7

--- a/solution.py
+++ b/solution.py
@@ -216,7 +216,7 @@
         name="terms",
     )
     dl_near, near_terms = terms(base, own_vox, near)
-    far, near_terms = lax.optimization_barrier((far, near_terms))
+    far, _ = lax.optimization_barrier((far, near_terms))
     dl_far, far_terms = terms(base, own_vox, far)
     matched = pl.pallas_call(
         functools.partial(match_kernel, scale),

time: 33.5 us -> 33.2 us (level)
  waiting for transfers between devices: 10.2 us -> 9.8 us
    ppermute x11, waiting for transfers between devices: 9.63 us -> 9.07 us  [over(): return lax.ppermute(value, 'batch', [(i, i ^ mask) for i in range(devices)])]
  transfers between devices with their start and end apart: 13 -> 13, of which waited for: 8 -> 7; matrix products, arithmetic and copies ran while one was open for 1% -> 1% of each run, Pallas kernels for 14% -> 14%
where the time goes in v8:
time: 33.2 us; the launch traced here: 33 us
  starting transfers between devices  16 us (48%)
  waiting for transfers between devices  9.8 us (30%)
  Pallas kernels  4.73 us (14%)
  other arithmetic  1.71 us (5%)
  between operations  0.76 us (2%)
    ppermute x11, starting transfers between devices, over(): return lax.ppermute(value, 'batch', [(i, i ^ mask) for i in range(devices)])  12.9 us
    ppermute x11, waiting for transfers between devices, over(): return lax.ppermute(value, 'batch', [(i, i ^ mask) for i in range(devices)])  9.07 us
    pallas_call x1, Pallas kernels, local(): pl.pallas_call(functools.partial(grad_kernel, block), out_shape=jax.Shape...  1.65 us
    ppermute x1, starting transfers between devices, local(): other = lax.ppermute(to_half(own, bound), 'crop', swap)  1.58 us
    ppermute x1, starting transfers between devices, local(): partner = lax.ppermute(chosen, 'crop', swap)  1.52 us
    pallas_call x1, Pallas kernels, local(): pl.pallas_call(functools.partial(match_kernel, scale), out_shape=jax.Shap...  0.82 us
    concatenate x1, other arithmetic, local(): jnp.concatenate([pair_ids, pair_ids])  0.81 us
    pallas_call x1, Pallas kernels, local(): dl_near, near_terms = terms(base, own_vox, near)  0.74 us
  transfers between devices with their start and end apart: 13, of which 7 were waited for; matrix products, arithmetic and copies ran while one was open for 1% of the time, Pallas kernels for 14%

profile of v8, /device:TPU:0, one launch (start us, length us, event | category | flops | bytes accessed | tf_op | source)
XLA Modules:
  0.0 33.0 jit_solution(8010727183558249221)
XLA Ops:
  0.6 0.8 %pad_add_fusion = s32[32]{0:T(128)S(1)} fusion(s32[16]{0:T(128)} %param.6), kind=kLoop, calls=%fused_computation.30 | loop fusion | flops 32 | bytes 192 | tf_op jit(solution)/shard_map/concatenate | solution.py:147
  1.5 0.0 copy-start
  1.5 0.0 copy-start.1
  1.5 3.5 %collective-permute-start.2 = (bf16[16,640]{1,0:T(8,128)(2,1)S(1)}, bf16[16,640]{1,0:T(8,128)(2,1)S(1)}, u32[]{:S(2)}, u32[]{:S(2)}) collective-permute-start(bf16[16,640]{1,0:T(8,128)(2,1)S(1)} %own_block.1.refs_0_), channel_id=1, source_target_pairs={{0,18},{2,16},{4,22},{6,20},{8,26},{10,24},{12,30},{14,28},{16,2},... | collective-permute-start | bytes 61448 | tf_op jit(solution)/shard_map/ppermute | solution.py:163
  5.0 1.6 %collective-permute-start.1 = (bf16[16,640]{1,0:T(8,128)(2,1)S(1)}, bf16[16,640]{1,0:T(8,128)(2,1)S(1)}, u32[]{:S(2)}, u32[]{:S(2)}) collective-permute-start(bf16[16,640]{1,0:T(8,128)(2,1)S(1)} %own_block.1.refs_0_), channel_id=1, source_target_pairs={{0,26},{2,24},{4,30},{6,28},{8,18},{10,16},{12,22},{14,20},{16,10}... | collective-permute-start | bytes 61448 | tf_op jit(solution)/shard_map/ppermute | solution.py:163
  6.7 0.0 collective-permute-start
  6.7 0.7 %margin_rows.1 = bf16[512,512]{1,0:T(8,128)(2,1)S(1)} custom-call(bf16[1024,512]{1,0:T(8,128)(2,1)S(1)} %bitcast.9, s32[1,512]{1,0:T(1,128)S(1)} %bitcast.6), custom_call_target="tpu_custom_call" | custom-call | flops 536870912 | bytes 1048576 | tf_op jit(solution)/shard_map/margin_rows/pallas_call | solution.py:184
  7.4 2.6 %collective-permute-done.1.refs_2_ = bf16[16,640]{1,0:T(8,128)(2,1)S(1)} collective-permute-done((bf16[16,640]{1,0:T(8,128)(2,1)S(1)}, bf16[16,640]{1,0:T(8,128)(2,1)S(1)}, u32[]{:S(2)}, u32[]{:S(2)}) %collective-permute-start.1) | collective-permute-done | bytes 20512 | tf_op jit(solution)/shard_map/ppermute | solution.py:163
  10.1 0.4 %collective-permute-done.refs_1_ = bf16[16,640]{1,0:T(8,128)(2,1)S(1)} collective-permute-done((bf16[16,640]{1,0:T(8,128)(2,1)S(1)}, bf16[16,640]{1,0:T(8,128)(2,1)S(1)}, u32[]{:S(2)}, u32[]{:S(2)}) %collective-permute-start) | collective-permute-done | bytes 20512 | tf_op jit(solution)/shard_map/ppermute | solution.py:163
  10.5 1.4 %collective-permute-start.3 = (bf16[64,640]{1,0:T(8,128)(2,1)S(1)}, bf16[64,640]{1,0:T(8,128)(2,1)S(1)}, u32[]{:S(2)}, u32[]{:S(2)}) collective-permute-start(bf16[64,640]{1,0:T(8,128)(2,1)S(1)} %stack.2.refs_0_), channel_id=1, source_target_pairs={{0,6},{2,4},{4,2},{6,0},{8,14},{10,12},{12,10},{14,8},{16,22},{18,... | collective-permute-start | bytes 245768 | tf_op jit(solution)/shard_map/ppermute | solution.py:163
  11.9 1.5 %collective-permute-start.12 = (bf16[512,512]{1,0:T(8,128)(2,1)S(1)}, bf16[512,512]{1,0:T(8,128)(2,1)S(1)}, u32[]{:S(2)}, u32[]{:S(2)}) collective-permute-start(bf16[512,512]{1,0:T(8,128)(2,1)S(1)} %margin_rows.1), channel_id=1, source_target_pairs={{0,1},{1,0},{2,3},{3,2},{4,5},{5,4},{6,7},{7,6},{8,9},{9,8},{10,11... | collective-permute-start | bytes 1572872 | tf_op jit(solution)/shard_map/ppermute | solution.py:197
  13.4 1.5 %collective-permute-done.3.refs_1_ = bf16[64,640]{1,0:T(8,128)(2,1)S(1)} collective-permute-done((bf16[64,640]{1,0:T(8,128)(2,1)S(1)}, bf16[64,640]{1,0:T(8,128)(2,1)S(1)}, u32[]{:S(2)}, u32[]{:S(2)}) %collective-permute-start.3) | collective-permute-done | bytes 81952 | tf_op jit(solution)/shard_map/ppermute | solution.py:163
  14.9 0.3 collective-permute-start.4
  15.2 0.7 %terms.2 = (bf16[128,1024]{1,0:T(8,128)(2,1)S(1)}, f32[128,512]{1,0:T(8,128)S(1)}) custom-call(s32[1]{0:T(128)} %bitcast.base_ref, bf16[1024,512]{1,0:T(8,128)(2,1)S(1)} %bitcast.10, bf16[128,640]{1,0:T(8,128)(2,1)S(1)} %stack.3.packed_ref.near_ref), custom_call_target="tpu_custom_call" | custom-call | flops 2684354560 | bytes 1048576 | tf_op jit(solution)/shard_map/terms/pallas_call | solution.py:218
  15.9 0.1 fusion
  16.0 1.5 %collective-permute-start.6 = (f16[64,512]{1,0:T(8,128)(2,1)S(1)}, f16[64,512]{1,0:T(8,128)(2,1)S(1)}, u32[]{:S(2)}, u32[]{:S(2)}) collective-permute-start(f16[64,512]{1,0:T(8,128)(2,1)S(1)} %fusion), channel_id=1, source_target_pairs={{0,6},{2,4},{4,2},{6,0},{8,14},{10,12},{12,10},{14,8},{16,22},{18,... | collective-permute-start | bytes 196616 | tf_op jit(solution)/shard_map/ppermute | solution.py:163
  17.5 0.7 %terms.3 = (bf16[128,1024]{1,0:T(8,128)(2,1)S(1)}, f32[128,512]{1,0:T(8,128)S(1)}) custom-call(s32[1]{0:T(128)} %bitcast.base_ref, bf16[1024,512]{1,0:T(8,128)(2,1)S(1)} %bitcast.11, bf16[128,640]{1,0:T(8,128)(2,1)S(1)} %collective-permute-done.4.packed_ref.far_ref), custom_call_target="tpu_custom_call" | custom-call | flops 2684354560 | bytes 1048576 | tf_op jit(solution)/shard_map/terms/pallas_call | solution.py:220
  18.2 0.1 fusion.19
  18.3 0.6 %collective-permute-start.7 = (f16[64,512]{1,0:T(8,128)(2,1)S(1)}, f16[64,512]{1,0:T(8,128)(2,1)S(1)}, u32[]{:S(2)}, u32[]{:S(2)}) collective-permute-start(f16[64,512]{1,0:T(8,128)(2,1)S(1)} %get-tuple-element.29), channel_id=1, source_target_pairs={{0,4},{2,6},{4,0},{6,2},{8,12},{10,14},{12,8},{14,10},{16,20},{18,... | collective-permute-start | bytes 196616 | tf_op jit(solution)/shard_map/ppermute | solution.py:163
  18.9 0.1 collective-permute-start.5
  19.0 0.8 %match_grad.1.part_ref = f32[1024,512]{1,0:T(8,128)S(1)} custom-call(s32[1,512]{1,0:T(1,128)S(1)} %bitcast.7, bf16[1024,512]{1,0:T(8,128)(2,1)S(1)} %bitcast.12, bf16[128,1024]{1,0:T(8,128)(2,1)S(1)} %get-tuple-element.18.dl_near, bf16[128,1024]{1,0:T(8,128)(2,1)S(1)} %get-tuple-element.19.dl_far, bf16[128,640]{1,0:T(8,128)(2,1)S(1)} %stack.3.packed_ref.near_ref, ...), custom_call_target="tpu_custom_call" | custom-call | flops 2684354560 | bytes 1048576 | tf_op jit(solution)/shard_map/match_grad/pallas_call | solution.py:221
  19.8 3.1 %collective-permute-done.7 = f16[64,512]{1,0:T(8,128)(2,1)S(1)} collective-permute-done((f16[64,512]{1,0:T(8,128)(2,1)S(1)}, f16[64,512]{1,0:T(8,128)(2,1)S(1)}, u32[]{:S(2)}, u32[]{:S(2)}) %collective-permute-start.7) | collective-permute-done | bytes 65568 | tf_op jit(solution)/shard_map/ppermute | solution.py:163
  22.9 0.1 fusion.3
  22.9 0.1 fusion.6
  23.0 0.8 %collective-permute-start.8 = (f16[16,512]{1,0:T(8,128)(2,1)S(1)}, f16[16,512]{1,0:T(8,128)(2,1)S(1)}, u32[]{:S(2)}, u32[]{:S(2)}) collective-permute-start(f16[16,512]{1,0:T(8,128)(2,1)S(1)} %get-tuple-element.30), channel_id=1, source_target_pairs={{0,26},{2,24},{4,30},{6,28},{8,18},{10,16},{12,22},{14,20},{16,10}... | collective-permute-start | bytes 49160 | tf_op jit(solution)/shard_map/ppermute | solution.py:163
  23.9 3.0 %collective-permute-start.9 = (f16[16,512]{1,0:T(8,128)(2,1)S(1)}, f16[16,512]{1,0:T(8,128)(2,1)S(1)}, u32[]{:S(2)}, u32[]{:S(2)}) collective-permute-start(f16[16,512]{1,0:T(8,128)(2,1)S(1)} %get-tuple-element.32), channel_id=1, source_target_pairs={{0,18},{2,16},{4,22},{6,20},{8,26},{10,24},{12,30},{14,28},{16,2},... | collective-permute-start | bytes 49160 | tf_op jit(solution)/shard_map/ppermute | solution.py:163
  26.9 1.4 %collective-permute-done.8 = f16[16,512]{1,0:T(8,128)(2,1)S(1)} collective-permute-done((f16[16,512]{1,0:T(8,128)(2,1)S(1)}, f16[16,512]{1,0:T(8,128)(2,1)S(1)}, u32[]{:S(2)}, u32[]{:S(2)}) %collective-permute-start.8) | collective-permute-done | bytes 16416 | tf_op jit(solution)/shard_map/ppermute | solution.py:163
  28.3 0.1 collective-permute-done.9
  28.4 1.6 %collective-permute-start.11 = (f16[16,512]{1,0:T(8,128)(2,1)S(1)}, f16[16,512]{1,0:T(8,128)(2,1)S(1)}, u32[]{:S(2)}, u32[]{:S(2)}) collective-permute-start(f16[16,512]{1,0:T(8,128)(2,1)S(1)} %get-tuple-element.26), channel_id=1, source_target_pairs={{0,1},{1,0},{2,3},{3,2},{4,5},{5,4},{6,7},{7,6},{8,9},{9,8},{10,11... | collective-permute-start | bytes 49160 | tf_op jit(solution)/shard_map/ppermute | solution.py:251
  30.0 1.6 %voxel_grad.1 = f32[1024,512]{1,0:T(8,128)} custom-call(s32[1,512]{1,0:T(1,128)S(1)} %bitcast.8, f32[1024,512]{1,0:T(8,128)S(1)} %match_grad.1.part_ref, bf16[512,512]{1,0:T(8,128)(2,1)S(1)} %collective-permute-done.12.partner_ref), custom_call_target="tpu_custom_call" | custom-call | flops 536870912 | bytes 4194304 | tf_op jit(solution)/shard_map/voxel_grad/pallas_call | solution.py:254
  31.7 0.7 %collective-permute-done.11 = f16[16,512]{1,0:T(8,128)(2,1)S(1)} collective-permute-done((f16[16,512]{1,0:T(8,128)(2,1)S(1)}, f16[16,512]{1,0:T(8,128)(2,1)S(1)}, u32[]{:S(2)}, u32[]{:S(2)}) %collective-permute-start.11) | collective-permute-done | bytes 16416 | tf_op jit(solution)/shard_map/ppermute | solution.py:251
  32.4 0.6 %fusion.17 = f32[16,512]{1,0:T(8,128)} fusion(f32[16,512]{1,0:T(8,128)S(1)} %get-tuple-element.27, f16[16,512]{1,0:T(8,128)(2,1)S(1)} %collective-permute-done.11), kind=kLoop, calls=%fused_computation.29 | loop fusion | flops 40960 | bytes 81920 | tf_op jit(solution)/shard_map/add | solution.py:267
  (17 shorter events, 0.1 us)
Async XLA Ops:
  0.6 0.8 %copy-start.2 = (bf16[16,512]{1,0:T(8,128)(2,1)S(1)}, bf16[16,512]{1,0:T(8,128)(2,1)}, u32[]{:S(2)}) copy-start(bf16[16,512]{1,0:T(8,128)(2,1)} %phrases_ref.1) | copy-start | bytes 49156
  1.5 5.2 %copy-start = (s32[1,1,512]{2,1,0:T(1,128)S(1)}, s32[1,1,512]{2,1,0:T(1,128)}, u32[]{:S(2)}) copy-start(s32[1,1,512]{2,1,0:T(1,128)} %param.7) | copy-start | bytes 6148
  1.5 5.2 %copy-start.1 = (bf16[1,1024,512]{2,1,0:T(8,128)(2,1)S(1)}, bf16[1,1024,512]{2,1,0:T(8,128)(2,1)}, u32[]{:S(2)}) copy-start(bf16[1,1024,512]{2,1,0:T(8,128)(2,1)} %param.4) | copy-start | bytes 3145732
  1.5 5.9 %collective-permute-start.2 = (bf16[16,640]{1,0:T(8,128)(2,1)S(1)}, bf16[16,640]{1,0:T(8,128)(2,1)S(1)}, u32[]{:S(2)}, u32[]{:S(2)}) collective-permute-start(bf16[16,640]{1,0:T(8,128)(2,1)S(1)} %own_block.1.refs_0_), channel_id=1, source_target_pairs={{0,18},{2,16},{4,22},{6,20},{8,26},{10,24},{12,30},{14,28},{16,2},... | collective-permute-start | bytes 61448 | tf_op jit(solution)/shard_map/ppermute | solution.py:163
  5.0 5.0 %collective-permute-start.1 = (bf16[16,640]{1,0:T(8,128)(2,1)S(1)}, bf16[16,640]{1,0:T(8,128)(2,1)S(1)}, u32[]{:S(2)}, u32[]{:S(2)}) collective-permute-start(bf16[16,640]{1,0:T(8,128)(2,1)S(1)} %own_block.1.refs_0_), channel_id=1, source_target_pairs={{0,26},{2,24},{4,30},{6,28},{8,18},{10,16},{12,22},{14,20},{16,10}... | collective-permute-start | bytes 61448 | tf_op jit(solution)/shard_map/ppermute | solution.py:163
  6.7 3.8 %collective-permute-start = (bf16[16,640]{1,0:T(8,128)(2,1)S(1)}, bf16[16,640]{1,0:T(8,128)(2,1)S(1)}, u32[]{:S(2)}, u32[]{:S(2)}) collective-permute-start(bf16[16,640]{1,0:T(8,128)(2,1)S(1)} %own_block.1.refs_0_), channel_id=1, source_target_pairs={{0,8},{2,10},{4,12},{6,14},{8,0},{10,2},{12,4},{14,6},{16,24},{18,... | collective-permute-start | bytes 61448 | tf_op jit(solution)/shard_map/ppermute | solution.py:163
  10.5 4.4 %collective-permute-start.3 = (bf16[64,640]{1,0:T(8,128)(2,1)S(1)}, bf16[64,640]{1,0:T(8,128)(2,1)S(1)}, u32[]{:S(2)}, u32[]{:S(2)}) collective-permute-start(bf16[64,640]{1,0:T(8,128)(2,1)S(1)} %stack.2.refs_0_), channel_id=1, source_target_pairs={{0,6},{2,4},{4,2},{6,0},{8,14},{10,12},{12,10},{14,8},{16,22},{18,... | collective-permute-start | bytes 245768 | tf_op jit(solution)/shard_map/ppermute | solution.py:163
  11.9 18.1 %collective-permute-start.12 = (bf16[512,512]{1,0:T(8,128)(2,1)S(1)}, bf16[512,512]{1,0:T(8,128)(2,1)S(1)}, u32[]{:S(2)}, u32[]{:S(2)}) collective-permute-start(bf16[512,512]{1,0:T(8,128)(2,1)S(1)} %margin_rows.1), channel_id=1, source_target_pairs={{0,1},{1,0},{2,3},{3,2},{4,5},{5,4},{6,7},{7,6},{8,9},{9,8},{10,11... | collective-permute-start | bytes 1572872 | tf_op jit(solution)/shard_map/ppermute | solution.py:197
  14.9 2.6 %collective-permute-start.4 = (bf16[128,640]{1,0:T(8,128)(2,1)S(1)}, bf16[128,640]{1,0:T(8,128)(2,1)S(1)}, u32[]{:S(2)}, u32[]{:S(2)}) collective-permute-start(bf16[128,640]{1,0:T(8,128)(2,1)S(1)} %stack.3.packed_ref.near_ref), channel_id=1, source_target_pairs={{0,2},{2,0},{4,6},{6,4},{8,10},{10,8},{12,14},{14,12},{16,18},{18,... | collective-permute-start | bytes 491528 | tf_op jit(solution)/shard_map/ppermute | solution.py:163
  16.0 6.9 %collective-permute-start.6 = (f16[64,512]{1,0:T(8,128)(2,1)S(1)}, f16[64,512]{1,0:T(8,128)(2,1)S(1)}, u32[]{:S(2)}, u32[]{:S(2)}) collective-permute-start(f16[64,512]{1,0:T(8,128)(2,1)S(1)} %fusion), channel_id=1, source_target_pairs={{0,6},{2,4},{4,2},{6,0},{8,14},{10,12},{12,10},{14,8},{16,22},{18,... | collective-permute-start | bytes 196616 | tf_op jit(solution)/shard_map/ppermute | solution.py:163
  18.3 4.6 %collective-permute-start.7 = (f16[64,512]{1,0:T(8,128)(2,1)S(1)}, f16[64,512]{1,0:T(8,128)(2,1)S(1)}, u32[]{:S(2)}, u32[]{:S(2)}) collective-permute-start(f16[64,512]{1,0:T(8,128)(2,1)S(1)} %get-tuple-element.29), channel_id=1, source_target_pairs={{0,4},{2,6},{4,0},{6,2},{8,12},{10,14},{12,8},{14,10},{16,20},{18,... | collective-permute-start | bytes 196616 | tf_op jit(solution)/shard_map/ppermute | solution.py:163
  18.9 4.0 %collective-permute-start.5 = (f32[64,512]{1,0:T(8,128)S(1)}, f32[64,512]{1,0:T(8,128)S(1)}, u32[]{:S(2)}, u32[]{:S(2)}) collective-permute-start(f32[64,512]{1,0:T(8,128)S(1)} %get-tuple-element.28), channel_id=1, source_target_pairs={{0,2},{2,0},{4,6},{6,4},{8,10},{10,8},{12,14},{14,12},{16,18},{18,... | collective-permute-start | bytes 393224 | tf_op jit(solution)/shard_map/ppermute | solution.py:163
  23.0 5.2 %collective-permute-start.8 = (f16[16,512]{1,0:T(8,128)(2,1)S(1)}, f16[16,512]{1,0:T(8,128)(2,1)S(1)}, u32[]{:S(2)}, u32[]{:S(2)}) collective-permute-start(f16[16,512]{1,0:T(8,128)(2,1)S(1)} %get-tuple-element.30), channel_id=1, source_target_pairs={{0,26},{2,24},{4,30},{6,28},{8,18},{10,16},{12,22},{14,20},{16,10}... | collective-permute-start | bytes 49160 | tf_op jit(solution)/shard_map/ppermute | solution.py:163
  23.9 4.4 %collective-permute-start.10 = (f16[16,512]{1,0:T(8,128)(2,1)S(1)}, f16[16,512]{1,0:T(8,128)(2,1)S(1)}, u32[]{:S(2)}, u32[]{:S(2)}) collective-permute-start(f16[16,512]{1,0:T(8,128)(2,1)S(1)} %get-tuple-element.31), channel_id=1, source_target_pairs={{0,8},{2,10},{4,12},{6,14},{8,0},{10,2},{12,4},{14,6},{16,24},{18,... | collective-permute-start | bytes 49160 | tf_op jit(solution)/shard_map/ppermute | solution.py:163
  23.9 4.5 %collective-permute-start.9 = (f16[16,512]{1,0:T(8,128)(2,1)S(1)}, f16[16,512]{1,0:T(8,128)(2,1)S(1)}, u32[]{:S(2)}, u32[]{:S(2)}) collective-permute-start(f16[16,512]{1,0:T(8,128)(2,1)S(1)} %get-tuple-element.32), channel_id=1, source_target_pairs={{0,18},{2,16},{4,22},{6,20},{8,26},{10,24},{12,30},{14,28},{16,2},... | collective-permute-start | bytes 49160 | tf_op jit(solution)/shard_map/ppermute | solution.py:163
  28.4 4.0 %collective-permute-start.11 = (f16[16,512]{1,0:T(8,128)(2,1)S(1)}, f16[16,512]{1,0:T(8,128)(2,1)S(1)}, u32[]{:S(2)}, u32[]{:S(2)}) collective-permute-start(f16[16,512]{1,0:T(8,128)(2,1)S(1)} %get-tuple-element.26), channel_id=1, source_target_pairs={{0,1},{1,0},{2,3},{3,2},{4,5},{5,4},{6,7},{7,6},{8,9},{9,8},{10,11... | collective-permute-start | bytes 49160 | tf_op jit(solution)/shard_map/ppermute | solution.py:251

commit v9 on v8

--- a/solution.py
+++ b/solution.py
@@ -26,6 +26,8 @@
     row = lax.broadcasted_iota(jnp.int32, out_ref.shape, 0)
     lane = lax.broadcasted_iota(jnp.int32, out_ref.shape, 1)
     ids = ids_ref[...]
+    rest = jnp.zeros((1, LANES - 2 * owned), jnp.int32)
+    ids = jnp.concatenate([ids, ids, rest], axis=1)
     cells = jnp.where(lane == row, ids >> 8, jnp.where(lane == row + owned, ids & 255, 0))
     out_ref[...] = cells.astype(F32).astype(BF16)
 
@@ -144,7 +146,7 @@
         compiler_params=params,
         cost_estimate=pl.CostEstimate(flops=10**9, bytes_accessed=1024, transcendentals=0),
         name="id_cells",
-    )(jnp.pad(jnp.concatenate([pair_ids, pair_ids]), (0, LANES - 2 * owned))[None, :])
+    )(pair_ids[None, :])
 
     def stack(blocks, order):
         starts = [sum(block.shape[0] for block in blocks[:i]) for i in order]

time: 33.2 us -> 33.2 us (level)
  other arithmetic: 1.71 us -> 0.9 us
  local copies, waits for them, and re-layouts: 0.02 us -> 0.67 us
    concatenate x1 -> x0, other arithmetic: 0.81 us -> none  [local(): jnp.concatenate([pair_ids, pair_ids])]
    unnamed x6 -> x8, local copies, waits for them, and re-layouts: 0.02 us -> 0.67 us
where the time goes in v9:
time: 33.2 us; the launch traced here: 32.9 us
  starting transfers between devices  16 us (48%)
  waiting for transfers between devices  9.81 us (30%)
  Pallas kernels  4.8 us (14%)
  other arithmetic  0.9 us (3%)
  between operations  0.76 us (2%)
  local copies, waits for them, and re-layouts  0.67 us (2%)
    ppermute x11, starting transfers between devices, over(): return lax.ppermute(value, 'batch', [(i, i ^ mask) for i in range(devices)])  12.9 us
    ppermute x11, waiting for transfers between devices, over(): return lax.ppermute(value, 'batch', [(i, i ^ mask) for i in range(devices)])  9.08 us
    pallas_call x1, Pallas kernels, local(): pl.pallas_call(functools.partial(grad_kernel, block), out_shape=jax.Shape...  1.65 us
    ppermute x1, starting transfers between devices, local(): other = lax.ppermute(to_half(own, bound), 'crop', swap)  1.58 us
    ppermute x1, starting transfers between devices, local(): partner = lax.ppermute(chosen, 'crop', swap)  1.52 us
    pallas_call x1, Pallas kernels, local(): pl.pallas_call(functools.partial(match_kernel, scale), out_shape=jax.Shap...  0.82 us
    pallas_call x1, Pallas kernels, local(): dl_far, far_terms = terms(base, own_vox, far)  0.74 us
    pallas_call x1, Pallas kernels, local(): dl_near, near_terms = terms(base, own_vox, near)  0.74 us
  transfers between devices with their start and end apart: 13, of which 7 were waited for; matrix products, arithmetic and copies ran while one was open for 1% of the time, Pallas kernels for 14%

profile of v9, /device:TPU:0, one launch (start us, length us, event | category | flops | bytes accessed | tf_op | source)
XLA Modules:
  0.0 32.9 jit_solution(13772295090998501082)
XLA Ops:
  0.6 0.7 %copy-done.3 = s32[16]{0:T(128)S(1)} copy-done((s32[16]{0:T(128)S(1)}, s32[16]{0:T(128)}, u32[]{:S(2)}) %copy-start.3) | copy-done | bytes 88
  1.3 0.1 id_cells.1.cells_ref
  1.4 0.0 copy-start.1
  1.4 3.5 %collective-permute-start.2 = (bf16[16,640]{1,0:T(8,128)(2,1)S(1)}, bf16[16,640]{1,0:T(8,128)(2,1)S(1)}, u32[]{:S(2)}, u32[]{:S(2)}) collective-permute-start(bf16[16,640]{1,0:T(8,128)(2,1)S(1)} %own_block.1.refs_0_), channel_id=1, source_target_pairs={{0,18},{2,16},{4,22},{6,20},{8,26},{10,24},{12,30},{14,28},{16,2},... | collective-permute-start | bytes 61448 | tf_op jit(solution)/shard_map/ppermute | solution.py:165
  4.9 1.6 %collective-permute-start.1 = (bf16[16,640]{1,0:T(8,128)(2,1)S(1)}, bf16[16,640]{1,0:T(8,128)(2,1)S(1)}, u32[]{:S(2)}, u32[]{:S(2)}) collective-permute-start(bf16[16,640]{1,0:T(8,128)(2,1)S(1)} %own_block.1.refs_0_), channel_id=1, source_target_pairs={{0,26},{2,24},{4,30},{6,28},{8,18},{10,16},{12,22},{14,20},{16,10}... | collective-permute-start | bytes 61448 | tf_op jit(solution)/shard_map/ppermute | solution.py:165
  6.6 0.0 collective-permute-start
  6.6 0.7 %margin_rows.1 = bf16[512,512]{1,0:T(8,128)(2,1)S(1)} custom-call(bf16[1024,512]{1,0:T(8,128)(2,1)S(1)} %bitcast.8, s32[1,512]{1,0:T(1,128)S(1)} %bitcast.5), custom_call_target="tpu_custom_call" | custom-call | flops 536870912 | bytes 1048576 | tf_op jit(solution)/shard_map/margin_rows/pallas_call | solution.py:186
  7.3 2.6 %collective-permute-done.1.refs_2_ = bf16[16,640]{1,0:T(8,128)(2,1)S(1)} collective-permute-done((bf16[16,640]{1,0:T(8,128)(2,1)S(1)}, bf16[16,640]{1,0:T(8,128)(2,1)S(1)}, u32[]{:S(2)}, u32[]{:S(2)}) %collective-permute-start.1) | collective-permute-done | bytes 20512 | tf_op jit(solution)/shard_map/ppermute | solution.py:165
  10.0 0.4 %collective-permute-done.refs_1_ = bf16[16,640]{1,0:T(8,128)(2,1)S(1)} collective-permute-done((bf16[16,640]{1,0:T(8,128)(2,1)S(1)}, bf16[16,640]{1,0:T(8,128)(2,1)S(1)}, u32[]{:S(2)}, u32[]{:S(2)}) %collective-permute-start) | collective-permute-done | bytes 20512 | tf_op jit(solution)/shard_map/ppermute | solution.py:165
  10.4 1.4 %collective-permute-start.3 = (bf16[64,640]{1,0:T(8,128)(2,1)S(1)}, bf16[64,640]{1,0:T(8,128)(2,1)S(1)}, u32[]{:S(2)}, u32[]{:S(2)}) collective-permute-start(bf16[64,640]{1,0:T(8,128)(2,1)S(1)} %stack.2.refs_0_), channel_id=1, source_target_pairs={{0,6},{2,4},{4,2},{6,0},{8,14},{10,12},{12,10},{14,8},{16,22},{18,... | collective-permute-start | bytes 245768 | tf_op jit(solution)/shard_map/ppermute | solution.py:165
  11.8 1.5 %collective-permute-start.12 = (bf16[512,512]{1,0:T(8,128)(2,1)S(1)}, bf16[512,512]{1,0:T(8,128)(2,1)S(1)}, u32[]{:S(2)}, u32[]{:S(2)}) collective-permute-start(bf16[512,512]{1,0:T(8,128)(2,1)S(1)} %margin_rows.1), channel_id=1, source_target_pairs={{0,1},{1,0},{2,3},{3,2},{4,5},{5,4},{6,7},{7,6},{8,9},{9,8},{10,11... | collective-permute-start | bytes 1572872 | tf_op jit(solution)/shard_map/ppermute | solution.py:199
  13.3 1.5 %collective-permute-done.3.refs_1_ = bf16[64,640]{1,0:T(8,128)(2,1)S(1)} collective-permute-done((bf16[64,640]{1,0:T(8,128)(2,1)S(1)}, bf16[64,640]{1,0:T(8,128)(2,1)S(1)}, u32[]{:S(2)}, u32[]{:S(2)}) %collective-permute-start.3) | collective-permute-done | bytes 81952 | tf_op jit(solution)/shard_map/ppermute | solution.py:165
  14.8 0.3 collective-permute-start.4
  15.1 0.7 %terms.2 = (bf16[128,1024]{1,0:T(8,128)(2,1)S(1)}, f32[128,512]{1,0:T(8,128)S(1)}) custom-call(s32[1]{0:T(128)} %bitcast.base_ref, bf16[1024,512]{1,0:T(8,128)(2,1)S(1)} %bitcast.9, bf16[128,640]{1,0:T(8,128)(2,1)S(1)} %stack.3.packed_ref.near_ref), custom_call_target="tpu_custom_call" | custom-call | flops 2684354560 | bytes 1048576 | tf_op jit(solution)/shard_map/terms/pallas_call | solution.py:220
  15.8 0.1 fusion
  15.9 1.5 %collective-permute-start.6 = (f16[64,512]{1,0:T(8,128)(2,1)S(1)}, f16[64,512]{1,0:T(8,128)(2,1)S(1)}, u32[]{:S(2)}, u32[]{:S(2)}) collective-permute-start(f16[64,512]{1,0:T(8,128)(2,1)S(1)} %fusion), channel_id=1, source_target_pairs={{0,6},{2,4},{4,2},{6,0},{8,14},{10,12},{12,10},{14,8},{16,22},{18,... | collective-permute-start | bytes 196616 | tf_op jit(solution)/shard_map/ppermute | solution.py:165
  17.4 0.7 %terms.3 = (bf16[128,1024]{1,0:T(8,128)(2,1)S(1)}, f32[128,512]{1,0:T(8,128)S(1)}) custom-call(s32[1]{0:T(128)} %bitcast.base_ref, bf16[1024,512]{1,0:T(8,128)(2,1)S(1)} %bitcast.10, bf16[128,640]{1,0:T(8,128)(2,1)S(1)} %collective-permute-done.4.packed_ref.far_ref), custom_call_target="tpu_custom_call" | custom-call | flops 2684354560 | bytes 1048576 | tf_op jit(solution)/shard_map/terms/pallas_call | solution.py:222
  18.1 0.1 fusion.19
  18.2 0.6 %collective-permute-start.7 = (f16[64,512]{1,0:T(8,128)(2,1)S(1)}, f16[64,512]{1,0:T(8,128)(2,1)S(1)}, u32[]{:S(2)}, u32[]{:S(2)}) collective-permute-start(f16[64,512]{1,0:T(8,128)(2,1)S(1)} %get-tuple-element.29), channel_id=1, source_target_pairs={{0,4},{2,6},{4,0},{6,2},{8,12},{10,14},{12,8},{14,10},{16,20},{18,... | collective-permute-start | bytes 196616 | tf_op jit(solution)/shard_map/ppermute | solution.py:165
  18.8 0.1 collective-permute-start.5
  18.9 0.8 %match_grad.1.part_ref = f32[1024,512]{1,0:T(8,128)S(1)} custom-call(s32[1,512]{1,0:T(1,128)S(1)} %bitcast.6, bf16[1024,512]{1,0:T(8,128)(2,1)S(1)} %bitcast.11, bf16[128,1024]{1,0:T(8,128)(2,1)S(1)} %get-tuple-element.18.dl_near, bf16[128,1024]{1,0:T(8,128)(2,1)S(1)} %get-tuple-element.19.dl_far, bf16[128,640]{1,0:T(8,128)(2,1)S(1)} %stack.3.packed_ref.near_ref, ...), custom_call_target="tpu_custom_call" | custom-call | flops 2684354560 | bytes 1048576 | tf_op jit(solution)/shard_map/match_grad/pallas_call | solution.py:223
  19.7 3.1 %collective-permute-done.7 = f16[64,512]{1,0:T(8,128)(2,1)S(1)} collective-permute-done((f16[64,512]{1,0:T(8,128)(2,1)S(1)}, f16[64,512]{1,0:T(8,128)(2,1)S(1)}, u32[]{:S(2)}, u32[]{:S(2)}) %collective-permute-start.7) | collective-permute-done | bytes 65568 | tf_op jit(solution)/shard_map/ppermute | solution.py:165
  22.8 0.1 fusion.3
  22.9 0.1 fusion.6
  22.9 0.8 %collective-permute-start.8 = (f16[16,512]{1,0:T(8,128)(2,1)S(1)}, f16[16,512]{1,0:T(8,128)(2,1)S(1)}, u32[]{:S(2)}, u32[]{:S(2)}) collective-permute-start(f16[16,512]{1,0:T(8,128)(2,1)S(1)} %get-tuple-element.30), channel_id=1, source_target_pairs={{0,26},{2,24},{4,30},{6,28},{8,18},{10,16},{12,22},{14,20},{16,10}... | collective-permute-start | bytes 49160 | tf_op jit(solution)/shard_map/ppermute | solution.py:165
  23.8 3.1 %collective-permute-start.9 = (f16[16,512]{1,0:T(8,128)(2,1)S(1)}, f16[16,512]{1,0:T(8,128)(2,1)S(1)}, u32[]{:S(2)}, u32[]{:S(2)}) collective-permute-start(f16[16,512]{1,0:T(8,128)(2,1)S(1)} %get-tuple-element.32), channel_id=1, source_target_pairs={{0,18},{2,16},{4,22},{6,20},{8,26},{10,24},{12,30},{14,28},{16,2},... | collective-permute-start | bytes 49160 | tf_op jit(solution)/shard_map/ppermute | solution.py:165
  26.8 1.4 %collective-permute-done.8 = f16[16,512]{1,0:T(8,128)(2,1)S(1)} collective-permute-done((f16[16,512]{1,0:T(8,128)(2,1)S(1)}, f16[16,512]{1,0:T(8,128)(2,1)S(1)}, u32[]{:S(2)}, u32[]{:S(2)}) %collective-permute-start.8) | collective-permute-done | bytes 16416 | tf_op jit(solution)/shard_map/ppermute | solution.py:165
  28.2 0.1 collective-permute-done.9
  28.4 1.6 %collective-permute-start.11 = (f16[16,512]{1,0:T(8,128)(2,1)S(1)}, f16[16,512]{1,0:T(8,128)(2,1)S(1)}, u32[]{:S(2)}, u32[]{:S(2)}) collective-permute-start(f16[16,512]{1,0:T(8,128)(2,1)S(1)} %get-tuple-element.26), channel_id=1, source_target_pairs={{0,1},{1,0},{2,3},{3,2},{4,5},{5,4},{6,7},{7,6},{8,9},{9,8},{10,11... | collective-permute-start | bytes 49160 | tf_op jit(solution)/shard_map/ppermute | solution.py:253
  29.9 1.6 %voxel_grad.1 = f32[1024,512]{1,0:T(8,128)} custom-call(s32[1,512]{1,0:T(1,128)S(1)} %bitcast.7, f32[1024,512]{1,0:T(8,128)S(1)} %match_grad.1.part_ref, bf16[512,512]{1,0:T(8,128)(2,1)S(1)} %collective-permute-done.12.partner_ref), custom_call_target="tpu_custom_call" | custom-call | flops 536870912 | bytes 4194304 | tf_op jit(solution)/shard_map/voxel_grad/pallas_call | solution.py:256
  31.6 0.7 %collective-permute-done.11 = f16[16,512]{1,0:T(8,128)(2,1)S(1)} collective-permute-done((f16[16,512]{1,0:T(8,128)(2,1)S(1)}, f16[16,512]{1,0:T(8,128)(2,1)S(1)}, u32[]{:S(2)}, u32[]{:S(2)}) %collective-permute-start.11) | collective-permute-done | bytes 16416 | tf_op jit(solution)/shard_map/ppermute | solution.py:253
  32.3 0.6 %fusion.17 = f32[16,512]{1,0:T(8,128)} fusion(f32[16,512]{1,0:T(8,128)S(1)} %get-tuple-element.27, f16[16,512]{1,0:T(8,128)(2,1)S(1)} %collective-permute-done.11), kind=kLoop, calls=%fused_computation.29 | loop fusion | flops 40960 | bytes 81920 | tf_op jit(solution)/shard_map/add | solution.py:269
  (17 shorter events, 0.1 us)
Async XLA Ops:
  0.6 0.8 %copy-start.2 = (bf16[16,512]{1,0:T(8,128)(2,1)S(1)}, bf16[16,512]{1,0:T(8,128)(2,1)}, u32[]{:S(2)}) copy-start(bf16[16,512]{1,0:T(8,128)(2,1)} %phrases_ref.1) | copy-start | bytes 49156
  0.6 0.7 %copy-start.3 = (s32[16]{0:T(128)S(1)}, s32[16]{0:T(128)}, u32[]{:S(2)}) copy-start(s32[16]{0:T(128)} %param.6) | copy-start | bytes 196
  1.4 5.2 %copy-start = (s32[1,1,512]{2,1,0:T(1,128)S(1)}, s32[1,1,512]{2,1,0:T(1,128)}, u32[]{:S(2)}) copy-start(s32[1,1,512]{2,1,0:T(1,128)} %param.7) | copy-start | bytes 6148
  1.4 5.2 %copy-start.1 = (bf16[1,1024,512]{2,1,0:T(8,128)(2,1)S(1)}, bf16[1,1024,512]{2,1,0:T(8,128)(2,1)}, u32[]{:S(2)}) copy-start(bf16[1,1024,512]{2,1,0:T(8,128)(2,1)} %param.4) | copy-start | bytes 3145732
  1.4 5.9 %collective-permute-start.2 = (bf16[16,640]{1,0:T(8,128)(2,1)S(1)}, bf16[16,640]{1,0:T(8,128)(2,1)S(1)}, u32[]{:S(2)}, u32[]{:S(2)}) collective-permute-start(bf16[16,640]{1,0:T(8,128)(2,1)S(1)} %own_block.1.refs_0_), channel_id=1, source_target_pairs={{0,18},{2,16},{4,22},{6,20},{8,26},{10,24},{12,30},{14,28},{16,2},... | collective-permute-start | bytes 61448 | tf_op jit(solution)/shard_map/ppermute | solution.py:165
  4.9 5.0 %collective-permute-start.1 = (bf16[16,640]{1,0:T(8,128)(2,1)S(1)}, bf16[16,640]{1,0:T(8,128)(2,1)S(1)}, u32[]{:S(2)}, u32[]{:S(2)}) collective-permute-start(bf16[16,640]{1,0:T(8,128)(2,1)S(1)} %own_block.1.refs_0_), channel_id=1, source_target_pairs={{0,26},{2,24},{4,30},{6,28},{8,18},{10,16},{12,22},{14,20},{16,10}... | collective-permute-start | bytes 61448 | tf_op jit(solution)/shard_map/ppermute | solution.py:165
  6.6 3.8 %collective-permute-start = (bf16[16,640]{1,0:T(8,128)(2,1)S(1)}, bf16[16,640]{1,0:T(8,128)(2,1)S(1)}, u32[]{:S(2)}, u32[]{:S(2)}) collective-permute-start(bf16[16,640]{1,0:T(8,128)(2,1)S(1)} %own_block.1.refs_0_), channel_id=1, source_target_pairs={{0,8},{2,10},{4,12},{6,14},{8,0},{10,2},{12,4},{14,6},{16,24},{18,... | collective-permute-start | bytes 61448 | tf_op jit(solution)/shard_map/ppermute | solution.py:165
  10.4 4.4 %collective-permute-start.3 = (bf16[64,640]{1,0:T(8,128)(2,1)S(1)}, bf16[64,640]{1,0:T(8,128)(2,1)S(1)}, u32[]{:S(2)}, u32[]{:S(2)}) collective-permute-start(bf16[64,640]{1,0:T(8,128)(2,1)S(1)} %stack.2.refs_0_), channel_id=1, source_target_pairs={{0,6},{2,4},{4,2},{6,0},{8,14},{10,12},{12,10},{14,8},{16,22},{18,... | collective-permute-start | bytes 245768 | tf_op jit(solution)/shard_map/ppermute | solution.py:165
  11.8 18.1 %collective-permute-start.12 = (bf16[512,512]{1,0:T(8,128)(2,1)S(1)}, bf16[512,512]{1,0:T(8,128)(2,1)S(1)}, u32[]{:S(2)}, u32[]{:S(2)}) collective-permute-start(bf16[512,512]{1,0:T(8,128)(2,1)S(1)} %margin_rows.1), channel_id=1, source_target_pairs={{0,1},{1,0},{2,3},{3,2},{4,5},{5,4},{6,7},{7,6},{8,9},{9,8},{10,11... | collective-permute-start | bytes 1572872 | tf_op jit(solution)/shard_map/ppermute | solution.py:199
  14.8 2.6 %collective-permute-start.4 = (bf16[128,640]{1,0:T(8,128)(2,1)S(1)}, bf16[128,640]{1,0:T(8,128)(2,1)S(1)}, u32[]{:S(2)}, u32[]{:S(2)}) collective-permute-start(bf16[128,640]{1,0:T(8,128)(2,1)S(1)} %stack.3.packed_ref.near_ref), channel_id=1, source_target_pairs={{0,2},{2,0},{4,6},{6,4},{8,10},{10,8},{12,14},{14,12},{16,18},{18,... | collective-permute-start | bytes 491528 | tf_op jit(solution)/shard_map/ppermute | solution.py:165
  15.9 6.9 %collective-permute-start.6 = (f16[64,512]{1,0:T(8,128)(2,1)S(1)}, f16[64,512]{1,0:T(8,128)(2,1)S(1)}, u32[]{:S(2)}, u32[]{:S(2)}) collective-permute-start(f16[64,512]{1,0:T(8,128)(2,1)S(1)} %fusion), channel_id=1, source_target_pairs={{0,6},{2,4},{4,2},{6,0},{8,14},{10,12},{12,10},{14,8},{16,22},{18,... | collective-permute-start | bytes 196616 | tf_op jit(solution)/shard_map/ppermute | solution.py:165
  18.2 4.6 %collective-permute-start.7 = (f16[64,512]{1,0:T(8,128)(2,1)S(1)}, f16[64,512]{1,0:T(8,128)(2,1)S(1)}, u32[]{:S(2)}, u32[]{:S(2)}) collective-permute-start(f16[64,512]{1,0:T(8,128)(2,1)S(1)} %get-tuple-element.29), channel_id=1, source_target_pairs={{0,4},{2,6},{4,0},{6,2},{8,12},{10,14},{12,8},{14,10},{16,20},{18,... | collective-permute-start | bytes 196616 | tf_op jit(solution)/shard_map/ppermute | solution.py:165
  18.8 4.0 %collective-permute-start.5 = (f32[64,512]{1,0:T(8,128)S(1)}, f32[64,512]{1,0:T(8,128)S(1)}, u32[]{:S(2)}, u32[]{:S(2)}) collective-permute-start(f32[64,512]{1,0:T(8,128)S(1)} %get-tuple-element.28), channel_id=1, source_target_pairs={{0,2},{2,0},{4,6},{6,4},{8,10},{10,8},{12,14},{14,12},{16,18},{18,... | collective-permute-start | bytes 393224 | tf_op jit(solution)/shard_map/ppermute | solution.py:165
  22.9 5.3 %collective-permute-start.8 = (f16[16,512]{1,0:T(8,128)(2,1)S(1)}, f16[16,512]{1,0:T(8,128)(2,1)S(1)}, u32[]{:S(2)}, u32[]{:S(2)}) collective-permute-start(f16[16,512]{1,0:T(8,128)(2,1)S(1)} %get-tuple-element.30), channel_id=1, source_target_pairs={{0,26},{2,24},{4,30},{6,28},{8,18},{10,16},{12,22},{14,20},{16,10}... | collective-permute-start | bytes 49160 | tf_op jit(solution)/shard_map/ppermute | solution.py:165
  23.8 4.4 %collective-permute-start.10 = (f16[16,512]{1,0:T(8,128)(2,1)S(1)}, f16[16,512]{1,0:T(8,128)(2,1)S(1)}, u32[]{:S(2)}, u32[]{:S(2)}) collective-permute-start(f16[16,512]{1,0:T(8,128)(2,1)S(1)} %get-tuple-element.31), channel_id=1, source_target_pairs={{0,8},{2,10},{4,12},{6,14},{8,0},{10,2},{12,4},{14,6},{16,24},{18,... | collective-permute-start | bytes 49160 | tf_op jit(solution)/shard_map/ppermute | solution.py:165
  23.8 4.6 %collective-permute-start.9 = (f16[16,512]{1,0:T(8,128)(2,1)S(1)}, f16[16,512]{1,0:T(8,128)(2,1)S(1)}, u32[]{:S(2)}, u32[]{:S(2)}) collective-permute-start(f16[16,512]{1,0:T(8,128)(2,1)S(1)} %get-tuple-element.32), channel_id=1, source_target_pairs={{0,18},{2,16},{4,22},{6,20},{8,26},{10,24},{12,30},{14,28},{16,2},... | collective-permute-start | bytes 49160 | tf_op jit(solution)/shard_map/ppermute | solution.py:165
  28.4 4.0 %collective-permute-start.11 = (f16[16,512]{1,0:T(8,128)(2,1)S(1)}, f16[16,512]{1,0:T(8,128)(2,1)S(1)}, u32[]{:S(2)}, u32[]{:S(2)}) collective-permute-start(f16[16,512]{1,0:T(8,128)(2,1)S(1)} %get-tuple-element.26), channel_id=1, source_target_pairs={{0,1},{1,0},{2,3},{3,2},{4,5},{5,4},{6,7},{7,6},{8,9},{9,8},{10,11... | collective-permute-start | bytes 49160 | tf_op jit(solution)/shard_map/ppermute | solution.py:253
